TPU v7x, 32 devices: a whole 2x2x4 slice. The times are simulated.
32 devices in a mesh: vocab: 16 (over z, x, core), hid: 2 (over y).
Axes of the slice: x: 2, y: 2, z: 4, core: 2. Of those that a mesh axis runs over, the one named last changes fastest.
Arguments:
- posterior: bfloat16 [128, 16384], P(None, 'vocab'), may hold values from 1.9e-09 to 1, as said below
- transition: bfloat16 [16384, 16384], P('vocab', 'hid'), may hold values from 1e-07 to 1, as said below
- emission: bfloat16 [16384, 16384], P('hid', 'vocab'), may hold values from 6e-06 to 90, as said below
- advance: bfloat16 [256, 16384], P(None, 'hid'), may hold values from 0.0099487305 to 1
- dfa_state: int32 [128], replicated, may hold values from 0 to 255
- edge_next: int32 [256, 8], replicated, may hold values from 0 to 255
- token_edge: int32 [256, 16384], P(None, 'vocab'), may hold values from 0 to 7
- allowed: int32 [128, 128], P(None, 'vocab'), may hold values from 0 to 1, as said below
Outputs:
- constrained_logprob: float32 [128, 16384], P('hid', 'vocab')
Inputs may be any that keep to these rules, and one draw needn't show every extreme that they name: `allowed`: every request allows at least one block. `posterior`: positive. `transition`: positive. `emission`: positive.
All inputs are finite; a program needn't handle non-finite values.
Results may differ from a plain program's by a relative error of at most 0.0015.
Values may be sent and summed in bfloat16 or wider, within the bound.
No kernel may reach another device: no remote copies, remote signals or barrier semaphores. Data moves between devices by JAX's collectives and lax.ppermute only.
A program may use at most 128 MiB of HBM per device.

v0:
```python
import jax
import jax.numpy as jnp
from jax import lax
from jax.sharding import PartitionSpec as P

BLK = 128


def request_scores(prior_rows, dfa_state, edge_next, token_edge, allowed, advance, emission):
    row_count = prior_rows.shape[0]
    successor = jnp.take(edge_next, dfa_state, axis=0)
    look_rows = jnp.take(advance, successor, axis=0)
    weighted = (prior_rows.astype(jnp.float32)[:, None, :] * look_rows.astype(jnp.float32)).astype(
        jnp.bfloat16
    )
    slot_count = successor.shape[1]
    flattened = weighted.reshape(row_count * slot_count, weighted.shape[2])
    candidate = jnp.dot(flattened, emission, preferred_element_type=jnp.float32).reshape(
        row_count, slot_count, emission.shape[1]
    )
    edge_slots = jnp.take(token_edge, dfa_state, axis=0)
    labels = jnp.arange(slot_count, dtype=jnp.int32)
    chosen = jnp.sum(
        jnp.where(edge_slots[:, None, :] == labels[None, :, None], candidate, jnp.float32(0.0)),
        axis=1,
    )
    token_mask = jnp.repeat(allowed, BLK, axis=1)
    return jnp.where(token_mask > 0, chosen, jnp.float32(0.0))


def body(posterior, transition, emission, advance, dfa_state, edge_next, token_edge, allowed):
    prior_own = lax.psum_scatter(
        jnp.dot(posterior, transition, preferred_element_type=jnp.float32),
        "vocab",
        scatter_dimension=0,
        tiled=True,
    ).astype(jnp.bfloat16)
    partials = request_scores(
        lax.all_gather(prior_own, "vocab", axis=0, tiled=True),
        dfa_state,
        edge_next,
        token_edge,
        allowed,
        advance,
        emission,
    )
    scores = lax.psum_scatter(
        partials.astype(jnp.bfloat16), "hid", scatter_dimension=0, tiled=True
    ).astype(jnp.float32)
    local_rows = scores.shape[0]
    first_local = lax.axis_index("hid") * local_rows
    totals = lax.psum(jnp.sum(scores, axis=1), "vocab")
    mask_rows = lax.dynamic_slice_in_dim(allowed, first_local, local_rows, 0)
    token_mask = jnp.repeat(mask_rows, BLK, axis=1) > 0
    safe = jnp.where(token_mask, scores, jnp.float32(1.0))
    return jnp.where(token_mask, jnp.log(safe) - jnp.log(totals)[:, None], jnp.float32(0.0))


def solution(mesh):
    in_specs = (
        P(None, "vocab"),
        P("vocab", "hid"),
        P("hid", "vocab"),
        P(None, "hid"),
        P(),
        P(),
        P(None, "vocab"),
        P(None, "vocab"),
    )
    out_specs = P("hid", "vocab")
    return jax.shard_map(body, mesh=mesh, in_specs=in_specs, out_specs=out_specs, check_vma=False)
```

profile of v0, /device:TPU:0, one launch (start us, length us, event | category | flops | bytes accessed | tf_op | source)
XLA Modules:
  0.0 228.0 jit_solution(1220230549765597126)
XLA Ops:
  6.5 0.0 copy-start
  6.5 0.0 copy-start.2
  6.5 0.0 copy-start.3
  6.5 0.0 copy-start.4
  6.5 0.0 reduce-scatter.3.cloned.1.call-start
  6.6 10.2 %fusion.11 = f32[128,8192]{1,0:T(8,128)} fusion(bf16[128,1024]{1,0:T(8,128)(2,1)} %param.8, bf16[1024,8192]{1,0:T(8,128)(2,1)} %param.9), kind=kOutput, calls=%fused_computation.30 | convolution fusion | flops 2147483648 | bytes 21233664 | tf_op jit(solution)/shard_map/dot_general | solution.py:33
  16.8 0.0 reduce-scatter.3.cloned.1.call-update
  16.8 0.0 all-gather.2.cloned.1.call-start
  16.9 75.1 %reduce-scatter.3.cloned.1.call-done = f32[8,8192]{1,0:T(8,128)} async-done(((f32[128,8192]{1,0:T(8,128)}), f32[8,8192]{1,0:T(8,128)}) %reduce-scatter.3.cloned.1.call-update) | async-done | bytes 262160 | tf_op jit(solution)/shard_map/reduce_scatter | solution.py:32
  92.0 1.6 convert_element_type.22
  93.6 0.0 all-gather.2.cloned.1.call-update
  93.6 0.2 reduce-scatter.5.cloned.1.call-start
  93.9 0.0 copy-done.2
  93.9 0.1 copy.17
  94.0 0.0 copy-done.3
  94.0 0.1 copy.18
  94.2 0.0 copy-done.4
  94.2 0.6 gather_fusion.1
  94.9 0.1 compare_and_fusion
  95.0 0.1 copy.19
  95.0 0.1 compare_select_fusion
  95.1 0.1 reshape.104
  95.2 0.0 copy-done
  95.2 0.8 gather_fusion
  96.0 30.6 %gather_fusion.2 = bf16[1024,8192]{1,0:T(8,128)(2,1)} fusion(bf16[256,8192]{1,0:T(8,128)(2,1)} %param.11, s32[1024]{0:T(1024)S(1)} %broadcast_clamp_fusion), kind=kCustom, calls=%fused_computation.2 | custom fusion | bytes 33558528 | tf_op jit(solution)/shard_map/jit(_take)/gather | solution.py:12
  126.7 0.1 broadcast_select_fusion
  126.8 8.1 %all-gather.2.cloned.1.call-done = bf16[128,8192]{1,0:T(8,128)(2,1)} async-done(((bf16[8,8192]{1,0:T(8,128)(2,1)}), bf16[128,8192]{1,0:T(8,128)(2,1)}) %all-gather.2.cloned.1.call-update) | async-done | bytes 2097168 | tf_op jit(solution)/shard_map/all_gather | solution.py:39
  134.9 2.0 convert_element_type.23
  136.9 0.0 copy-start.1
  137.0 36.8 %select_reduce_fusion = bf16[128,1024]{1,0:T(8,128)(2,1)S(1)} fusion(s32[128,1024]{1,0:T(8,128)S(1)} %broadcast_select_fusion, bf16[8192,1024]{1,0:T(8,128)(2,1)} %param.10, bf16[128,8,8192]{2,1,0:T(8,128)(2,1)} %bitcast.20, f32[128,8192]{1,0:T(8,128)S(1)} %convert_element_type.23, pred[128,8]{0,1:T(8,128)(4,1)S(1)} %copy.19), kind=kOutput, calls=%fused_computation.10 | convolution fusion | flops 17216438272 | bytes 38536192 | tf_op jit(solution)/shard_map/dot_general | solution.py:18
  173.8 0.2 broadcast_in_dim.62
  174.0 0.8 select_convert_fusion
  174.8 0.0 reduce-scatter.5.cloned.1.call-update
  174.8 0.1 dynamic-slice_compare_fusion
  174.9 0.1 copy.15
  175.0 10.4 %reduce-scatter.5.cloned.1.call-done = bf16[64,1024]{1,0:T(8,128)(2,1)} async-done(((bf16[128,1024]{1,0:T(8,128)(2,1)}), bf16[64,1024]{1,0:T(8,128)(2,1)}) %reduce-scatter.5.cloned.1.call-update) | async-done | bytes 131088 | tf_op jit(solution)/shard_map/reduce_scatter | solution.py:47
  185.4 1.0 convert_reduce_fusion
  186.4 33.1 %psum.7 = f32[64]{0:T(128)S(1)} all-reduce(f32[64]{0:T(128)S(1)} %convert_reduce_fusion), channel_id=1, replica_groups=mesh['vocab'=16,'hid'=2] {'vocab'}, use_global_device_ids=true, to_apply=%region_4.5 | all-reduce | flops 64 | bytes 512 | tf_op jit(solution)/shard_map/psum | solution.py:52
  219.6 0.1 broadcast_in_dim.61
  219.7 1.7 fusion.9
  221.5 0.0 copy-done.1
  (6 shorter events, 0.0 us)
Async XLA Ops:
  6.5 88.7 %copy-start = (s32[256,1024]{1,0:T(8,128)S(1)}, s32[256,1024]{1,0:T(8,128)}, u32[]{:S(2)}) copy-start(s32[256,1024]{1,0:T(8,128)} %param.14) | copy-start | bytes 3145732
  6.5 87.3 %copy-start.2 = (s32[128,8]{0,1:T(8,128)S(1)}, s32[128,8]{0,1:T(8,128)}, u32[]{:S(2)}) copy-start(s32[128,8]{0,1:T(8,128)} %param.15) | copy-start | bytes 12292
  6.5 87.5 %copy-start.3 = (s32[256,8]{0,1:T(8,128)S(1)}, s32[256,8]{0,1:T(8,128)}, u32[]{:S(2)}) copy-start(s32[256,8]{0,1:T(8,128)} %param.13) | copy-start | bytes 24580
  6.5 87.6 %copy-start.4 = (s32[128]{0:T(128)S(1)}, s32[128]{0:T(128)}, u32[]{:S(2)}) copy-start(s32[128]{0:T(128)} %param.12) | copy-start | bytes 1540
  6.5 85.5 %reduce-scatter.3.cloned.1.call-start = ((), (), s32[]{:S(2)}) async-start(), calls=%async_computation.2 | async-start | bytes 4456448 | tf_op jit(solution)/shard_map/reduce_scatter | solution.py:32
  16.8 118.1 %all-gather.2.cloned.1.call-start = ((), (), s32[]{:S(2)}) async-start(), calls=%async_computation.3 | async-start | bytes 2228224 | tf_op jit(solution)/shard_map/all_gather | solution.py:39
  93.6 91.8 %reduce-scatter.5.cloned.1.call-start = ((), (), s32[]{:S(2)}) async-start(), calls=%async_computation.4 | async-start | bytes 393216 | tf_op jit(solution)/shard_map/reduce_scatter | solution.py:47
  136.9 84.5 %copy-start.1 = (s32[256,1024]{1,0:T(8,128)S(1)}, s32[256,1024]{1,0:T(8,128)}, u32[]{:S(2)}) copy-start(s32[256,1024]{1,0:T(8,128)} %param.14) | copy-start | bytes 3145732
Sparse Core Ops, SparseCore 0:
  16.9 75.0 reduce-scatter.2
  94.4 40.4 all-gather.1
  174.9 10.4 reduce-scatter.4
where the time goes:
time: 228 us
  waiting for transfers between devices  93.7 us (41%)
  matrix products  47.1 us (21%)
  blocking collectives  33.1 us (15%)
  local copies, waits for them, and re-layouts  33 us (14%)
  between operations  13.3 us (6%)
  other arithmetic  7.54 us (3%)
    reduce_scatter x1, waiting for transfers between devices, body(): lax.psum_scatter(jnp.dot(posterior, transition, preferred_element_type=jn...  75.1 us
    dot_general x1, matrix products, request_scores(): jnp.dot(flattened, emission, preferred_element_type=jnp.float32)  36.8 us
    psum x1, blocking collectives, body(): totals = lax.psum(jnp.sum(scores, axis=1), 'vocab')  33.1 us
    gather x1, local copies, waits for them, and re-layouts, request_scores(): look_rows = jnp.take(advance, successor, axis=0)  30.6 us
    reduce_scatter x1, waiting for transfers between devices, body(): lax.psum_scatter(partials.astype(jnp.bfloat16), 'hid', scatter_dimension=...  10.4 us
    dot_general x1, matrix products, body(): jnp.dot(posterior, transition, preferred_element_type=jnp.float32)  10.2 us
    all_gather x1, waiting for transfers between devices, body(): lax.all_gather(prior_own, 'vocab', axis=0, tiled=True)  8.15 us
  transfers between devices with their start and end apart: 3, of which 3 were waited for; matrix products, arithmetic and copies ran while one was open for 14% of the time, Pallas kernels for 0%

commit v1 on v0

v1 whole, which is shorter than its diff:
```python
import functools
import jax
import jax.numpy as jnp
from jax import lax
from jax.experimental import pallas as pl
from jax.experimental.pallas import tpu as pltpu
from jax.sharding import PartitionSpec as P

BLK = 128
BF16 = jnp.bfloat16
F32 = jnp.float32


def params(mib):
    return pltpu.CompilerParams(vmem_limit_bytes=mib << 20)


def half_product(posterior, transition, place, half, pieces, width):
    rows, depth = posterior.shape

    def kernel(place_ref, post_ref, trans_ref, out_ref):
        out_ref[0] = jnp.dot(post_ref[...], trans_ref[...], preferred_element_type=F32).astype(BF16)

    return pl.pallas_call(
        kernel,
        grid_spec=pltpu.PrefetchScalarGridSpec(
            num_scalar_prefetch=1,
            grid=(pieces,),
            in_specs=[
                pl.BlockSpec((rows, depth), lambda m, p: (0, 0)),
                pl.BlockSpec((depth, width), lambda m, p: (0, p[1 + half] * pieces + (p[0] ^ m))),
            ],
            out_specs=pl.BlockSpec((1, rows, width), lambda m, p: (m, 0, 0)),
        ),
        out_shape=jax.ShapeDtypeStruct((pieces, rows, width), BF16),
        compiler_params=params(40),
        cost_estimate=pl.CostEstimate(
            flops=2 * rows * depth * pieces * width, bytes_accessed=2 * depth * pieces * width, transcendentals=0
        ),
        name="prior_half",
    )(place, posterior, transition)


def successor_rows(onehot, advance, width):
    count, states = onehot.shape
    columns = advance.shape[1]

    def kernel(onehot_ref, adv_ref, out_ref):
        out_ref[...] = jnp.dot(onehot_ref[...], adv_ref[...], preferred_element_type=F32).astype(BF16)

    return pl.pallas_call(
        kernel,
        grid=(columns // width,),
        in_specs=[
            pl.BlockSpec((count, states), lambda i: (0, 0)),
            pl.BlockSpec((states, width), lambda i: (0, i)),
        ],
        out_specs=pl.BlockSpec((count, width), lambda i: (0, i)),
        out_shape=jax.ShapeDtypeStruct((count, columns), BF16),
        compiler_params=params(40),
        cost_estimate=pl.CostEstimate(
            flops=2 * count * states * columns, bytes_accessed=2 * columns * (count + states), transcendentals=0
        ),
        name="advance_rows",
    )(onehot, advance)


def piece_scores(pieces, places, look, emission, edges, mask, before, slots):
    count = len(pieces)
    rows, width = pieces[0].shape
    columns = emission.shape[1]
    has_before = before is not None

    def kernel(place_ref, *refs):
        piece_refs = refs[:count]
        look_ref, emit_ref, edge_ref, mask_ref = refs[count : count + 4]
        before_ref = refs[count + 4] if has_before else None
        out_ref, weighted, total = refs[-3:]
        step = pl.program_id(0)
        for j in range(count):

            @pl.when(step == j)
            def _():
                prior = piece_refs[j][...].astype(F32)
                for k in range(slots):
                    part = pl.ds(k * rows, rows)
                    weighted[part, :] = (prior * look_ref[part, :].astype(F32)).astype(BF16)

        @pl.when(step == 0)
        def _():
            total[...] = jnp.zeros_like(total)

        @pl.loop(0, slots)
        def _(k):
            part = pl.ds(k * rows, rows)
            total[part, :] += jnp.dot(weighted[part, :], emit_ref[...], preferred_element_type=F32)

        @pl.when(step == count - 1)
        def _():
            chosen = jnp.zeros((rows, columns), F32)
            for k in range(slots):
                chosen = jnp.where(edge_ref[...] == k, total[pl.ds(k * rows, rows), :], chosen)
            chosen = jnp.where(mask_ref[...] > 0, chosen, 0.0)
            out_ref[...] = chosen + before_ref[...] if has_before else chosen

    whole = lambda i, p: (0, 0)
    block = pl.BlockSpec((rows, columns), whole)
    return pl.pallas_call(
        kernel,
        grid_spec=pltpu.PrefetchScalarGridSpec(
            num_scalar_prefetch=1,
            grid=(count,),
            in_specs=[pl.BlockSpec((rows, width), whole) for _ in pieces]
            + [
                pl.BlockSpec((slots * rows, width), lambda i, p: (0, p[i])),
                pl.BlockSpec((width, columns), lambda i, p: (p[i], 0)),
                block,
                block,
            ]
            + [block] * has_before,
            out_specs=block,
            scratch_shapes=[pltpu.VMEM((slots * rows, width), BF16), pltpu.VMEM((slots * rows, columns), F32)],
        ),
        out_shape=jax.ShapeDtypeStruct((rows, columns), F32),
        compiler_params=params(44),
        cost_estimate=pl.CostEstimate(
            flops=2 * slots * rows * width * columns * count,
            bytes_accessed=2 * count * width * (slots * rows + columns),
            transcendentals=0,
        ),
        name="piece_scores",
    )(places, *pieces, look, emission, edges, mask, *([before] if has_before else []))


def body(sizes, posterior, transition, emission, advance, dfa_state, edge_next, token_edge, allowed):
    vocab_size, hid_size = sizes
    rows = posterior.shape[0]
    hidden = transition.shape[1]
    slots = edge_next.shape[1]
    me = lax.axis_index("vocab")
    core, chip = me % 2, me // 2
    chips = vocab_size // 2
    width = hidden // vocab_size
    direct = chips <= 8 and width % 128 == 0

    states = lax.broadcasted_iota(jnp.int32, (1, 1, advance.shape[0]), 2)
    successor = jnp.take(edge_next, dfa_state, axis=0, mode="clip")
    onehot = (successor.T[:, :, None] == states).astype(BF16).reshape(slots * rows, advance.shape[0])
    edges = jnp.take(token_edge, dfa_state, axis=0, mode="clip")
    mask = jnp.repeat(allowed, BLK, axis=1)

    def swap(array, bits):
        return lax.ppermute(array, "vocab", [(i, i ^ bits) for i in range(vocab_size)])

    scores = None
    if direct:
        place = jnp.stack([chip, 1 - core, core]).astype(jnp.int32)
        away = half_product(posterior, transition, place, 0, chips, width)
        came = swap(away, 1)
        kept = half_product(posterior, transition, place, 1, chips, width)
        sums = [kept[m].astype(F32) + came[m].astype(F32) for m in range(chips)]
        sent = [swap(sums[m].astype(BF16), 2 * m) for m in range(1, chips)]
        look = successor_rows(onehot, advance, 512)
        total = sums[0]
        for part in sent:
            total = total + part.astype(F32)
        own = total.astype(BF16)
        held = [own] + [swap(own, 2 * m) for m in range(1, chips)]
        for group in ([0, 1, 2], [3, 4, 5], [6, 7]):
            group = [m for m in group if m < chips]
            if not group:
                continue
            pieces = [held[m] for m in group] + [swap(held[m], 1) for m in group]
            places = jnp.stack(
                [core * chips + (chip ^ m) for m in group] + [(1 - core) * chips + (chip ^ m) for m in group]
            ).astype(jnp.int32)
            scores = piece_scores(pieces, places, look, emission, edges, mask, scores, slots)
    else:
        own = lax.psum_scatter(
            jnp.dot(posterior, transition, preferred_element_type=F32), "vocab", scatter_dimension=0, tiled=True
        ).astype(BF16)
        prior = lax.all_gather(own, "vocab", axis=0, tiled=True)
        look = successor_rows(onehot, advance, 512)
        count = hidden // 512
        pieces = [prior[:, 512 * j : 512 * (j + 1)] for j in range(count)]
        scores = piece_scores(
            pieces, jnp.arange(count, dtype=jnp.int32), look, emission, edges, mask, None, slots
        )

    sums = jnp.sum(scores, axis=1)
    local = rows // hid_size
    first = lax.axis_index("hid") * local
    if hid_size == 2:
        part = jnp.reshape(sums, (1, rows))
        part = part + lax.ppermute(part, "hid", [(0, 1), (1, 0)])
        bits = vocab_size // 2
        while bits:
            part = part + swap(part, bits)
            bits //= 2
        totals = lax.dynamic_slice_in_dim(part[0], first, local, 0)
        other = lax.dynamic_slice_in_dim(scores, local - first, local, 0).astype(BF16)
        came = lax.ppermute(other, "hid", [(0, 1), (1, 0)])
        mine = lax.dynamic_slice_in_dim(scores, first, local, 0) + came.astype(F32)
    else:
        mine = lax.psum_scatter(scores.astype(BF16), "hid", scatter_dimension=0, tiled=True).astype(F32)
        totals = lax.psum(jnp.sum(mine, axis=1), "vocab")
    token_mask = lax.dynamic_slice_in_dim(mask, first, local, 0) > 0
    safe = jnp.where(token_mask, mine, jnp.float32(1.0))
    return jnp.where(token_mask, jnp.log(safe) - jnp.log(totals)[:, None], jnp.float32(0.0))


def solution(mesh):
    in_specs = (
        P(None, "vocab"),
        P("vocab", "hid"),
        P("hid", "vocab"),
        P(None, "hid"),
        P(),
        P(),
        P(None, "vocab"),
        P(None, "vocab"),
    )
    sizes = (mesh.shape["vocab"], mesh.shape["hid"])
    return jax.shard_map(
        functools.partial(body, sizes), mesh=mesh, in_specs=in_specs, out_specs=P("hid", "vocab"), check_vma=False
    )
```

time: 228 us -> 158 us (0.69)
  Pallas kernels: 0 us -> 79.5 us
  waiting for transfers between devices: 93.7 us -> 23.1 us
  matrix products: 47.1 us -> 0 us
  starting transfers between devices: 0.3 us -> 44.7 us
  blocking collectives: 33.1 us -> 0 us
  local copies, waits for them, and re-layouts: 33 us -> 6.17 us
  between operations: 13.3 us -> 0.22 us
  other arithmetic: 7.54 us -> 3.63 us
    reduce_scatter x2 -> x0, waiting for transfers between devices: 85.5 us -> none  [the longest x1 75.1 us: body(): lax.psum_scatter(jnp.dot(posterior, transition, preferred_element_type=jn...]
    pallas_call x0 -> x6, Pallas kernels: none -> 79.5 us  [the longest x3 52.7 us: piece_scores(): pl.pallas_call(kernel, grid_spec=pltpu.PrefetchScalarGridSpec(num_scalar_...]
    dot_general x2 -> x0, matrix products: 47.1 us -> none  [the longest x1 36.8 us: request_scores(): jnp.dot(flattened, emission, preferred_element_type=jnp.float32)]
    ppermute x0 -> x29, starting transfers between devices: none -> 44.7 us  [the longest x27 42.5 us: swap(): lax.ppermute(array, 'vocab', [(i, i ^ bits) for i in range(vocab_size)])]
    psum x1 -> x0, blocking collectives: 33.1 us -> none  [body(): totals = lax.psum(jnp.sum(scores, axis=1), 'vocab')]
    gather x3 -> x2, local copies, waits for them, and re-layouts: 32.1 us -> 1.45 us  [the longest x1 0.8 us: body(): edges = jnp.take(token_edge, dfa_state, axis=0, mode='clip')]
    ppermute x0 -> x29, waiting for transfers between devices: none -> 23.1 us  [the longest x27 21.7 us: swap(): lax.ppermute(array, 'vocab', [(i, i ^ bits) for i in range(vocab_size)])]
    all_gather x1 -> x0, waiting for transfers between devices: 8.15 us -> none  [body(): lax.all_gather(prior_own, 'vocab', axis=0, tiled=True)]
  transfers between devices with their start and end apart: 3 -> 29, of which waited for: 3 -> 8; matrix products, arithmetic and copies ran while one was open for 14% -> 2% of each run, Pallas kernels for 0% -> 37%
where the time goes in v1:
time: 158 us; the launch traced here: 157 us
  Pallas kernels  79.5 us (50%)
  starting transfers between devices  44.7 us (28%)
  waiting for transfers between devices  23.1 us (15%)
  local copies, waits for them, and re-layouts  6.17 us (4%)
  other arithmetic  3.63 us (2%)
    pallas_call x3, Pallas kernels, piece_scores(): pl.pallas_call(kernel, grid_spec=pltpu.PrefetchScalarGridSpec(num_scalar_...  52.7 us
    ppermute x27, starting transfers between devices, swap(): lax.ppermute(array, 'vocab', [(i, i ^ bits) for i in range(vocab_size)])  42.5 us
    ppermute x27, waiting for transfers between devices, swap(): lax.ppermute(array, 'vocab', [(i, i ^ bits) for i in range(vocab_size)])  21.7 us
    pallas_call x2, Pallas kernels, half_product(): pl.pallas_call(kernel, grid_spec=pltpu.PrefetchScalarGridSpec(num_scalar_...  14.7 us
    pallas_call x1, Pallas kernels, successor_rows(): pl.pallas_call(kernel, grid=(columns // width,), in_specs=[pl.BlockSpec((...  12.2 us
    unnamed x19, local copies, waits for them, and re-layouts  4.21 us
  transfers between devices with their start and end apart: 29, of which 8 were waited for; matrix products, arithmetic and copies ran while one was open for 2% of the time, Pallas kernels for 37%

profile of v1, /device:TPU:0, one launch (start us, length us, event | category | flops | bytes accessed | tf_op | source)
XLA Modules:
  0.0 157.3 jit_solution(6619723054237784733)
XLA Ops:
  0.1 1.0 copy-done.3
  1.1 7.3 %prior_half.3 = bf16[8,128,512]{2,1,0:T(8,128)(2,1)S(1)} custom-call(s32[3]{0:T(128)S(1)} %pad_add_fusion.1.place_ref, bf16[128,1024]{1,0:T(8,128)(2,1)S(1)} %copy-done.3, bf16[1024,8192]{1,0:T(8,128)(2,1)} %trans_ref.3), custom_call_target="tpu_custom_call" | custom-call | flops 1073741824 | bytes 8388608 | tf_op jit(solution)/shard_map/prior_half/pallas_call | solution.py:24
  8.4 0.5 collective-permute-start
  9.0 7.3 %prior_half.2 = bf16[8,128,512]{2,1,0:T(8,128)(2,1)S(1)} custom-call(s32[3]{0:T(128)S(1)} %pad_add_fusion.1.place_ref, bf16[128,1024]{1,0:T(8,128)(2,1)S(1)} %copy-done.3, bf16[1024,8192]{1,0:T(8,128)(2,1)} %trans_ref.3), custom_call_target="tpu_custom_call" | custom-call | flops 1073741824 | bytes 8388608 | tf_op jit(solution)/shard_map/prior_half/pallas_call | solution.py:24
  16.3 1.0 fusion.8
  17.3 2.5 %collective-permute-start.1 = (bf16[128,512]{1,0:T(8,128)(2,1)S(1)}, bf16[128,512]{1,0:T(8,128)(2,1)S(1)}, u32[]{:S(2)}, u32[]{:S(2)}) collective-permute-start(bf16[128,512]{1,0:T(8,128)(2,1)S(1)} %get-tuple-element.5), channel_id=1, source_target_pairs={{0,4},{2,6},{4,0},{6,2},{8,12},{10,14},{12,8},{14,10},{16,20},{18,... | collective-permute-start | bytes 393224 | tf_op jit(solution)/shard_map/ppermute | solution.py:153
  19.8 1.6 %collective-permute-start.2 = (bf16[128,512]{1,0:T(8,128)(2,1)S(1)}, bf16[128,512]{1,0:T(8,128)(2,1)S(1)}, u32[]{:S(2)}, u32[]{:S(2)}) collective-permute-start(bf16[128,512]{1,0:T(8,128)(2,1)S(1)} %get-tuple-element.11), channel_id=1, source_target_pairs={{0,8},{2,10},{4,12},{6,14},{8,0},{10,2},{12,4},{14,6},{16,24},{18,... | collective-permute-start | bytes 393224 | tf_op jit(solution)/shard_map/ppermute | solution.py:153
  21.4 3.0 %collective-permute-start.4 = (bf16[128,512]{1,0:T(8,128)(2,1)}, bf16[128,512]{1,0:T(8,128)(2,1)}, u32[]{:S(2)}, u32[]{:S(2)}) collective-permute-start(bf16[128,512]{1,0:T(8,128)(2,1)} %get-tuple-element.9), channel_id=1, source_target_pairs={{0,16},{2,18},{4,20},{6,22},{8,24},{10,26},{12,28},{14,30},{16,0},... | collective-permute-start | bytes 393224 | tf_op jit(solution)/shard_map/ppermute | solution.py:153
  24.4 1.3 collective-permute-start.5
  25.7 3.6 %collective-permute-start.6 = (bf16[128,512]{1,0:T(8,128)(2,1)}, bf16[128,512]{1,0:T(8,128)(2,1)}, u32[]{:S(2)}, u32[]{:S(2)}) collective-permute-start(bf16[128,512]{1,0:T(8,128)(2,1)} %get-tuple-element.7), channel_id=1, source_target_pairs={{0,24},{2,26},{4,28},{6,30},{8,16},{10,18},{12,20},{14,22},{16,8},... | collective-permute-start | bytes 393224 | tf_op jit(solution)/shard_map/ppermute | solution.py:153
  29.3 1.1 collective-permute-done.2
  30.4 0.7 copy-done.4
  31.1 0.1 copy.12
  31.2 0.6 gather_fusion
  31.9 0.4 collective-permute-done.3
  32.4 11.6 %collective-permute-done.5 = bf16[128,512]{1,0:T(8,128)(2,1)} collective-permute-done((bf16[128,512]{1,0:T(8,128)(2,1)}, bf16[128,512]{1,0:T(8,128)(2,1)}, u32[]{:S(2)}, u32[]{:S(2)}) %collective-permute-start.5) | collective-permute-done | bytes 131104 | tf_op jit(solution)/shard_map/ppermute | solution.py:153
  44.0 1.4 fusion.7.refs_0_
  45.4 1.5 collective-permute-start.18
  46.9 4.7 %collective-permute-start.19 = (bf16[128,512]{1,0:T(8,128)(2,1)S(1)}, bf16[128,512]{1,0:T(8,128)(2,1)S(1)}, u32[]{:S(2)}, u32[]{:S(2)}) collective-permute-start(bf16[128,512]{1,0:T(8,128)(2,1)S(1)} %fusion.7.refs_0_), channel_id=1, source_target_pairs={{0,8},{2,10},{4,12},{6,14},{8,0},{10,2},{12,4},{14,6},{16,24},{18,... | collective-permute-start | bytes 393224 | tf_op jit(solution)/shard_map/ppermute | solution.py:153
  51.6 0.5 collective-permute-start.12
  52.2 4.2 %collective-permute-start.13 = (bf16[128,512]{1,0:T(8,128)(2,1)S(1)}, bf16[128,512]{1,0:T(8,128)(2,1)S(1)}, u32[]{:S(2)}, u32[]{:S(2)}) collective-permute-start(bf16[128,512]{1,0:T(8,128)(2,1)S(1)} %fusion.7.refs_0_), channel_id=1, source_target_pairs={{0,16},{2,18},{4,20},{6,22},{8,24},{10,26},{12,28},{14,30},{16,0},... | collective-permute-start | bytes 393224 | tf_op jit(solution)/shard_map/ppermute | solution.py:153
  56.3 0.2 fusion.onehot_ref
  56.6 1.2 collective-permute-start.14
  57.8 1.2 collective-permute-start.8
  59.0 3.8 %collective-permute-start.9 = (bf16[128,512]{1,0:T(8,128)(2,1)S(1)}, bf16[128,512]{1,0:T(8,128)(2,1)S(1)}, u32[]{:S(2)}, u32[]{:S(2)}) collective-permute-start(bf16[128,512]{1,0:T(8,128)(2,1)S(1)} %fusion.7.refs_0_), channel_id=1, source_target_pairs={{0,28},{2,30},{4,24},{6,26},{8,20},{10,22},{12,16},{14,18},{16,12}... | collective-permute-start | bytes 393224 | tf_op jit(solution)/shard_map/ppermute | solution.py:153
  62.8 0.5 collective-permute-start.22
  63.4 2.2 %copy-done.2 = bf16[256,8192]{1,0:T(8,128)(2,1)S(1)} copy-done((bf16[256,8192]{1,0:T(8,128)(2,1)S(1)}, bf16[256,8192]{1,0:T(8,128)(2,1)}, u32[]{:S(2)}) %copy-start.2) | copy-done | bytes 4194328
  65.5 12.2 %advance_rows.1.refs_6_.refs_4_ = bf16[1024,8192]{1,0:T(8,128)(2,1)} custom-call(bf16[1024,256]{1,0:T(8,128)(2,1)S(1)} %fusion.onehot_ref, bf16[256,8192]{1,0:T(8,128)(2,1)S(1)} %copy-done.2), custom_call_target="tpu_custom_call" | custom-call | flops 4294967296 | bytes 20971520 | tf_op jit(solution)/shard_map/advance_rows/pallas_call | solution.py:51
  77.7 0.1 copy.11
  77.8 0.2 broadcast_in_dim.18
  78.1 0.8 gather_fusion.1
  79.3 0.4 collective-permute-start.16
  79.8 0.4 collective-permute-start.10
  80.3 19.4 %piece_scores.3.refs_10_ = f32[128,1024]{1,0:T(8,128)S(1)} custom-call(s32[6]{0:T(128)S(1)} %stack.91.place_ref, bf16[128,512]{1,0:T(8,128)(2,1)S(1)} %fusion.7.refs_0_, bf16[128,512]{1,0:T(8,128)(2,1)S(1)} %collective-permute-done.18.refs_1_, bf16[128,512]{1,0:T(8,128)(2,1)S(1)} %collective-permute-done.19.refs_2_, ...), custom_call_target="tpu_custom_call" | custom-call | flops 6442450944 | bytes 12582912 | tf_op jit(solution)/shard_map/piece_scores/pallas_call | solution.py:108
  99.7 19.5 %piece_scores.4.refs_8_ = f32[128,1024]{1,0:T(8,128)S(1)} custom-call(s32[6]{0:T(128)S(1)} %stack.84.place_ref, bf16[128,512]{1,0:T(8,128)(2,1)S(1)} %collective-permute-done.12.refs_0_, bf16[128,512]{1,0:T(8,128)(2,1)S(1)} %collective-permute-done.13.refs_1_, bf16[128,512]{1,0:T(8,128)(2,1)S(1)} %collective-permute-done.14.refs_2_, ...), custom_call_target="tpu_custom_call" | custom-call | flops 6442450944 | bytes 12582912 | tf_op jit(solution)/shard_map/piece_scores/pallas_call | solution.py:108
  119.2 13.8 %piece_scores.5 = f32[128,1024]{1,0:T(8,128)S(1)} custom-call(s32[4]{0:T(128)S(1)} %pad_add_fusion.place_ref, bf16[128,512]{1,0:T(8,128)(2,1)S(1)} %collective-permute-done.8.refs_0_, bf16[128,512]{1,0:T(8,128)(2,1)S(1)} %collective-permute-done.9.refs_1_, bf16[128,512]{1,0:T(8,128)(2,1)S(1)} %collective-permute-done.10.refs_2_, ...), custom_call_target="tpu_custom_call" | custom-call | flops 4294967296 | bytes 8388608 | tf_op jit(solution)/shard_map/piece_scores/pallas_call | solution.py:108
  133.1 0.1 reduce_sum.9
  133.2 1.6 %collective-permute-start.24 = (f32[1,128]{1,0:T(1,128)S(1)}, f32[1,128]{1,0:T(1,128)S(1)}, u32[]{:S(2)}, u32[]{:S(2)}) collective-permute-start(f32[1,128]{1,0:T(1,128)S(1)} %bitcast.66), channel_id=1, source_target_pairs={{0,1},{1,0},{2,3},{3,2},{4,5},{5,4},{6,7},{7,6},{8,9},{9,8},{10,11... | collective-permute-start | bytes 1544 | tf_op jit(solution)/shard_map/ppermute | solution.py:195
  134.8 0.6 collective-permute-start.23
  135.3 1.4 collective-permute-done.24
  136.8 1.6 %collective-permute-start.25 = (f32[1,128]{1,0:T(1,128)S(1)}, f32[1,128]{1,0:T(1,128)S(1)}, u32[]{:S(2)}, u32[]{:S(2)}) collective-permute-start(f32[1,128]{1,0:T(1,128)S(1)} %bitcast_add_fusion.1), channel_id=1, source_target_pairs={{0,16},{2,18},{4,20},{6,22},{8,24},{10,26},{12,28},{14,30},{16,0},... | collective-permute-start | bytes 1544 | tf_op jit(solution)/shard_map/ppermute | solution.py:153
  138.4 2.8 %collective-permute-done.25 = f32[1,128]{1,0:T(1,128)S(1)} collective-permute-done((f32[1,128]{1,0:T(1,128)S(1)}, f32[1,128]{1,0:T(1,128)S(1)}, u32[]{:S(2)}, u32[]{:S(2)}) %collective-permute-start.25) | collective-permute-done | bytes 544 | tf_op jit(solution)/shard_map/ppermute | solution.py:153
  141.2 9.0 %collective-permute-start.26 = (f32[1,128]{1,0:T(1,128)S(1)}, f32[1,128]{1,0:T(1,128)S(1)}, u32[]{:S(2)}, u32[]{:S(2)}) collective-permute-start(f32[1,128]{1,0:T(1,128)S(1)} %add.172), channel_id=1, source_target_pairs={{0,8},{2,10},{4,12},{6,14},{8,0},{10,2},{12,4},{14,6},{16,24},{18,... | collective-permute-start | bytes 1544 | tf_op jit(solution)/shard_map/ppermute | solution.py:153
  150.2 1.5 collective-permute-done.26
  151.8 0.5 collective-permute-start.27
  152.3 3.0 %collective-permute-done.27 = f32[1,128]{1,0:T(1,128)S(1)} collective-permute-done((f32[1,128]{1,0:T(1,128)S(1)}, f32[1,128]{1,0:T(1,128)S(1)}, u32[]{:S(2)}, u32[]{:S(2)}) %collective-permute-start.27) | collective-permute-done | bytes 544 | tf_op jit(solution)/shard_map/ppermute | solution.py:153
  155.3 1.1 collective-permute-done.28
  156.5 0.8 subtract_select_fusion
  (56 shorter events, 0.9 us)
Async XLA Ops:
  0.0 78.1 %copy-start = (s32[256,1024]{1,0:T(8,128)S(1)}, s32[256,1024]{1,0:T(8,128)}, u32[]{:S(2)}) copy-start(s32[256,1024]{1,0:T(8,128)} %param.14) | copy-start | bytes 3145732
  0.1 1.0 copy-start.3
  1.1 30.0 %copy-start.5 = (s32[256,8]{0,1:T(8,128)S(1)}, s32[256,8]{0,1:T(8,128)}, u32[]{:S(2)}) copy-start(s32[256,8]{0,1:T(8,128)} %param.13) | copy-start | bytes 24580
  1.1 30.1 %copy-start.7 = (s32[128]{0:T(128)S(1)}, s32[128]{0:T(128)}, u32[]{:S(2)}) copy-start(s32[128]{0:T(128)} %param.12) | copy-start | bytes 1540
  8.4 7.9 %collective-permute-start = (bf16[8,128,512]{2,1,0:T(8,128)(2,1)S(1)}, bf16[8,128,512]{2,1,0:T(8,128)(2,1)S(1)}, u32[]{:S(2)}, u32[]{:S(2)}) collective-permute-start(bf16[8,128,512]{2,1,0:T(8,128)(2,1)S(1)} %prior_half.3), channel_id=1, source_target_pairs={{0,2},{2,0},{4,6},{6,4},{8,10},{10,8},{12,14},{14,12},{16,18},{18,... | collective-permute-start | bytes 3145736 | tf_op jit(solution)/shard_map/ppermute | solution.py:153
  16.3 61.4 %copy-start.6 = (s32[128,8]{0,1:T(8,128)S(1)}, s32[128,8]{0,1:T(8,128)}, u32[]{:S(2)}) copy-start(s32[128,8]{0,1:T(8,128)} %param.15) | copy-start | bytes 12292
  17.3 8.4 %collective-permute-start.1 = (bf16[128,512]{1,0:T(8,128)(2,1)S(1)}, bf16[128,512]{1,0:T(8,128)(2,1)S(1)}, u32[]{:S(2)}, u32[]{:S(2)}) collective-permute-start(bf16[128,512]{1,0:T(8,128)(2,1)S(1)} %get-tuple-element.5), channel_id=1, source_target_pairs={{0,4},{2,6},{4,0},{6,2},{8,12},{10,14},{12,8},{14,10},{16,20},{18,... | collective-permute-start | bytes 393224 | tf_op jit(solution)/shard_map/ppermute | solution.py:153
  19.8 10.6 %collective-permute-start.2 = (bf16[128,512]{1,0:T(8,128)(2,1)S(1)}, bf16[128,512]{1,0:T(8,128)(2,1)S(1)}, u32[]{:S(2)}, u32[]{:S(2)}) collective-permute-start(bf16[128,512]{1,0:T(8,128)(2,1)S(1)} %get-tuple-element.11), channel_id=1, source_target_pairs={{0,8},{2,10},{4,12},{6,14},{8,0},{10,2},{12,4},{14,6},{16,24},{18,... | collective-permute-start | bytes 393224 | tf_op jit(solution)/shard_map/ppermute | solution.py:153
  21.4 11.0 %collective-permute-start.3 = (bf16[128,512]{1,0:T(8,128)(2,1)}, bf16[128,512]{1,0:T(8,128)(2,1)}, u32[]{:S(2)}, u32[]{:S(2)}) collective-permute-start(bf16[128,512]{1,0:T(8,128)(2,1)} %get-tuple-element.10), channel_id=1, source_target_pairs={{0,12},{2,14},{4,8},{6,10},{8,4},{10,6},{12,0},{14,2},{16,28},{18,... | collective-permute-start | bytes 393224 | tf_op jit(solution)/shard_map/ppermute | solution.py:153
  21.4 11.0 %collective-permute-start.4 = (bf16[128,512]{1,0:T(8,128)(2,1)}, bf16[128,512]{1,0:T(8,128)(2,1)}, u32[]{:S(2)}, u32[]{:S(2)}) collective-permute-start(bf16[128,512]{1,0:T(8,128)(2,1)} %get-tuple-element.9), channel_id=1, source_target_pairs={{0,16},{2,18},{4,20},{6,22},{8,24},{10,26},{12,28},{14,30},{16,0},... | collective-permute-start | bytes 393224 | tf_op jit(solution)/shard_map/ppermute | solution.py:153
  24.4 19.6 %collective-permute-start.5 = (bf16[128,512]{1,0:T(8,128)(2,1)}, bf16[128,512]{1,0:T(8,128)(2,1)}, u32[]{:S(2)}, u32[]{:S(2)}) collective-permute-start(bf16[128,512]{1,0:T(8,128)(2,1)} %get-tuple-element.8), channel_id=1, source_target_pairs={{0,20},{2,22},{4,16},{6,18},{8,28},{10,30},{12,24},{14,26},{16,4},... | collective-permute-start | bytes 393224 | tf_op jit(solution)/shard_map/ppermute | solution.py:153
  25.7 18.3 %collective-permute-start.6 = (bf16[128,512]{1,0:T(8,128)(2,1)}, bf16[128,512]{1,0:T(8,128)(2,1)}, u32[]{:S(2)}, u32[]{:S(2)}) collective-permute-start(bf16[128,512]{1,0:T(8,128)(2,1)} %get-tuple-element.7), channel_id=1, source_target_pairs={{0,24},{2,26},{4,28},{6,30},{8,16},{10,18},{12,20},{14,22},{16,8},... | collective-permute-start | bytes 393224 | tf_op jit(solution)/shard_map/ppermute | solution.py:153
  30.4 0.7 copy-start.4
  31.1 12.9 %collective-permute-start.7 = (bf16[128,512]{1,0:T(8,128)(2,1)}, bf16[128,512]{1,0:T(8,128)(2,1)}, u32[]{:S(2)}, u32[]{:S(2)}) collective-permute-start(bf16[128,512]{1,0:T(8,128)(2,1)} %get-tuple-element.6), channel_id=1, source_target_pairs={{0,28},{2,30},{4,24},{6,26},{8,20},{10,22},{12,16},{14,18},{16,12}... | collective-permute-start | bytes 393224 | tf_op jit(solution)/shard_map/ppermute | solution.py:153
  45.4 11.2 %collective-permute-start.18 = (bf16[128,512]{1,0:T(8,128)(2,1)S(1)}, bf16[128,512]{1,0:T(8,128)(2,1)S(1)}, u32[]{:S(2)}, u32[]{:S(2)}) collective-permute-start(bf16[128,512]{1,0:T(8,128)(2,1)S(1)} %fusion.7.refs_0_), channel_id=1, source_target_pairs={{0,4},{2,6},{4,0},{6,2},{8,12},{10,14},{12,8},{14,10},{16,20},{18,... | collective-permute-start | bytes 393224 | tf_op jit(solution)/shard_map/ppermute | solution.py:153
  46.9 10.9 %collective-permute-start.19 = (bf16[128,512]{1,0:T(8,128)(2,1)S(1)}, bf16[128,512]{1,0:T(8,128)(2,1)S(1)}, u32[]{:S(2)}, u32[]{:S(2)}) collective-permute-start(bf16[128,512]{1,0:T(8,128)(2,1)S(1)} %fusion.7.refs_0_), channel_id=1, source_target_pairs={{0,8},{2,10},{4,12},{6,14},{8,0},{10,2},{12,4},{14,6},{16,24},{18,... | collective-permute-start | bytes 393224 | tf_op jit(solution)/shard_map/ppermute | solution.py:153
  51.6 7.4 %collective-permute-start.20 = (bf16[128,512]{1,0:T(8,128)(2,1)S(1)}, bf16[128,512]{1,0:T(8,128)(2,1)S(1)}, u32[]{:S(2)}, u32[]{:S(2)}) collective-permute-start(bf16[128,512]{1,0:T(8,128)(2,1)S(1)} %fusion.7.refs_0_), channel_id=1, source_target_pairs={{0,2},{2,0},{4,6},{6,4},{8,10},{10,8},{12,14},{14,12},{16,18},{18,... | collective-permute-start | bytes 393224 | tf_op jit(solution)/shard_map/ppermute | solution.py:153
  51.6 11.2 %collective-permute-start.12 = (bf16[128,512]{1,0:T(8,128)(2,1)S(1)}, bf16[128,512]{1,0:T(8,128)(2,1)S(1)}, u32[]{:S(2)}, u32[]{:S(2)}) collective-permute-start(bf16[128,512]{1,0:T(8,128)(2,1)S(1)} %fusion.7.refs_0_), channel_id=1, source_target_pairs={{0,12},{2,14},{4,8},{6,10},{8,4},{10,6},{12,0},{14,2},{16,28},{18,... | collective-permute-start | bytes 393224 | tf_op jit(solution)/shard_map/ppermute | solution.py:153
  52.2 10.7 %collective-permute-start.13 = (bf16[128,512]{1,0:T(8,128)(2,1)S(1)}, bf16[128,512]{1,0:T(8,128)(2,1)S(1)}, u32[]{:S(2)}, u32[]{:S(2)}) collective-permute-start(bf16[128,512]{1,0:T(8,128)(2,1)S(1)} %fusion.7.refs_0_), channel_id=1, source_target_pairs={{0,16},{2,18},{4,20},{6,22},{8,24},{10,26},{12,28},{14,30},{16,0},... | collective-permute-start | bytes 393224 | tf_op jit(solution)/shard_map/ppermute | solution.py:153
  56.6 22.6 %collective-permute-start.14 = (bf16[128,512]{1,0:T(8,128)(2,1)S(1)}, bf16[128,512]{1,0:T(8,128)(2,1)S(1)}, u32[]{:S(2)}, u32[]{:S(2)}) collective-permute-start(bf16[128,512]{1,0:T(8,128)(2,1)S(1)} %fusion.7.refs_0_), channel_id=1, source_target_pairs={{0,20},{2,22},{4,16},{6,18},{8,28},{10,30},{12,24},{14,26},{16,4},... | collective-permute-start | bytes 393224 | tf_op jit(solution)/shard_map/ppermute | solution.py:153
  57.8 21.5 %collective-permute-start.8 = (bf16[128,512]{1,0:T(8,128)(2,1)S(1)}, bf16[128,512]{1,0:T(8,128)(2,1)S(1)}, u32[]{:S(2)}, u32[]{:S(2)}) collective-permute-start(bf16[128,512]{1,0:T(8,128)(2,1)S(1)} %fusion.7.refs_0_), channel_id=1, source_target_pairs={{0,24},{2,26},{4,28},{6,30},{8,16},{10,18},{12,20},{14,22},{16,8},... | collective-permute-start | bytes 393224 | tf_op jit(solution)/shard_map/ppermute | solution.py:153
  59.0 20.7 %collective-permute-start.9 = (bf16[128,512]{1,0:T(8,128)(2,1)S(1)}, bf16[128,512]{1,0:T(8,128)(2,1)S(1)}, u32[]{:S(2)}, u32[]{:S(2)}) collective-permute-start(bf16[128,512]{1,0:T(8,128)(2,1)S(1)} %fusion.7.refs_0_), channel_id=1, source_target_pairs={{0,28},{2,30},{4,24},{6,26},{8,20},{10,22},{12,16},{14,18},{16,12}... | collective-permute-start | bytes 393224 | tf_op jit(solution)/shard_map/ppermute | solution.py:153
  62.8 17.0 %collective-permute-start.21 = (bf16[128,512]{1,0:T(8,128)(2,1)S(1)}, bf16[128,512]{1,0:T(8,128)(2,1)S(1)}, u32[]{:S(2)}, u32[]{:S(2)}) collective-permute-start(bf16[128,512]{1,0:T(8,128)(2,1)S(1)} %collective-permute-done.18.refs_1_), channel_id=1, source_target_pairs={{0,2},{2,0},{4,6},{6,4},{8,10},{10,8},{12,14},{14,12},{16,18},{18,... | collective-permute-start | bytes 393224 | tf_op jit(solution)/shard_map/ppermute | solution.py:153
  62.8 17.4 %collective-permute-start.22 = (bf16[128,512]{1,0:T(8,128)(2,1)S(1)}, bf16[128,512]{1,0:T(8,128)(2,1)S(1)}, u32[]{:S(2)}, u32[]{:S(2)}) collective-permute-start(bf16[128,512]{1,0:T(8,128)(2,1)S(1)} %collective-permute-done.19.refs_2_), channel_id=1, source_target_pairs={{0,2},{2,0},{4,6},{6,4},{8,10},{10,8},{12,14},{14,12},{16,18},{18,... | collective-permute-start | bytes 393224 | tf_op jit(solution)/shard_map/ppermute | solution.py:153
  63.4 2.2 %copy-start.2 = (bf16[256,8192]{1,0:T(8,128)(2,1)S(1)}, bf16[256,8192]{1,0:T(8,128)(2,1)}, u32[]{:S(2)}) copy-start(bf16[256,8192]{1,0:T(8,128)(2,1)} %adv_ref.1) | copy-start | bytes 12582916
  79.2 20.5 %collective-permute-start.15 = (bf16[128,512]{1,0:T(8,128)(2,1)S(1)}, bf16[128,512]{1,0:T(8,128)(2,1)S(1)}, u32[]{:S(2)}, u32[]{:S(2)}) collective-permute-start(bf16[128,512]{1,0:T(8,128)(2,1)S(1)} %collective-permute-done.12.refs_0_), channel_id=1, source_target_pairs={{0,2},{2,0},{4,6},{6,4},{8,10},{10,8},{12,14},{14,12},{16,18},{18,... | collective-permute-start | bytes 393224 | tf_op jit(solution)/shard_map/ppermute | solution.py:153
  79.3 20.4 %collective-permute-start.16 = (bf16[128,512]{1,0:T(8,128)(2,1)S(1)}, bf16[128,512]{1,0:T(8,128)(2,1)S(1)}, u32[]{:S(2)}, u32[]{:S(2)}) collective-permute-start(bf16[128,512]{1,0:T(8,128)(2,1)S(1)} %collective-permute-done.13.refs_1_), channel_id=1, source_target_pairs={{0,2},{2,0},{4,6},{6,4},{8,10},{10,8},{12,14},{14,12},{16,18},{18,... | collective-permute-start | bytes 393224 | tf_op jit(solution)/shard_map/ppermute | solution.py:153
  79.7 20.0 %collective-permute-start.17 = (bf16[128,512]{1,0:T(8,128)(2,1)S(1)}, bf16[128,512]{1,0:T(8,128)(2,1)S(1)}, u32[]{:S(2)}, u32[]{:S(2)}) collective-permute-start(bf16[128,512]{1,0:T(8,128)(2,1)S(1)} %collective-permute-done.14.refs_2_), channel_id=1, source_target_pairs={{0,2},{2,0},{4,6},{6,4},{8,10},{10,8},{12,14},{14,12},{16,18},{18,... | collective-permute-start | bytes 393224 | tf_op jit(solution)/shard_map/ppermute | solution.py:153
  79.8 39.4 %collective-permute-start.10 = (bf16[128,512]{1,0:T(8,128)(2,1)S(1)}, bf16[128,512]{1,0:T(8,128)(2,1)S(1)}, u32[]{:S(2)}, u32[]{:S(2)}) collective-permute-start(bf16[128,512]{1,0:T(8,128)(2,1)S(1)} %collective-permute-done.8.refs_0_), channel_id=1, source_target_pairs={{0,2},{2,0},{4,6},{6,4},{8,10},{10,8},{12,14},{14,12},{16,18},{18,... | collective-permute-start | bytes 393224 | tf_op jit(solution)/shard_map/ppermute | solution.py:153
  80.2 39.0 %collective-permute-start.11 = (bf16[128,512]{1,0:T(8,128)(2,1)S(1)}, bf16[128,512]{1,0:T(8,128)(2,1)S(1)}, u32[]{:S(2)}, u32[]{:S(2)}) collective-permute-start(bf16[128,512]{1,0:T(8,128)(2,1)S(1)} %collective-permute-done.9.refs_1_), channel_id=1, source_target_pairs={{0,2},{2,0},{4,6},{6,4},{8,10},{10,8},{12,14},{14,12},{16,18},{18,... | collective-permute-start | bytes 393224 | tf_op jit(solution)/shard_map/ppermute | solution.py:153
  99.7 57.6 %copy-start.1 = (s32[256,1024]{1,0:T(8,128)S(1)}, s32[256,1024]{1,0:T(8,128)}, u32[]{:S(2)}) copy-start(s32[256,1024]{1,0:T(8,128)} %param.14) | copy-start | bytes 3145732
  133.2 3.6 %collective-permute-start.24 = (f32[1,128]{1,0:T(1,128)S(1)}, f32[1,128]{1,0:T(1,128)S(1)}, u32[]{:S(2)}, u32[]{:S(2)}) collective-permute-start(f32[1,128]{1,0:T(1,128)S(1)} %bitcast.66), channel_id=1, source_target_pairs={{0,1},{1,0},{2,3},{3,2},{4,5},{5,4},{6,7},{7,6},{8,9},{9,8},{10,11... | collective-permute-start | bytes 1544 | tf_op jit(solution)/shard_map/ppermute | solution.py:195
  134.8 21.8 %collective-permute-start.23 = (bf16[64,1024]{1,0:T(8,128)(2,1)S(1)}, bf16[64,1024]{1,0:T(8,128)(2,1)S(1)}, u32[]{:S(2)}, u32[]{:S(2)}) collective-permute-start(bf16[64,1024]{1,0:T(8,128)(2,1)S(1)} %dynamic-slice_convert_fusion), channel_id=1, source_target_pairs={{0,1},{1,0},{2,3},{3,2},{4,5},{5,4},{6,7},{7,6},{8,9},{9,8},{10,11... | collective-permute-start | bytes 393224 | tf_op jit(solution)/shard_map/ppermute | solution.py:202
  136.8 4.4 %collective-permute-start.25 = (f32[1,128]{1,0:T(1,128)S(1)}, f32[1,128]{1,0:T(1,128)S(1)}, u32[]{:S(2)}, u32[]{:S(2)}) collective-permute-start(f32[1,128]{1,0:T(1,128)S(1)} %bitcast_add_fusion.1), channel_id=1, source_target_pairs={{0,16},{2,18},{4,20},{6,22},{8,24},{10,26},{12,28},{14,30},{16,0},... | collective-permute-start | bytes 1544 | tf_op jit(solution)/shard_map/ppermute | solution.py:153
  141.2 10.5 %collective-permute-start.26 = (f32[1,128]{1,0:T(1,128)S(1)}, f32[1,128]{1,0:T(1,128)S(1)}, u32[]{:S(2)}, u32[]{:S(2)}) collective-permute-start(f32[1,128]{1,0:T(1,128)S(1)} %add.172), channel_id=1, source_target_pairs={{0,8},{2,10},{4,12},{6,14},{8,0},{10,2},{12,4},{14,6},{16,24},{18,... | collective-permute-start | bytes 1544 | tf_op jit(solution)/shard_map/ppermute | solution.py:153
  151.8 3.5 %collective-permute-start.27 = (f32[1,128]{1,0:T(1,128)S(1)}, f32[1,128]{1,0:T(1,128)S(1)}, u32[]{:S(2)}, u32[]{:S(2)}) collective-permute-start(f32[1,128]{1,0:T(1,128)S(1)} %add.173), channel_id=1, source_target_pairs={{0,4},{2,6},{4,0},{6,2},{8,12},{10,14},{12,8},{14,10},{16,20},{18,... | collective-permute-start | bytes 1544 | tf_op jit(solution)/shard_map/ppermute | solution.py:153
  155.3 1.1 collective-permute-start.28

commit v2 on v0

v2 whole, which is shorter than its diff:
```python
import functools
import jax
import jax.numpy as jnp
from jax import lax
from jax.experimental import pallas as pl
from jax.experimental.pallas import tpu as pltpu
from jax.sharding import PartitionSpec as P

BLK = 128
GROUP = 32
UNIT = 256
BATCH = 4
CHEAP = 1 << 20
BF16 = jnp.bfloat16
F32 = jnp.float32
FAR_OTHER, FAR_SAME, NEAR_OTHER, NEAR_SAME = (5, 7), (4, 6), (1, 3), (0, 2)
ORDER = FAR_OTHER + FAR_SAME + NEAR_OTHER + NEAR_SAME


def params(mib):
    return pltpu.CompilerParams(vmem_limit_bytes=mib << 20)


def cheap():
    return pl.CostEstimate(flops=CHEAP, bytes_accessed=CHEAP, transcendentals=0)


def piece_place(chips, other, bits):
    me = lax.axis_index("vocab")
    core, chip = lax.rem(me, 2), lax.div(me, 2)
    return (1 - core if other else core) * chips + (chip ^ bits)


def transposed_dot(a, b):
    return lax.dot_general(a, b, (((0,), (0,)), ((), ())), preferred_element_type=F32)


SMEM = pl.BlockSpec(memory_space=pltpu.SMEM)
VMEM = pl.BlockSpec(memory_space=pltpu.VMEM)
HBM = pl.BlockSpec(memory_space=pltpu.HBM)


def half_product(posterior, transition, other, order, chips, width):
    rows, depth = posterior.shape
    pieces = len(order)

    def kernel(post_ref, trans_ref, out_ref, held, arrived):
        def copy(n):
            first = piece_place(chips, other, order[n])
            columns = pl.ds(pl.multiple_of(first * width, width), width)
            return pltpu.make_async_copy(trans_ref.at[:, columns], held.at[n], arrived.at[n])

        for n in range(pieces):
            copy(n).start()
        for n in range(pieces):
            copy(n).wait()
            out_ref[n] = jnp.dot(post_ref[...], held[n], preferred_element_type=F32).astype(BF16)

    return pl.pallas_call(
        kernel,
        in_specs=[VMEM, HBM],
        out_specs=VMEM,
        out_shape=jax.ShapeDtypeStruct((pieces, rows, width), BF16),
        scratch_shapes=[pltpu.VMEM((pieces, depth, width), BF16), pltpu.SemaphoreType.DMA((pieces,))],
        compiler_params=params(50),
        cost_estimate=cheap(),
        name="prior_half",
    )(posterior, transition)


def prepare(allowed, state, edge_next, token_edge, advance, tile):
    blocks, rows = allowed.shape
    states, columns = token_edge.shape
    slots = edge_next.shape[1]
    hidden = advance.shape[1]
    tiles = columns // tile
    each = tile // BLK
    seats = tiles * rows
    width = min(1024, hidden)
    steps = hidden // width
    pair = 2

    def kernel(allow_ref, state_ref, next_ref, token_ref, adv_ref, head_ref, select_ref, edge_ref, look_ref, hot, after, held, left):
        who = (lax.broadcasted_iota(jnp.int32, (states, rows), 0) == state_ref[...]).astype(F32).astype(BF16)
        allow = allow_ref[...].astype(F32)
        earlier = lax.broadcasted_iota(jnp.int32, (rows, rows), 0) < lax.broadcasted_iota(jnp.int32, (rows, rows), 1)
        earlier = earlier.astype(F32).astype(BF16)
        number = lax.broadcasted_iota(jnp.int32, (seats, rows), 0)
        taken = jnp.zeros((seats, rows), F32)
        used = jnp.int32(0)
        for t in range(tiles):
            need = allow[t * each : t * each + 1]
            for b in range(1, each):
                need = jnp.maximum(need, allow[t * each + b : t * each + b + 1])
            rank = jnp.dot(jnp.broadcast_to(need, (8, rows)).astype(BF16), earlier, preferred_element_type=F32)[0:1]
            units = (jnp.sum(need).astype(jnp.int32) + GROUP - 1) // GROUP
            seat = jnp.where(need > 0, rank.astype(jnp.int32) + used * GROUP, -1)
            taken += (number == seat).astype(F32)

            @pl.loop(0, units)
            def _(u):
                head_ref[1 + used + u] = t

            used = used + units
        head_ref[0] = used
        taken = taken.astype(BF16)
        select_ref[...] = taken
        following = transposed_dot(who, next_ref[...].astype(F32).astype(BF16))
        after[...] = jnp.dot(taken, following.astype(BF16), preferred_element_type=F32).astype(jnp.int32)
        names = lax.broadcasted_iota(jnp.int32, (GROUP, states), 1)

        def copy(c, n):
            span = pl.ds(pl.multiple_of(c * pair * UNIT, pair * UNIT), pair * UNIT)
            return pltpu.make_async_copy(held.at[n], look_ref.at[span, pl.ds(n * width, width)], left.at[n])

        chunks = (used + pair - 1) // pair

        @pl.loop(0, chunks)
        def _(c):
            for u in range(pair):
                succ = after[pl.ds(pl.multiple_of((c * pair + u) * GROUP, GROUP), GROUP), :]
                for k in range(slots):
                    hot[u * UNIT + k * GROUP : u * UNIT + (k + 1) * GROUP, :] = (
                        (names == succ[:, k : k + 1]).astype(F32).astype(BF16)
                    )
            for n in range(steps):

                @pl.when(c > 0)
                def _():
                    copy(c - 1, n).wait()

                held[n] = jnp.dot(
                    hot[...], adv_ref[:, n * width : (n + 1) * width], preferred_element_type=F32
                ).astype(BF16)
                copy(c, n).start()

        allow = allow.astype(BF16)
        token = token_ref[...].astype(F32).astype(BF16)
        slot = transposed_dot(who, token)
        block = lax.broadcasted_iota(jnp.int32, (blocks, columns), 1) // BLK
        spread = (block == lax.broadcasted_iota(jnp.int32, (blocks, columns), 0)).astype(F32).astype(BF16)
        edge_ref[...] = jnp.where(transposed_dot(allow, spread) > 0, slot, float(slots)).astype(BF16)

        @pl.when(chunks > 0)
        def _():
            for n in range(steps):
                copy(chunks - 1, n).wait()

    return pl.pallas_call(
        kernel,
        in_specs=[VMEM] * 5,
        out_specs=[SMEM, VMEM, VMEM, HBM],
        scratch_shapes=[
            pltpu.VMEM((pair * UNIT, states), BF16),
            pltpu.VMEM((seats, slots), jnp.int32),
            pltpu.VMEM((steps, pair * UNIT, width), BF16),
            pltpu.SemaphoreType.DMA((steps,)),
        ],
        out_shape=[
            jax.ShapeDtypeStruct((1 + seats // GROUP,), jnp.int32),
            jax.ShapeDtypeStruct((seats, rows), BF16),
            jax.ShapeDtypeStruct((rows, columns), BF16),
            jax.ShapeDtypeStruct((seats * slots, hidden), BF16),
        ],
        compiler_params=params(16),
        cost_estimate=cheap(),
        name="prepare",
    )(allowed, state, edge_next, token_edge, advance)


def piece_scores(arrays, places, head, select, look, emission, edges, before, slots, tile, last, local):
    each, rows, width = arrays[0].shape
    count = len(arrays) * each
    columns = emission.shape[1]
    seats = select.shape[0]
    started = before is not None

    def kernel(head_ref, *refs):
        piece_refs = refs[: len(arrays)]
        select_ref, look_ref, emit_ref, edge_ref = refs[len(arrays) : len(arrays) + 4]
        before_ref = refs[len(arrays) + 4] if started else None
        looks, prior, total, arrived = refs[-4:]
        outs = refs[len(arrays) + 4 + started : -4]
        units = head_ref[0]
        deep = [pl.ds(pl.multiple_of(place * width, width), width) for place in places()]

        def look_copy(i, c, u):
            here = pl.ds(pl.multiple_of((c * BATCH + u) * UNIT, UNIT), UNIT)
            return pltpu.make_async_copy(look_ref.at[here, deep[i]], looks.at[i, u], arrived.at[i, u])

        if last:
            total[...] = jnp.zeros_like(total)

        @pl.loop(0, (units + BATCH - 1) // BATCH)
        def _(c):
            here = jnp.minimum(units - c * BATCH, BATCH)

            @pl.loop(0, here)
            def _(u):
                for i in range(count):
                    look_copy(i, c, u).start()

            span = pl.ds(pl.multiple_of(c * BATCH * GROUP, BATCH * GROUP), BATCH * GROUP)
            for i in range(count):
                prior[i] = jnp.dot(
                    select_ref[span, :], piece_refs[i // each][i % each], preferred_element_type=F32
                ).astype(BF16)

            @pl.loop(0, here)
            def _(u):
                at = pl.multiple_of(head_ref[1 + c * BATCH + u] * tile, tile)
                span = pl.ds(pl.multiple_of((c * BATCH + u) * GROUP, GROUP), GROUP)
                seat = pl.ds(pl.multiple_of(u * GROUP, GROUP), GROUP)
                for i in range(count):
                    look_copy(i, c, u).wait()
                values = None
                for i in range(count):
                    rowed = looks[i, u].reshape(slots, GROUP, width)
                    weighted = (rowed * prior[i, seat, :][None]).reshape(UNIT, width)
                    part = jnp.dot(weighted, emit_ref[deep[i], pl.ds(at, tile)], preferred_element_type=F32)
                    values = part if values is None else values + part
                own = select_ref[span, :]
                edge = jnp.dot(own, edge_ref[:, pl.ds(at, tile)], preferred_element_type=F32)
                chosen = before_ref[span, :] if started else jnp.zeros((GROUP, tile), F32)
                for k in range(slots):
                    chosen += jnp.where(edge == k, values[k * GROUP : (k + 1) * GROUP], 0.0)
                if not last:
                    outs[0][span, :] = chosen
                    return
                spread = jnp.zeros((rows, tile), F32)
                for _ in range(3):
                    high = chosen.astype(BF16)
                    chosen = chosen - high.astype(F32)
                    spread += transposed_dot(own, high)
                total[:, pl.ds(at, tile)] += spread

        if last:
            first = lax.axis_index("hid") * local if local < rows else 0
            outs[0][...] = total[pl.ds(pl.multiple_of(first, local), local), :]
            theirs = local - first if local < rows else 0
            outs[1][...] = total[pl.ds(pl.multiple_of(theirs, local), local), :].astype(BF16)
            sums = jnp.sum(total[...], axis=1, keepdims=True)
            outs[2][...] = jnp.broadcast_to(sums, (rows, 128)).T[0:1, :]

    if last:
        shapes = [((local, columns), F32), ((local, columns), BF16), ((1, rows), F32)]
    else:
        shapes = [((seats, tile), F32)]
    return pl.pallas_call(
        kernel,
        in_specs=[SMEM] + [VMEM] * len(arrays) + [VMEM, HBM, VMEM, VMEM] + [VMEM] * started,
        out_specs=[VMEM] * len(shapes),
        scratch_shapes=[
            pltpu.VMEM((count, BATCH, UNIT, width), BF16),
            pltpu.VMEM((count, BATCH * GROUP, width), BF16),
            pltpu.VMEM((rows, columns), F32),
            pltpu.SemaphoreType.DMA((count, BATCH)),
        ],
        out_shape=[jax.ShapeDtypeStruct(*shape) for shape in shapes],
        compiler_params=params(12),
        cost_estimate=cheap(),
        name="piece_scores",
    )(head, *arrays, select, look, emission, edges, *([before] if started else []))


def body(sizes, posterior, transition, emission, advance, dfa_state, edge_next, token_edge, allowed):
    vocab_size, hid_size = sizes
    rows = posterior.shape[0]
    hidden = transition.shape[1]
    slots = edge_next.shape[1]
    chips = vocab_size // 2
    width = hidden // vocab_size
    direct = chips == 8 and width % 128 == 0
    local = rows // hid_size
    first = lax.axis_index("hid") * local
    blocks = allowed.shape[1]
    tile = min(2, blocks) * BLK

    def swap(array, bits):
        return lax.ppermute(array, "vocab", [(i, i ^ bits) for i in range(vocab_size)])

    def made_ready(allowed, dfa_state, edge_next, token_edge, advance):
        return prepare(allowed.T, dfa_state[None, :], edge_next, token_edge, advance, tile)

    small = (allowed, dfa_state, edge_next, token_edge, advance)
    if direct:
        away = half_product(posterior, transition, True, ORDER, chips, width)
        came = swap(away, 1)
        kept = half_product(posterior, transition, False, ORDER, chips, width)
        parts = [(kept[n : n + 2].astype(F32) + came[n : n + 2].astype(F32)).astype(BF16) for n in (0, 2, 4, 6)]
        parts, small = lax.optimization_barrier((parts, small))
        far = swap(parts[0], 2)
        near = swap(parts[2], 2)
        far, small = lax.optimization_barrier((far, small))
        far = parts[1].astype(F32) + far.astype(F32)
        sent = [swap(far[0].astype(BF16), 8), swap(far[1].astype(BF16), 12)]
        near = parts[3].astype(F32) + near.astype(F32)
        sent.append(swap(near[1].astype(BF16), 4))
        head, select, edges, look = made_ready(*small)
        sent, head, select, edges, look = lax.optimization_barrier((sent, head, select, edges, look))
        own = near[0] + sent[0].astype(F32) + sent[1].astype(F32) + sent[2].astype(F32)
        own = own.astype(BF16)

        far = [swap(own, 8), swap(own, 12)]
        near = jnp.stack([own, swap(own, 4)])
        batches = [(near, NEAR_SAME)]
        batches.append((swap(near, 2), NEAR_OTHER))
        far = jnp.stack(far)
        batches.append((far, FAR_SAME))
        batches.append((swap(far, 2), FAR_OTHER))

        def one_batch(array, bits, before, last):
            def places():
                return [piece_place(chips, other, b) for other in (False, True) for b in bits]

            return piece_scores(
                [array, swap(array, 1)], places, head, select, look, emission, edges, before, slots, tile, last, local
            )

    else:
        own = lax.psum_scatter(
            jnp.dot(posterior, transition, preferred_element_type=F32), "vocab", scatter_dimension=0, tiled=True
        ).astype(BF16)
        prior = lax.all_gather(own, "vocab", axis=0, tiled=True)
        head, select, edges, look = made_ready(*small)
        wide = min(512, hidden)
        batches = [(prior[None, :, wide * j : wide * (j + 1)], j) for j in range(hidden // wide)]

        def one_batch(array, j, before, last):
            return piece_scores(
                [array], lambda: [j], head, select, look, emission, edges, before, slots, tile, last, rows
            )

    chosen = None
    for n, (array, where) in enumerate(batches):
        got = one_batch(array, where, chosen, n == len(batches) - 1)
        chosen = got[0]
    mine, theirs, part = got

    if hid_size == 2:
        part = part + lax.ppermute(part, "hid", [(0, 1), (1, 0)])
        bits = vocab_size // 2
        while bits:
            part = part + swap(part, bits)
            bits //= 2
        totals = lax.dynamic_slice_in_dim(part[0], first, local, 0)
        mine = mine + lax.ppermute(theirs, "hid", [(0, 1), (1, 0)]).astype(F32)
    else:
        mine = lax.psum_scatter(theirs, "hid", scatter_dimension=0, tiled=True).astype(F32)
        totals = lax.psum(jnp.sum(mine, axis=1), "vocab")
    mask = jnp.repeat(lax.dynamic_slice_in_dim(allowed, first, local, 0), BLK, axis=1) > 0
    safe = jnp.where(mask, mine, jnp.float32(1.0))
    return jnp.where(mask, jnp.log(safe) - jnp.log(totals)[:, None], jnp.float32(0.0))


def solution(mesh):
    in_specs = (
        P(None, "vocab"),
        P("vocab", "hid"),
        P("hid", "vocab"),
        P(None, "hid"),
        P(),
        P(),
        P(None, "vocab"),
        P(None, "vocab"),
    )
    sizes = (mesh.shape["vocab"], mesh.shape["hid"])
    return jax.shard_map(
        functools.partial(body, sizes), mesh=mesh, in_specs=in_specs, out_specs=P("hid", "vocab"), check_vma=False
    )
```

time: 228 us -> 106 us (0.46)
  waiting for transfers between devices: 93.7 us -> 29.4 us
  matrix products: 47.1 us -> 0 us
  Pallas kernels: 0 us -> 35 us
  blocking collectives: 33.1 us -> 0 us
  starting transfers between devices: 0.3 us -> 27.5 us
  local copies, waits for them, and re-layouts: 33 us -> 12.3 us
  between operations: 13.3 us -> 0.24 us
  other arithmetic: 7.54 us -> 1.45 us
    reduce_scatter x2 -> x0, waiting for transfers between devices: 85.5 us -> none  [the longest x1 75.1 us: body(): lax.psum_scatter(jnp.dot(posterior, transition, preferred_element_type=jn...]
    dot_general x2 -> x0, matrix products: 47.1 us -> none  [the longest x1 36.8 us: request_scores(): jnp.dot(flattened, emission, preferred_element_type=jnp.float32)]
    pallas_call x0 -> x7, Pallas kernels: none -> 35 us  [the longest x4 17 us: piece_scores(): pl.pallas_call(kernel, in_specs=[SMEM] + [VMEM] * len(arrays) + [VMEM, HB...]
    psum x1 -> x0, blocking collectives: 33.1 us -> none  [body(): totals = lax.psum(jnp.sum(scores, axis=1), 'vocab')]
    gather x3 -> x0, local copies, waits for them, and re-layouts: 32.1 us -> none  [the longest x1 30.6 us: request_scores(): look_rows = jnp.take(advance, successor, axis=0)]
    ppermute x0 -> x21, waiting for transfers between devices: none -> 29.4 us  [the longest x19 25.6 us: swap(): lax.ppermute(array, 'vocab', [(i, i ^ bits) for i in range(vocab_size)])]
    ppermute x0 -> x21, starting transfers between devices: none -> 27.5 us  [the longest x19 24.7 us: swap(): lax.ppermute(array, 'vocab', [(i, i ^ bits) for i in range(vocab_size)])]
    unnamed x11 -> x16, local copies, waits for them, and re-layouts: 0.14 us -> 11.8 us
  transfers between devices with their start and end apart: 3 -> 21, of which waited for: 3 -> 12; matrix products, arithmetic and copies ran while one was open for 14% -> 1% of each run, Pallas kernels for 0% -> 24%
where the time goes in v2:
time: 106 us
  Pallas kernels  35 us (33%)
  waiting for transfers between devices  29.4 us (28%)
  starting transfers between devices  27.5 us (26%)
  local copies, waits for them, and re-layouts  12.3 us (12%)
  other arithmetic  1.45 us (1%)
    ppermute x19, waiting for transfers between devices, swap(): lax.ppermute(array, 'vocab', [(i, i ^ bits) for i in range(vocab_size)])  25.6 us
    ppermute x19, starting transfers between devices, swap(): lax.ppermute(array, 'vocab', [(i, i ^ bits) for i in range(vocab_size)])  24.7 us
    pallas_call x4, Pallas kernels, piece_scores(): pl.pallas_call(kernel, in_specs=[SMEM] + [VMEM] * len(arrays) + [VMEM, HB...  17 us
    unnamed x16, local copies, waits for them, and re-layouts  11.8 us
    pallas_call x1, Pallas kernels, prepare(): pl.pallas_call(kernel, in_specs=[VMEM] * 5, out_specs=[SMEM, VMEM, VMEM,...  10.2 us
    pallas_call x2, Pallas kernels, half_product(): pl.pallas_call(kernel, in_specs=[VMEM, HBM], out_specs=VMEM, out_shape=ja...  7.82 us
    ppermute x1, waiting for transfers between devices, body(): part = part + lax.ppermute(part, 'hid', [(0, 1), (1, 0)])  2.33 us
  transfers between devices with their start and end apart: 21, of which 12 were waited for; matrix products, arithmetic and copies ran while one was open for 1% of the time, Pallas kernels for 24%

profile of v2, /device:TPU:0, one launch (start us, length us, event | category | flops | bytes accessed | tf_op | source)
XLA Modules:
  0.0 105.9 jit_solution(4782865261693009995)
XLA Ops:
  0.0 0.9 copy-done.3
  1.0 4.0 %prior_half.3 = bf16[8,128,512]{2,1,0:T(8,128)(2,1)S(1)} custom-call(bf16[128,1024]{1,0:T(8,128)(2,1)S(1)} %copy-done.3, bf16[1024,8192]{1,0:T(8,128)(2,1)} %trans_ref.3), custom_call_target="tpu_custom_call" | custom-call | flops 1048576 | bytes 1048576 | tf_op jit(solution)/shard_map/prior_half/pallas_call | solution.py:59
  4.9 0.5 collective-permute-start
  5.4 3.9 %prior_half.2 = bf16[8,128,512]{2,1,0:T(8,128)(2,1)S(1)} custom-call(bf16[128,1024]{1,0:T(8,128)(2,1)S(1)} %copy-done.3, bf16[1024,8192]{1,0:T(8,128)(2,1)} %trans_ref.3), custom_call_target="tpu_custom_call" | custom-call | flops 1048576 | bytes 1048576 | tf_op jit(solution)/shard_map/prior_half/pallas_call | solution.py:59
  9.3 0.3 add_convert_fusion.1
  9.6 2.6 %collective-permute-start.1 = (bf16[2,128,512]{2,1,0:T(8,128)(2,1)S(1)}, bf16[2,128,512]{2,1,0:T(8,128)(2,1)S(1)}, u32[]{:S(2)}, u32[]{:S(2)}) collective-permute-start(bf16[2,128,512]{2,1,0:T(8,128)(2,1)S(1)} %get-tuple-element.35), channel_id=1, source_target_pairs={{0,4},{2,6},{4,0},{6,2},{8,12},{10,14},{12,8},{14,10},{16,20},{18,... | collective-permute-start | bytes 786440 | tf_op jit(solution)/shard_map/ppermute | solution.py:280
  12.2 0.1 collective-permute-start.4
  12.3 7.1 %collective-permute-done.1 = bf16[2,128,512]{2,1,0:T(8,128)(2,1)S(1)} collective-permute-done((bf16[2,128,512]{2,1,0:T(8,128)(2,1)S(1)}, bf16[2,128,512]{2,1,0:T(8,128)(2,1)S(1)}, u32[]{:S(2)}, u32[]{:S(2)}) %collective-permute-start.1) | collective-permute-done | bytes 262176 | tf_op jit(solution)/shard_map/ppermute | solution.py:280
  19.5 3.1 %collective-permute-start.2 = (bf16[128,512]{1,0:T(8,128)(2,1)S(1)}, bf16[128,512]{1,0:T(8,128)(2,1)S(1)}, u32[]{:S(2)}, u32[]{:S(2)}) collective-permute-start(bf16[128,512]{1,0:T(8,128)(2,1)S(1)} %get-tuple-element.68), channel_id=1, source_target_pairs={{0,16},{2,18},{4,20},{6,22},{8,24},{10,26},{12,28},{14,30},{16,0},... | collective-permute-start | bytes 393224 | tf_op jit(solution)/shard_map/ppermute | solution.py:280
  22.6 1.3 %collective-permute-start.3 = (bf16[128,512]{1,0:T(8,128)(2,1)S(1)}, bf16[128,512]{1,0:T(8,128)(2,1)S(1)}, u32[]{:S(2)}, u32[]{:S(2)}) collective-permute-start(bf16[128,512]{1,0:T(8,128)(2,1)S(1)} %get-tuple-element.67), channel_id=1, source_target_pairs={{0,24},{2,26},{4,28},{6,30},{8,16},{10,18},{12,20},{14,22},{16,8},... | collective-permute-start | bytes 393224 | tf_op jit(solution)/shard_map/ppermute | solution.py:280
  23.9 0.8 collective-permute-done.4
  24.8 0.1 convert_add_fusion
  24.9 1.9 %collective-permute-start.5 = (bf16[128,512]{1,0:T(8,128)(2,1)S(1)}, bf16[128,512]{1,0:T(8,128)(2,1)S(1)}, u32[]{:S(2)}, u32[]{:S(2)}) collective-permute-start(bf16[128,512]{1,0:T(8,128)(2,1)S(1)} %fusion.4), channel_id=1, source_target_pairs={{0,8},{2,10},{4,12},{6,14},{8,0},{10,2},{12,4},{14,6},{16,24},{18,... | collective-permute-start | bytes 393224 | tf_op jit(solution)/shard_map/ppermute | solution.py:280
  26.8 0.1 copy.10.next_ref
  27.0 2.2 %copy-done.2 = bf16[256,8192]{1,0:T(8,128)(2,1)S(1)} copy-done((bf16[256,8192]{1,0:T(8,128)(2,1)S(1)}, bf16[256,8192]{1,0:T(8,128)(2,1)}, u32[]{:S(2)}) %copy-start.2) | copy-done | bytes 4194328
  29.1 10.2 %prepare.1 = (s32[17]{0:T(128)S(1)}, bf16[512,128]{1,0:T(8,128)(2,1)S(1)}, bf16[128,1024]{1,0:T(8,128)(2,1)S(1)}, bf16[4096,8192]{1,0:T(8,128)(2,1)}) custom-call(s32[8,128]{1,0:T(8,128)S(1)} %bitcast.27, s32[1,128]{1,0:T(1,128)S(1)} %bitcast.28, s32[256,8]{1,0:T(8,128)S(1)} %copy.10.next_ref, s32[256,1024]{1,0:T(8,128)S(1)} %copy-done.4, ...), custom_call_target="tpu_custom_call" | custom-call | flops 1048576 | bytes 1048576 | tf_op jit(solution)/shard_map/prepare/pallas_call | solution.py:149
  39.4 0.3 collective-permute-start.11
  39.7 2.8 %collective-permute-start.6 = (bf16[128,512]{1,0:T(8,128)(2,1)S(1)}, bf16[128,512]{1,0:T(8,128)(2,1)S(1)}, u32[]{:S(2)}, u32[]{:S(2)}) collective-permute-start(bf16[128,512]{1,0:T(8,128)(2,1)S(1)} %fusion.3), channel_id=1, source_target_pairs={{0,16},{2,18},{4,20},{6,22},{8,24},{10,26},{12,28},{14,30},{16,0},... | collective-permute-start | bytes 393224 | tf_op jit(solution)/shard_map/ppermute | solution.py:280
  42.5 1.3 %collective-permute-start.7 = (bf16[128,512]{1,0:T(8,128)(2,1)S(1)}, bf16[128,512]{1,0:T(8,128)(2,1)S(1)}, u32[]{:S(2)}, u32[]{:S(2)}) collective-permute-start(bf16[128,512]{1,0:T(8,128)(2,1)S(1)} %fusion.3), channel_id=1, source_target_pairs={{0,24},{2,26},{4,28},{6,30},{8,16},{10,18},{12,20},{14,22},{16,8},... | collective-permute-start | bytes 393224 | tf_op jit(solution)/shard_map/ppermute | solution.py:280
  43.9 3.1 %collective-permute-done.11 = bf16[128,512]{1,0:T(8,128)(2,1)S(1)} collective-permute-done((bf16[128,512]{1,0:T(8,128)(2,1)S(1)}, bf16[128,512]{1,0:T(8,128)(2,1)S(1)}, u32[]{:S(2)}, u32[]{:S(2)}) %collective-permute-start.11) | collective-permute-done | bytes 131104 | tf_op jit(solution)/shard_map/ppermute | solution.py:280
  47.0 1.2 %collective-permute-start.12 = (bf16[2,128,512]{2,1,0:T(8,128)(2,1)S(1)}, bf16[2,128,512]{2,1,0:T(8,128)(2,1)S(1)}, u32[]{:S(2)}, u32[]{:S(2)}) collective-permute-start(bf16[2,128,512]{2,1,0:T(8,128)(2,1)S(1)} %pad_maximum_fusion.1.refs_0_), channel_id=1, source_target_pairs={{0,4},{2,6},{4,0},{6,2},{8,12},{10,14},{12,8},{14,10},{16,20},{18,... | collective-permute-start | bytes 786440 | tf_op jit(solution)/shard_map/ppermute | solution.py:280
  48.2 3.8 %collective-permute-done.7 = bf16[128,512]{1,0:T(8,128)(2,1)S(1)} collective-permute-done((bf16[128,512]{1,0:T(8,128)(2,1)S(1)}, bf16[128,512]{1,0:T(8,128)(2,1)S(1)}, u32[]{:S(2)}, u32[]{:S(2)}) %collective-permute-start.7) | collective-permute-done | bytes 131104 | tf_op jit(solution)/shard_map/ppermute | solution.py:280
  52.1 1.9 %collective-permute-start.8 = (bf16[2,128,512]{2,1,0:T(8,128)(2,1)S(1)}, bf16[2,128,512]{2,1,0:T(8,128)(2,1)S(1)}, u32[]{:S(2)}, u32[]{:S(2)}) collective-permute-start(bf16[2,128,512]{2,1,0:T(8,128)(2,1)S(1)} %pad_maximum_fusion.refs_0_), channel_id=1, source_target_pairs={{0,4},{2,6},{4,0},{6,2},{8,12},{10,14},{12,8},{14,10},{16,20},{18,... | collective-permute-start | bytes 786440 | tf_op jit(solution)/shard_map/ppermute | solution.py:280
  53.9 0.7 collective-permute-done.12.refs_0_
  54.6 0.5 collective-permute-start.10
  55.2 4.3 %collective-permute-done.8.refs_0_ = bf16[2,128,512]{2,1,0:T(8,128)(2,1)S(1)} collective-permute-done((bf16[2,128,512]{2,1,0:T(8,128)(2,1)S(1)}, bf16[2,128,512]{2,1,0:T(8,128)(2,1)S(1)}, u32[]{:S(2)}, u32[]{:S(2)}) %collective-permute-start.8) | collective-permute-done | bytes 262176 | tf_op jit(solution)/shard_map/ppermute | solution.py:280
  59.4 5.8 %copy-done = bf16[8192,1024]{1,0:T(8,128)(2,1)S(1)} copy-done((bf16[8192,1024]{1,0:T(8,128)(2,1)S(1)}, bf16[8192,1024]{1,0:T(8,128)(2,1)}, u32[]{:S(2)}) %copy-start) | copy-done | bytes 16777240
  65.2 4.1 %piece_scores.4.refs_6_ = f32[512,256]{1,0:T(8,128)S(1)} custom-call(s32[17]{0:T(128)S(1)} %get-tuple-element.53.head_ref, bf16[2,128,512]{2,1,0:T(8,128)(2,1)S(1)} %pad_maximum_fusion.1.refs_0_, bf16[2,128,512]{2,1,0:T(8,128)(2,1)S(1)} %collective-permute-done.14.refs_1_, bf16[512,128]{1,0:T(8,128)(2,1)S(1)} %get-tuple-element.57.refs_2_, ...), custom_call_target="tpu_custom_call" | custom-call | flops 1048576 | bytes 1048576 | tf_op jit(solution)/shard_map/piece_scores/pallas_call | solution.py:249
  69.3 2.9 %copy-done.1 = bf16[8192,1024]{1,0:T(8,128)(2,1)S(1)} copy-done((bf16[8192,1024]{1,0:T(8,128)(2,1)S(1)}, bf16[8192,1024]{1,0:T(8,128)(2,1)}, u32[]{:S(2)}) %copy-start.1) | copy-done | bytes 16777240
  72.3 3.9 %piece_scores.5.refs_6_ = f32[512,256]{1,0:T(8,128)S(1)} custom-call(s32[17]{0:T(128)S(1)} %get-tuple-element.53.head_ref, bf16[2,128,512]{2,1,0:T(8,128)(2,1)S(1)} %collective-permute-done.12.refs_0_, bf16[2,128,512]{2,1,0:T(8,128)(2,1)S(1)} %collective-permute-done.13.refs_1_, bf16[512,128]{1,0:T(8,128)(2,1)S(1)} %get-tuple-element.57.refs_2_, ...), custom_call_target="tpu_custom_call" | custom-call | flops 1048576 | bytes 1048576 | tf_op jit(solution)/shard_map/piece_scores/pallas_call | solution.py:249
  76.2 3.9 %piece_scores.6.refs_6_ = f32[512,256]{1,0:T(8,128)S(1)} custom-call(s32[17]{0:T(128)S(1)} %get-tuple-element.53.head_ref, bf16[2,128,512]{2,1,0:T(8,128)(2,1)S(1)} %pad_maximum_fusion.refs_0_, bf16[2,128,512]{2,1,0:T(8,128)(2,1)S(1)} %collective-permute-done.10.refs_1_, bf16[512,128]{1,0:T(8,128)(2,1)S(1)} %get-tuple-element.57.refs_2_, ...), custom_call_target="tpu_custom_call" | custom-call | flops 1048576 | bytes 1048576 | tf_op jit(solution)/shard_map/piece_scores/pallas_call | solution.py:249
  80.1 5.1 %piece_scores.7 = (f32[64,1024]{1,0:T(8,128)S(1)}, bf16[64,1024]{1,0:T(8,128)(2,1)S(1)}, f32[1,128]{1,0:T(1,128)S(1)}) custom-call(s32[17]{0:T(128)S(1)} %get-tuple-element.53.head_ref, bf16[2,128,512]{2,1,0:T(8,128)(2,1)S(1)} %collective-permute-done.8.refs_0_, bf16[2,128,512]{2,1,0:T(8,128)(2,1)S(1)} %collective-permute-done.9.refs_1_, ...), custom_call_target="tpu_custom_call" | custom-call | flops 1048576 | bytes 1048576 | tf_op jit(solution)/shard_map/piece_scores/pallas_call | solution.py:249
  85.2 1.3 %collective-permute-start.16 = (f32[1,128]{1,0:T(1,128)S(1)}, f32[1,128]{1,0:T(1,128)S(1)}, u32[]{:S(2)}, u32[]{:S(2)}) collective-permute-start(f32[1,128]{1,0:T(1,128)S(1)} %get-tuple-element.62), channel_id=1, source_target_pairs={{0,1},{1,0},{2,3},{3,2},{4,5},{5,4},{6,7},{7,6},{8,9},{9,8},{10,11... | collective-permute-start | bytes 1544 | tf_op jit(solution)/shard_map/ppermute | solution.py:341
  86.5 2.3 %collective-permute-done.16 = f32[1,128]{1,0:T(1,128)S(1)} collective-permute-done((f32[1,128]{1,0:T(1,128)S(1)}, f32[1,128]{1,0:T(1,128)S(1)}, u32[]{:S(2)}, u32[]{:S(2)}) %collective-permute-start.16) | collective-permute-done | bytes 544 | tf_op jit(solution)/shard_map/ppermute | solution.py:341
  88.8 4.9 %collective-permute-start.17 = (f32[1,128]{1,0:T(1,128)S(1)}, f32[1,128]{1,0:T(1,128)S(1)}, u32[]{:S(2)}, u32[]{:S(2)}) collective-permute-start(f32[1,128]{1,0:T(1,128)S(1)} %add.60), channel_id=1, source_target_pairs={{0,16},{2,18},{4,20},{6,22},{8,24},{10,26},{12,28},{14,30},{16,0},... | collective-permute-start | bytes 1544 | tf_op jit(solution)/shard_map/ppermute | solution.py:280
  93.7 1.5 %collective-permute-done.17 = f32[1,128]{1,0:T(1,128)S(1)} collective-permute-done((f32[1,128]{1,0:T(1,128)S(1)}, f32[1,128]{1,0:T(1,128)S(1)}, u32[]{:S(2)}, u32[]{:S(2)}) %collective-permute-start.17) | collective-permute-done | bytes 544 | tf_op jit(solution)/shard_map/ppermute | solution.py:280
  95.2 1.0 collective-permute-start.18
  96.2 2.5 %collective-permute-done.18 = f32[1,128]{1,0:T(1,128)S(1)} collective-permute-done((f32[1,128]{1,0:T(1,128)S(1)}, f32[1,128]{1,0:T(1,128)S(1)}, u32[]{:S(2)}, u32[]{:S(2)}) %collective-permute-start.18) | collective-permute-done | bytes 544 | tf_op jit(solution)/shard_map/ppermute | solution.py:280
  98.8 1.2 %collective-permute-start.19 = (f32[1,128]{1,0:T(1,128)S(1)}, f32[1,128]{1,0:T(1,128)S(1)}, u32[]{:S(2)}, u32[]{:S(2)}) collective-permute-start(f32[1,128]{1,0:T(1,128)S(1)} %add.62), channel_id=1, source_target_pairs={{0,4},{2,6},{4,0},{6,2},{8,12},{10,14},{12,8},{14,10},{16,20},{18,... | collective-permute-start | bytes 1544 | tf_op jit(solution)/shard_map/ppermute | solution.py:280
  100.0 1.5 %collective-permute-start.15 = (bf16[64,1024]{1,0:T(8,128)(2,1)S(1)}, bf16[64,1024]{1,0:T(8,128)(2,1)S(1)}, u32[]{:S(2)}, u32[]{:S(2)}) collective-permute-start(bf16[64,1024]{1,0:T(8,128)(2,1)S(1)} %get-tuple-element.61), channel_id=1, source_target_pairs={{0,1},{1,0},{2,3},{3,2},{4,5},{5,4},{6,7},{7,6},{8,9},{9,8},{10,11... | collective-permute-start | bytes 393224 | tf_op jit(solution)/shard_map/ppermute | solution.py:347
  101.5 0.8 collective-permute-done.19
  102.3 0.1 dynamic-slice_compare_fusion
  102.4 0.1 copy.9
  102.5 0.9 collective-permute-done.20
  103.4 0.1 log_bitcast_fusion
  103.5 1.5 %collective-permute-done.15 = bf16[64,1024]{1,0:T(8,128)(2,1)S(1)} collective-permute-done((bf16[64,1024]{1,0:T(8,128)(2,1)S(1)}, bf16[64,1024]{1,0:T(8,128)(2,1)S(1)}, u32[]{:S(2)}, u32[]{:S(2)}) %collective-permute-start.15) | collective-permute-done | bytes 131104 | tf_op jit(solution)/shard_map/ppermute | solution.py:347
  105.0 0.1 broadcast_in_dim.14
  105.1 0.8 subtract_select_fusion
  (36 shorter events, 0.3 us)
Async XLA Ops:
  0.0 0.9 copy-start.3
  1.0 25.8 %copy-start.7 = (s32[256,8]{0,1:T(8,128)S(1)}, s32[256,8]{0,1:T(8,128)}, u32[]{:S(2)}) copy-start(s32[256,8]{0,1:T(8,128)} %param.13) | copy-start | bytes 24580
  1.0 26.0 %copy-start.4 = (s32[256,1024]{1,0:T(8,128)S(1)}, s32[256,1024]{1,0:T(8,128)}, u32[]{:S(2)}) copy-start(s32[256,1024]{1,0:T(8,128)} %token_ref) | copy-start | bytes 3145732
  1.0 26.0 %copy-start.5 = (s32[128,8]{0,1:T(8,128)S(1)}, s32[128,8]{0,1:T(8,128)}, u32[]{:S(2)}) copy-start(s32[128,8]{0,1:T(8,128)} %param.15) | copy-start | bytes 12292
  1.0 26.0 %copy-start.6 = (s32[128]{0:T(128)S(1)}, s32[128]{0:T(128)}, u32[]{:S(2)}) copy-start(s32[128]{0:T(128)} %param.12) | copy-start | bytes 1540
  4.9 4.4 %collective-permute-start = (bf16[8,128,512]{2,1,0:T(8,128)(2,1)S(1)}, bf16[8,128,512]{2,1,0:T(8,128)(2,1)S(1)}, u32[]{:S(2)}, u32[]{:S(2)}) collective-permute-start(bf16[8,128,512]{2,1,0:T(8,128)(2,1)S(1)} %prior_half.3), channel_id=1, source_target_pairs={{0,2},{2,0},{4,6},{6,4},{8,10},{10,8},{12,14},{14,12},{16,18},{18,... | collective-permute-start | bytes 3145736 | tf_op jit(solution)/shard_map/ppermute | solution.py:280
  9.6 9.7 %collective-permute-start.1 = (bf16[2,128,512]{2,1,0:T(8,128)(2,1)S(1)}, bf16[2,128,512]{2,1,0:T(8,128)(2,1)S(1)}, u32[]{:S(2)}, u32[]{:S(2)}) collective-permute-start(bf16[2,128,512]{2,1,0:T(8,128)(2,1)S(1)} %get-tuple-element.35), channel_id=1, source_target_pairs={{0,4},{2,6},{4,0},{6,2},{8,12},{10,14},{12,8},{14,10},{16,20},{18,... | collective-permute-start | bytes 786440 | tf_op jit(solution)/shard_map/ppermute | solution.py:280
  12.2 12.6 %collective-permute-start.4 = (bf16[2,128,512]{2,1,0:T(8,128)(2,1)S(1)}, bf16[2,128,512]{2,1,0:T(8,128)(2,1)S(1)}, u32[]{:S(2)}, u32[]{:S(2)}) collective-permute-start(bf16[2,128,512]{2,1,0:T(8,128)(2,1)S(1)} %get-tuple-element.43), channel_id=1, source_target_pairs={{0,4},{2,6},{4,0},{6,2},{8,12},{10,14},{12,8},{14,10},{16,20},{18,... | collective-permute-start | bytes 786440 | tf_op jit(solution)/shard_map/ppermute | solution.py:280
  19.5 19.9 %collective-permute-start.2 = (bf16[128,512]{1,0:T(8,128)(2,1)S(1)}, bf16[128,512]{1,0:T(8,128)(2,1)S(1)}, u32[]{:S(2)}, u32[]{:S(2)}) collective-permute-start(bf16[128,512]{1,0:T(8,128)(2,1)S(1)} %get-tuple-element.68), channel_id=1, source_target_pairs={{0,16},{2,18},{4,20},{6,22},{8,24},{10,26},{12,28},{14,30},{16,0},... | collective-permute-start | bytes 393224 | tf_op jit(solution)/shard_map/ppermute | solution.py:280
  22.6 16.8 %collective-permute-start.3 = (bf16[128,512]{1,0:T(8,128)(2,1)S(1)}, bf16[128,512]{1,0:T(8,128)(2,1)S(1)}, u32[]{:S(2)}, u32[]{:S(2)}) collective-permute-start(bf16[128,512]{1,0:T(8,128)(2,1)S(1)} %get-tuple-element.67), channel_id=1, source_target_pairs={{0,24},{2,26},{4,28},{6,30},{8,16},{10,18},{12,20},{14,22},{16,8},... | collective-permute-start | bytes 393224 | tf_op jit(solution)/shard_map/ppermute | solution.py:280
  24.9 14.5 %collective-permute-start.5 = (bf16[128,512]{1,0:T(8,128)(2,1)S(1)}, bf16[128,512]{1,0:T(8,128)(2,1)S(1)}, u32[]{:S(2)}, u32[]{:S(2)}) collective-permute-start(bf16[128,512]{1,0:T(8,128)(2,1)S(1)} %fusion.4), channel_id=1, source_target_pairs={{0,8},{2,10},{4,12},{6,14},{8,0},{10,2},{12,4},{14,6},{16,24},{18,... | collective-permute-start | bytes 393224 | tf_op jit(solution)/shard_map/ppermute | solution.py:280
  26.9 2.2 %copy-start.2 = (bf16[256,8192]{1,0:T(8,128)(2,1)S(1)}, bf16[256,8192]{1,0:T(8,128)(2,1)}, u32[]{:S(2)}) copy-start(bf16[256,8192]{1,0:T(8,128)(2,1)} %adv_ref) | copy-start | bytes 12582916
  39.4 7.5 %collective-permute-start.11 = (bf16[128,512]{1,0:T(8,128)(2,1)S(1)}, bf16[128,512]{1,0:T(8,128)(2,1)S(1)}, u32[]{:S(2)}, u32[]{:S(2)}) collective-permute-start(bf16[128,512]{1,0:T(8,128)(2,1)S(1)} %fusion.3), channel_id=1, source_target_pairs={{0,8},{2,10},{4,12},{6,14},{8,0},{10,2},{12,4},{14,6},{16,24},{18,... | collective-permute-start | bytes 393224 | tf_op jit(solution)/shard_map/ppermute | solution.py:280
  39.7 8.5 %collective-permute-start.6 = (bf16[128,512]{1,0:T(8,128)(2,1)S(1)}, bf16[128,512]{1,0:T(8,128)(2,1)S(1)}, u32[]{:S(2)}, u32[]{:S(2)}) collective-permute-start(bf16[128,512]{1,0:T(8,128)(2,1)S(1)} %fusion.3), channel_id=1, source_target_pairs={{0,16},{2,18},{4,20},{6,22},{8,24},{10,26},{12,28},{14,30},{16,0},... | collective-permute-start | bytes 393224 | tf_op jit(solution)/shard_map/ppermute | solution.py:280
  42.5 9.5 %collective-permute-start.7 = (bf16[128,512]{1,0:T(8,128)(2,1)S(1)}, bf16[128,512]{1,0:T(8,128)(2,1)S(1)}, u32[]{:S(2)}, u32[]{:S(2)}) collective-permute-start(bf16[128,512]{1,0:T(8,128)(2,1)S(1)} %fusion.3), channel_id=1, source_target_pairs={{0,24},{2,26},{4,28},{6,30},{8,16},{10,18},{12,20},{14,22},{16,8},... | collective-permute-start | bytes 393224 | tf_op jit(solution)/shard_map/ppermute | solution.py:280
  47.0 7.6 %collective-permute-start.12 = (bf16[2,128,512]{2,1,0:T(8,128)(2,1)S(1)}, bf16[2,128,512]{2,1,0:T(8,128)(2,1)S(1)}, u32[]{:S(2)}, u32[]{:S(2)}) collective-permute-start(bf16[2,128,512]{2,1,0:T(8,128)(2,1)S(1)} %pad_maximum_fusion.1.refs_0_), channel_id=1, source_target_pairs={{0,4},{2,6},{4,0},{6,2},{8,12},{10,14},{12,8},{14,10},{16,20},{18,... | collective-permute-start | bytes 786440 | tf_op jit(solution)/shard_map/ppermute | solution.py:280
  52.1 7.4 %collective-permute-start.8 = (bf16[2,128,512]{2,1,0:T(8,128)(2,1)S(1)}, bf16[2,128,512]{2,1,0:T(8,128)(2,1)S(1)}, u32[]{:S(2)}, u32[]{:S(2)}) collective-permute-start(bf16[2,128,512]{2,1,0:T(8,128)(2,1)S(1)} %pad_maximum_fusion.refs_0_), channel_id=1, source_target_pairs={{0,4},{2,6},{4,0},{6,2},{8,12},{10,14},{12,8},{14,10},{16,20},{18,... | collective-permute-start | bytes 786440 | tf_op jit(solution)/shard_map/ppermute | solution.py:280
  53.9 5.5 %collective-permute-start.14 = (bf16[2,128,512]{2,1,0:T(8,128)(2,1)S(1)}, bf16[2,128,512]{2,1,0:T(8,128)(2,1)S(1)}, u32[]{:S(2)}, u32[]{:S(2)}) collective-permute-start(bf16[2,128,512]{2,1,0:T(8,128)(2,1)S(1)} %pad_maximum_fusion.1.refs_0_), channel_id=1, source_target_pairs={{0,2},{2,0},{4,6},{6,4},{8,10},{10,8},{12,14},{14,12},{16,18},{18,... | collective-permute-start | bytes 786440 | tf_op jit(solution)/shard_map/ppermute | solution.py:280
  54.6 14.7 %collective-permute-start.13 = (bf16[2,128,512]{2,1,0:T(8,128)(2,1)S(1)}, bf16[2,128,512]{2,1,0:T(8,128)(2,1)S(1)}, u32[]{:S(2)}, u32[]{:S(2)}) collective-permute-start(bf16[2,128,512]{2,1,0:T(8,128)(2,1)S(1)} %collective-permute-done.12.refs_0_), channel_id=1, source_target_pairs={{0,2},{2,0},{4,6},{6,4},{8,10},{10,8},{12,14},{14,12},{16,18},{18,... | collective-permute-start | bytes 786440 | tf_op jit(solution)/shard_map/ppermute | solution.py:280
  54.6 21.5 %collective-permute-start.10 = (bf16[2,128,512]{2,1,0:T(8,128)(2,1)S(1)}, bf16[2,128,512]{2,1,0:T(8,128)(2,1)S(1)}, u32[]{:S(2)}, u32[]{:S(2)}) collective-permute-start(bf16[2,128,512]{2,1,0:T(8,128)(2,1)S(1)} %pad_maximum_fusion.refs_0_), channel_id=1, source_target_pairs={{0,2},{2,0},{4,6},{6,4},{8,10},{10,8},{12,14},{14,12},{16,18},{18,... | collective-permute-start | bytes 786440 | tf_op jit(solution)/shard_map/ppermute | solution.py:280
  59.4 20.6 %collective-permute-start.9 = (bf16[2,128,512]{2,1,0:T(8,128)(2,1)S(1)}, bf16[2,128,512]{2,1,0:T(8,128)(2,1)S(1)}, u32[]{:S(2)}, u32[]{:S(2)}) collective-permute-start(bf16[2,128,512]{2,1,0:T(8,128)(2,1)S(1)} %collective-permute-done.8.refs_0_), channel_id=1, source_target_pairs={{0,2},{2,0},{4,6},{6,4},{8,10},{10,8},{12,14},{14,12},{16,18},{18,... | collective-permute-start | bytes 786440 | tf_op jit(solution)/shard_map/ppermute | solution.py:280
  59.4 5.8 %copy-start = (bf16[8192,1024]{1,0:T(8,128)(2,1)S(1)}, bf16[8192,1024]{1,0:T(8,128)(2,1)}, u32[]{:S(2)}) copy-start(bf16[8192,1024]{1,0:T(8,128)(2,1)} %refs_4_.7) | copy-start | bytes 50331652
  65.2 7.1 %copy-start.1 = (bf16[8192,1024]{1,0:T(8,128)(2,1)S(1)}, bf16[8192,1024]{1,0:T(8,128)(2,1)}, u32[]{:S(2)}) copy-start(bf16[8192,1024]{1,0:T(8,128)(2,1)} %refs_4_.7) | copy-start | bytes 50331652
  85.2 3.6 %collective-permute-start.16 = (f32[1,128]{1,0:T(1,128)S(1)}, f32[1,128]{1,0:T(1,128)S(1)}, u32[]{:S(2)}, u32[]{:S(2)}) collective-permute-start(f32[1,128]{1,0:T(1,128)S(1)} %get-tuple-element.62), channel_id=1, source_target_pairs={{0,1},{1,0},{2,3},{3,2},{4,5},{5,4},{6,7},{7,6},{8,9},{9,8},{10,11... | collective-permute-start | bytes 1544 | tf_op jit(solution)/shard_map/ppermute | solution.py:341
  88.8 6.4 %collective-permute-start.17 = (f32[1,128]{1,0:T(1,128)S(1)}, f32[1,128]{1,0:T(1,128)S(1)}, u32[]{:S(2)}, u32[]{:S(2)}) collective-permute-start(f32[1,128]{1,0:T(1,128)S(1)} %add.60), channel_id=1, source_target_pairs={{0,16},{2,18},{4,20},{6,22},{8,24},{10,26},{12,28},{14,30},{16,0},... | collective-permute-start | bytes 1544 | tf_op jit(solution)/shard_map/ppermute | solution.py:280
  95.2 3.5 %collective-permute-start.18 = (f32[1,128]{1,0:T(1,128)S(1)}, f32[1,128]{1,0:T(1,128)S(1)}, u32[]{:S(2)}, u32[]{:S(2)}) collective-permute-start(f32[1,128]{1,0:T(1,128)S(1)} %add.61), channel_id=1, source_target_pairs={{0,8},{2,10},{4,12},{6,14},{8,0},{10,2},{12,4},{14,6},{16,24},{18,... | collective-permute-start | bytes 1544 | tf_op jit(solution)/shard_map/ppermute | solution.py:280
  98.8 3.5 %collective-permute-start.19 = (f32[1,128]{1,0:T(1,128)S(1)}, f32[1,128]{1,0:T(1,128)S(1)}, u32[]{:S(2)}, u32[]{:S(2)}) collective-permute-start(f32[1,128]{1,0:T(1,128)S(1)} %add.62), channel_id=1, source_target_pairs={{0,4},{2,6},{4,0},{6,2},{8,12},{10,14},{12,8},{14,10},{16,20},{18,... | collective-permute-start | bytes 1544 | tf_op jit(solution)/shard_map/ppermute | solution.py:280
  100.0 5.0 %collective-permute-start.15 = (bf16[64,1024]{1,0:T(8,128)(2,1)S(1)}, bf16[64,1024]{1,0:T(8,128)(2,1)S(1)}, u32[]{:S(2)}, u32[]{:S(2)}) collective-permute-start(bf16[64,1024]{1,0:T(8,128)(2,1)S(1)} %get-tuple-element.61), channel_id=1, source_target_pairs={{0,1},{1,0},{2,3},{3,2},{4,5},{5,4},{6,7},{7,6},{8,9},{9,8},{10,11... | collective-permute-start | bytes 393224 | tf_op jit(solution)/shard_map/ppermute | solution.py:347
  102.3 1.1 %collective-permute-start.20 = (f32[1,128]{1,0:T(1,128)S(1)}, f32[1,128]{1,0:T(1,128)S(1)}, u32[]{:S(2)}, u32[]{:S(2)}) collective-permute-start(f32[1,128]{1,0:T(1,128)S(1)} %add.63), channel_id=1, source_target_pairs={{0,2},{2,0},{4,6},{6,4},{8,10},{10,8},{12,14},{14,12},{16,18},{18,... | collective-permute-start | bytes 1544 | tf_op jit(solution)/shard_map/ppermute | solution.py:280

commit v3 on v2

v3 whole, which is shorter than its diff:
```python
import functools
import jax
import jax.numpy as jnp
from jax import lax
from jax.experimental import pallas as pl
from jax.experimental.pallas import tpu as pltpu
from jax.sharding import PartitionSpec as P

BLK = 128
GROUP = 32
UNIT = 256
BATCH = 4
CHEAP = 1 << 20
BF16 = jnp.bfloat16
F32 = jnp.float32
FAR_OTHER, FAR_SAME, NEAR_OTHER, NEAR_SAME = (5, 7), (4, 6), (1, 3), (0, 2)


def params(mib):
    return pltpu.CompilerParams(vmem_limit_bytes=mib << 20)


def cheap():
    return pl.CostEstimate(flops=CHEAP, bytes_accessed=CHEAP, transcendentals=0)


def piece_place(chips, other, bits):
    me = lax.axis_index("vocab")
    core, chip = lax.rem(me, 2), lax.div(me, 2)
    return (1 - core if other else core) * chips + (chip ^ bits)


def transposed_dot(a, b):
    return lax.dot_general(a, b, (((0,), (0,)), ((), ())), preferred_element_type=F32)


def in_hbm(array):
    return pltpu.with_memory_space_constraint(array, pltpu.HBM)


SMEM = pl.BlockSpec(memory_space=pltpu.SMEM)
VMEM = pl.BlockSpec(memory_space=pltpu.VMEM)
HBM = pl.BlockSpec(memory_space=pltpu.HBM)


def half_product(posterior, transition, other, order, chips, width):
    rows, depth = posterior.shape
    pieces = len(order)

    def kernel(post_ref, trans_ref, out_ref, held, arrived):
        def copy(n):
            first = piece_place(chips, other, order[n])
            columns = pl.ds(pl.multiple_of(first * width, width), width)
            return pltpu.make_async_copy(trans_ref.at[:, columns], held.at[n], arrived.at[n])

        for n in range(pieces):
            copy(n).start()
        for n in range(pieces):
            copy(n).wait()
            out_ref[n] = jnp.dot(post_ref[...], held[n], preferred_element_type=F32).astype(BF16)

    return pl.pallas_call(
        kernel,
        in_specs=[VMEM, HBM],
        out_specs=VMEM,
        out_shape=jax.ShapeDtypeStruct((pieces, rows, width), BF16),
        scratch_shapes=[
            pltpu.VMEM((pieces, depth, width), BF16),
            pltpu.SemaphoreType.DMA((pieces,)),
        ],
        compiler_params=params(24),
        cost_estimate=cheap(),
        name="prior_half",
    )(posterior, in_hbm(transition))


def take_seats(allowed, state, edge_next, token_edge, tile):
    blocks, rows = allowed.shape
    states, columns = token_edge.shape
    slots = edge_next.shape[1]
    tiles = columns // tile
    each = tile // BLK
    seats = tiles * rows

    def kernel(allow_ref, state_ref, next_ref, token_hbm, head_ref, select_ref, after_ref, edge_ref, token_ref, came):
        inward = pltpu.make_async_copy(token_hbm, token_ref, came)
        inward.start()
        who = (lax.broadcasted_iota(jnp.int32, (states, rows), 0) == state_ref[...]).astype(F32).astype(BF16)
        allow = allow_ref[...].astype(F32)
        earlier = lax.broadcasted_iota(jnp.int32, (rows, rows), 0) < lax.broadcasted_iota(jnp.int32, (rows, rows), 1)
        earlier = earlier.astype(F32).astype(BF16)
        number = lax.broadcasted_iota(jnp.int32, (seats, rows), 0)
        taken = jnp.zeros((seats, rows), F32)
        used = jnp.int32(0)
        for t in range(tiles):
            need = allow[t * each : t * each + 1]
            for b in range(1, each):
                need = jnp.maximum(need, allow[t * each + b : t * each + b + 1])
            rank = jnp.dot(jnp.broadcast_to(need, (8, rows)).astype(BF16), earlier, preferred_element_type=F32)[0:1]
            units = (jnp.sum(need).astype(jnp.int32) + GROUP - 1) // GROUP
            seat = jnp.where(need > 0, rank.astype(jnp.int32) + used * GROUP, -1)
            taken += (number == seat).astype(F32)

            @pl.loop(0, units)
            def _(u):
                head_ref[1 + used + u] = t

            used = used + units
        head_ref[0] = used
        taken = taken.astype(BF16)
        select_ref[...] = taken
        following = transposed_dot(who, next_ref[...].astype(F32).astype(BF16))
        after_ref[...] = jnp.dot(taken, following.astype(BF16), preferred_element_type=F32).astype(jnp.int32)
        allow = allow.astype(BF16)
        block = lax.broadcasted_iota(jnp.int32, (blocks, columns), 1) // BLK
        spread = (block == lax.broadcasted_iota(jnp.int32, (blocks, columns), 0)).astype(F32).astype(BF16)
        mask = transposed_dot(allow, spread)
        inward.wait()
        token = token_ref[...].astype(F32).astype(BF16)
        edge_ref[...] = jnp.where(mask > 0, transposed_dot(who, token), float(slots)).astype(BF16)

    return pl.pallas_call(
        kernel,
        in_specs=[VMEM] * 3 + [HBM],
        out_specs=[SMEM, VMEM, VMEM, VMEM],
        scratch_shapes=[pltpu.VMEM((states, columns), jnp.int32), pltpu.SemaphoreType.DMA],
        out_shape=[
            jax.ShapeDtypeStruct((1 + seats // GROUP,), jnp.int32),
            jax.ShapeDtypeStruct((seats, rows), BF16),
            jax.ShapeDtypeStruct((seats, slots), jnp.int32),
            jax.ShapeDtypeStruct((rows, columns), BF16),
        ],
        compiler_params=params(16),
        cost_estimate=cheap(),
        name="take_seats",
    )(allowed, state, edge_next, token_edge)


def successor_rows(head, after, advance):
    seats, slots = after.shape
    states, hidden = advance.shape
    width = min(1024, hidden)
    steps = hidden // width
    full = BATCH * UNIT

    def kernel(head_ref, after_ref, adv_hbm, first_ref, rest_ref, adv_ref, hot, held, left, came):
        def inward(n):
            span = pl.ds(n * width, width)
            return pltpu.make_async_copy(adv_hbm.at[:, span], adv_ref.at[:, span], came.at[n])

        for n in range(steps):
            inward(n).start()
        names = lax.broadcasted_iota(jnp.int32, (GROUP, states), 1)

        def mark(c):
            for u in range(BATCH):
                succ = after_ref[pl.ds(pl.multiple_of((c * BATCH + u) * GROUP, GROUP), GROUP), :]
                for k in range(slots):
                    hot[u * UNIT + k * GROUP : u * UNIT + (k + 1) * GROUP, :] = (
                        (names == succ[:, k : k + 1]).astype(F32).astype(BF16)
                    )

        def rows(n):
            span = slice(n * width, (n + 1) * width)
            return jnp.dot(hot[...], adv_ref[:, span], preferred_element_type=F32).astype(BF16)

        def copy(c, n):
            span = pl.ds(pl.multiple_of(c * full, full), full)
            return pltpu.make_async_copy(held, rest_ref.at[span, pl.ds(n * width, width)], left)

        mark(0)
        for n in range(steps):
            inward(n).wait()
            first_ref[:, n * width : (n + 1) * width] = rows(n)

        @pl.loop(1, (head_ref[0] + BATCH - 1) // BATCH)
        def _(c):
            mark(c)
            for n in range(steps):
                held[...] = rows(n)
                copy(c, n).start()
                copy(c, n).wait()

    return pl.pallas_call(
        kernel,
        in_specs=[SMEM, VMEM, HBM],
        out_specs=[VMEM, HBM],
        scratch_shapes=[
            pltpu.VMEM((states, hidden), BF16),
            pltpu.VMEM((full, states), BF16),
            pltpu.VMEM((full, width), BF16),
            pltpu.SemaphoreType.DMA,
            pltpu.SemaphoreType.DMA((steps,)),
        ],
        out_shape=[pltpu.VMEM((full, hidden), BF16), jax.ShapeDtypeStruct((seats * slots, hidden), BF16)],
        compiler_params=params(16),
        cost_estimate=cheap(),
        name="successor_rows",
    )(head, after, advance)


def stage(emission):
    deep = emission.shape[0] // 8

    def kernel(hbm, out_ref, came):
        copies = []
        for n in range(8):
            span = pl.ds(n * deep, deep)
            copies.append(pltpu.make_async_copy(hbm.at[span, :], out_ref.at[span, :], came.at[n]))
        for copy in copies:
            copy.start()
        for copy in copies:
            copy.wait()

    return pl.pallas_call(
        kernel,
        in_specs=[HBM],
        out_specs=VMEM,
        out_shape=pltpu.VMEM(emission.shape, BF16),
        scratch_shapes=[pltpu.SemaphoreType.DMA((8,))],
        compiler_params=params(16),
        cost_estimate=cheap(),
        name="stage",
    )(emission)


def piece_scores(arrays, places, head, select, look, emission, edges, before, slots, tile, last, local):
    each, rows, width = arrays[0].shape
    count = len(arrays) * each
    columns = emission.shape[1]
    seats = select.shape[0]
    started = before is not None

    def kernel(head_ref, *refs):
        piece_refs = refs[: len(arrays)]
        select_ref, near_ref, look_ref, emit_ref, edge_ref = refs[len(arrays) : len(arrays) + 5]
        before_ref = refs[len(arrays) + 5] if started else None
        looks, prior, total, arrived = refs[-4:]
        outs = refs[len(arrays) + 5 + started : -4]
        units = head_ref[0]
        deep = [pl.ds(pl.multiple_of(place * width, width), width) for place in places()]

        def look_copy(i, c, u):
            here = pl.ds(pl.multiple_of((c * BATCH + u) * UNIT, UNIT), UNIT)
            return pltpu.make_async_copy(look_ref.at[here, deep[i]], looks.at[i, u], arrived.at[i, u])

        if last:
            total[...] = jnp.zeros_like(total)

        def spread_prior(c):
            span = pl.ds(pl.multiple_of(c * BATCH * GROUP, BATCH * GROUP), BATCH * GROUP)
            for i in range(count):
                prior[i] = jnp.dot(
                    select_ref[span, :], piece_refs[i // each][i % each], preferred_element_type=F32
                ).astype(BF16)

        def one_unit(c, u, rows_of):
            at = pl.multiple_of(head_ref[1 + c * BATCH + u] * tile, tile)
            span = pl.ds(pl.multiple_of((c * BATCH + u) * GROUP, GROUP), GROUP)
            seat = pl.ds(pl.multiple_of(u * GROUP, GROUP), GROUP)
            values = None
            for i in range(count):
                rowed = rows_of(i, u).reshape(slots, GROUP, width)
                weighted = (rowed * prior[i, seat, :][None]).reshape(UNIT, width)
                part = jnp.dot(weighted, emit_ref[deep[i], pl.ds(at, tile)], preferred_element_type=F32)
                values = part if values is None else values + part
            own = select_ref[span, :]
            edge = jnp.dot(own, edge_ref[:, pl.ds(at, tile)], preferred_element_type=F32)
            chosen = before_ref[span, :] if started else jnp.zeros((GROUP, tile), F32)
            for k in range(slots):
                chosen += jnp.where(edge == k, values[k * GROUP : (k + 1) * GROUP], 0.0)
            if not last:
                outs[0][span, :] = chosen
                return
            spread = jnp.zeros((rows, tile), F32)
            for _ in range(3):
                high = chosen.astype(BF16)
                chosen = chosen - high.astype(F32)
                spread += transposed_dot(own, high)
            total[:, pl.ds(at, tile)] += spread

        spread_prior(0)

        @pl.loop(0, jnp.minimum(units, BATCH))
        def _(u):
            one_unit(0, u, lambda i, u: near_ref[pl.ds(pl.multiple_of(u * UNIT, UNIT), UNIT), deep[i]])

        @pl.loop(1, (units + BATCH - 1) // BATCH)
        def _(c):
            here = jnp.minimum(units - c * BATCH, BATCH)

            @pl.loop(0, here)
            def _(u):
                for i in range(count):
                    look_copy(i, c, u).start()

            spread_prior(c)

            @pl.loop(0, here)
            def _(u):
                for i in range(count):
                    look_copy(i, c, u).wait()
                one_unit(c, u, lambda i, u: looks[i, u])

        if last:
            first = lax.axis_index("hid") * local if local < rows else 0
            outs[0][...] = total[pl.ds(pl.multiple_of(first, local), local), :]
            theirs = local - first if local < rows else 0
            outs[1][...] = total[pl.ds(pl.multiple_of(theirs, local), local), :].astype(BF16)
            sums = jnp.sum(total[...], axis=1, keepdims=True)
            outs[2][...] = jnp.broadcast_to(sums, (rows, 128)).T[0:1, :]

    if last:
        shapes = [((local, columns), F32), ((local, columns), BF16), ((1, rows), F32)]
    else:
        shapes = [((seats, tile), F32)]
    return pl.pallas_call(
        kernel,
        in_specs=[SMEM] + [VMEM] * len(arrays) + [VMEM, VMEM, HBM, VMEM, VMEM] + [VMEM] * started,
        out_specs=[VMEM] * len(shapes),
        scratch_shapes=[
            pltpu.VMEM((count, BATCH, UNIT, width), BF16),
            pltpu.VMEM((count, BATCH * GROUP, width), BF16),
            pltpu.VMEM((rows, columns), F32),
            pltpu.SemaphoreType.DMA((count, BATCH)),
        ],
        out_shape=[jax.ShapeDtypeStruct(*shape) for shape in shapes],
        compiler_params=params(16),
        cost_estimate=cheap(),
        name="piece_scores",
    )(head, *arrays, select, *look, emission, edges, *([before] if started else []))


def body(sizes, posterior, transition, emission, advance, dfa_state, edge_next, token_edge, allowed):
    vocab_size, hid_size = sizes
    rows = posterior.shape[0]
    hidden = transition.shape[1]
    slots = edge_next.shape[1]
    chips = vocab_size // 2
    width = hidden // vocab_size
    direct = chips == 8 and width % 128 == 0
    local = rows // hid_size
    first = lax.axis_index("hid") * local
    blocks = allowed.shape[1]
    tile = min(2, blocks) * BLK

    def swap(array, bits):
        return lax.ppermute(array, "vocab", [(i, i ^ bits) for i in range(vocab_size)])

    def seated(allowed, dfa_state, edge_next, token_edge):
        return take_seats(allowed.T, dfa_state[None, :], edge_next, in_hbm(token_edge), tile)

    small = (allowed, dfa_state, edge_next, token_edge)
    if direct:
        order = FAR_OTHER + FAR_SAME + NEAR_OTHER + NEAR_SAME
        away = half_product(posterior, transition, True, order, chips, width)
        came = swap(away, 1)
        kept = half_product(posterior, transition, False, order, chips, width)
        parts = [(kept[n : n + 2].astype(F32) + came[n : n + 2].astype(F32)).astype(BF16) for n in (0, 2, 4, 6)]
        far = swap(parts[0], 2)
        parts, small = lax.optimization_barrier((parts, small))
        near = swap(parts[2], 2)
        head, select, after, edges = seated(*small)
        far, head, select, after, edges = lax.optimization_barrier((far, head, select, after, edges))
        far = parts[1].astype(F32) + far.astype(F32)
        sent = [swap(far[0].astype(BF16), 8), swap(far[1].astype(BF16), 12)]
        near = parts[3].astype(F32) + near.astype(F32)
        sent.append(swap(near[1].astype(BF16), 4))
        look = successor_rows(head, after, in_hbm(advance))
        sent, look = lax.optimization_barrier((sent, look))
        own = near[0] + sent[0].astype(F32) + sent[1].astype(F32) + sent[2].astype(F32)
        own = own.astype(BF16)

        own, emission = lax.optimization_barrier((own, emission))
        far = [swap(own, 8), swap(own, 12)]
        far, emission = lax.optimization_barrier((far, stage(in_hbm(emission))))
        far = jnp.stack(far)
        near = jnp.stack([own, swap(own, 2)])
        batches = [((near, far), (0, 1, 4, 6)), ((swap(near, 4), swap(far, 2)), (2, 3, 5, 7))]

        def one_batch(arrays, bits, before, last):
            def places():
                groups = (bits[:2], bits[2:])
                return [piece_place(chips, other, b) for group in groups for other in (False, True) for b in group]

            first, second = arrays
            if before is not None:
                first, second, before = lax.optimization_barrier((first, second, before))
            arrays = [first, swap(first, 1), second, swap(second, 1)]
            return piece_scores(
                arrays, places, head, select, look, emission, edges, before, slots, tile, last, local
            )

    else:
        own = lax.psum_scatter(
            jnp.dot(posterior, transition, preferred_element_type=F32), "vocab", scatter_dimension=0, tiled=True
        ).astype(BF16)
        prior = lax.all_gather(own, "vocab", axis=0, tiled=True)
        head, select, after, edges = seated(*small)
        look = successor_rows(head, after, in_hbm(advance))
        wide = min(512, hidden)
        batches = [(prior[None, :, wide * j : wide * (j + 1)], j) for j in range(hidden // wide)]

        def one_batch(array, j, before, last):
            return piece_scores(
                [array], lambda: [j], head, select, look, emission, edges, before, slots, tile, last, rows
            )

    chosen = None
    for n, (array, where) in enumerate(batches):
        got = one_batch(array, where, chosen, n == len(batches) - 1)
        chosen = got[0]
    mine, theirs, part = got

    if hid_size == 2:
        bits = vocab_size // 2
        while bits:
            part = part + swap(part, bits)
            if bits == vocab_size // 2:
                part, theirs = lax.optimization_barrier((part, theirs))
                theirs = lax.ppermute(theirs, "hid", [(0, 1), (1, 0)])
            bits //= 2
        part, theirs = lax.optimization_barrier((part, theirs))
        part = part + lax.ppermute(part, "hid", [(0, 1), (1, 0)])
        totals = lax.dynamic_slice_in_dim(part[0], first, local, 0)
        mine = mine + theirs.astype(F32)
    else:
        mine = lax.psum_scatter(theirs, "hid", scatter_dimension=0, tiled=True).astype(F32)
        totals = lax.psum(jnp.sum(mine, axis=1), "vocab")
    mask = jnp.repeat(lax.dynamic_slice_in_dim(allowed, first, local, 0), BLK, axis=1) > 0
    safe = jnp.where(mask, mine, jnp.float32(1.0))
    return jnp.where(mask, jnp.log(safe) - jnp.log(totals)[:, None], jnp.float32(0.0))


def solution(mesh):
    in_specs = (
        P(None, "vocab"),
        P("vocab", "hid"),
        P("hid", "vocab"),
        P(None, "hid"),
        P(),
        P(),
        P(None, "vocab"),
        P(None, "vocab"),
    )
    sizes = (mesh.shape["vocab"], mesh.shape["hid"])
    return jax.shard_map(
        functools.partial(body, sizes), mesh=mesh, in_specs=in_specs, out_specs=P("hid", "vocab"), check_vma=False
    )
```

time: 106 us -> 85.1 us (0.80)
  local copies, waits for them, and re-layouts: 12.3 us -> 1.44 us
  waiting for transfers between devices: 29.4 us -> 22.3 us
  Pallas kernels: 35 us -> 32.9 us
    unnamed x16 -> x8, local copies, waits for them, and re-layouts: 11.8 us -> 0.96 us
    ppermute x19, waiting for transfers between devices: 25.6 us -> 19.4 us  [swap(): lax.ppermute(array, 'vocab', [(i, i ^ bits) for i in range(vocab_size)])]
    pallas_call x5, Pallas kernels: 27.2 us -> 25.2 us  [the longest x2 9.89 us: piece_scores(): pl.pallas_call(kernel, in_specs=[SMEM] + [VMEM] * len(arrays) + [VMEM, VM...]
    ppermute x1, waiting for transfers between devices: 1.47 us -> 0.01 us  [body(): theirs = lax.ppermute(theirs, 'hid', [(0, 1), (1, 0)])]
  transfers between devices with their start and end apart: 21 -> 21, of which waited for: 12 -> 11; matrix products, arithmetic and copies ran while one was open for 1% -> 1% of each run, Pallas kernels for 24% -> 28%
where the time goes in v3:
time: 85.1 us; the launch traced here: 85 us
  Pallas kernels  32.9 us (39%)
  starting transfers between devices  26.7 us (31%)
  waiting for transfers between devices  22.3 us (26%)
  other arithmetic  1.45 us (2%)
  local copies, waits for them, and re-layouts  1.44 us (2%)
    ppermute x19, starting transfers between devices, swap(): lax.ppermute(array, 'vocab', [(i, i ^ bits) for i in range(vocab_size)])  24.7 us
    ppermute x19, waiting for transfers between devices, swap(): lax.ppermute(array, 'vocab', [(i, i ^ bits) for i in range(vocab_size)])  19.4 us
    pallas_call x2, Pallas kernels, piece_scores(): pl.pallas_call(kernel, in_specs=[SMEM] + [VMEM] * len(arrays) + [VMEM, VM...  9.89 us
    pallas_call x2, Pallas kernels, half_product(): pl.pallas_call(kernel, in_specs=[VMEM, HBM], out_specs=VMEM, out_shape=ja...  7.76 us
    pallas_call x1, Pallas kernels, successor_rows(): pl.pallas_call(kernel, in_specs=[SMEM, VMEM, HBM], out_specs=[VMEM, HBM],...  7.52 us
    pallas_call x1, Pallas kernels, stage(): pl.pallas_call(kernel, in_specs=[HBM], out_specs=VMEM, out_shape=pltpu.VM...  5.92 us
    ppermute x1, waiting for transfers between devices, body(): part = part + lax.ppermute(part, 'hid', [(0, 1), (1, 0)])  2.87 us
    pallas_call x1, Pallas kernels, take_seats(): pl.pallas_call(kernel, in_specs=[VMEM] * 3 + [HBM], out_specs=[SMEM, VMEM...  1.83 us
  transfers between devices with their start and end apart: 21, of which 11 were waited for; matrix products, arithmetic and copies ran while one was open for 1% of the time, Pallas kernels for 28%

profile of v3, /device:TPU:0, one launch (start us, length us, event | category | flops | bytes accessed | tf_op | source)
XLA Modules:
  0.0 85.0 jit_solution(7135809897315241447)
XLA Ops:
  0.0 0.9 %copy-done = bf16[128,1024]{1,0:T(8,128)(2,1)S(1)} copy-done((bf16[128,1024]{1,0:T(8,128)(2,1)S(1)}, bf16[128,1024]{1,0:T(8,128)(2,1)}, u32[]{:S(2)}) %copy-start) | copy-done | bytes 262168
  1.0 3.9 %prior_half.3 = bf16[8,128,512]{2,1,0:T(8,128)(2,1)S(1)} custom-call(bf16[128,1024]{1,0:T(8,128)(2,1)S(1)} %copy-done, bf16[1024,8192]{1,0:T(8,128)(2,1)} %trans_ref.3), custom_call_target="tpu_custom_call" | custom-call | flops 1048576 | bytes 1048576 | tf_op jit(solution)/shard_map/prior_half/pallas_call | solution.py:62
  4.9 0.5 collective-permute-start
  5.4 3.9 %prior_half.2 = bf16[8,128,512]{2,1,0:T(8,128)(2,1)S(1)} custom-call(bf16[128,1024]{1,0:T(8,128)(2,1)S(1)} %copy-done, bf16[1024,8192]{1,0:T(8,128)(2,1)} %trans_ref.3), custom_call_target="tpu_custom_call" | custom-call | flops 1048576 | bytes 1048576 | tf_op jit(solution)/shard_map/prior_half/pallas_call | solution.py:62
  9.3 0.3 add_convert_fusion.1
  9.6 2.6 %collective-permute-start.1 = (bf16[2,128,512]{2,1,0:T(8,128)(2,1)S(1)}, bf16[2,128,512]{2,1,0:T(8,128)(2,1)S(1)}, u32[]{:S(2)}, u32[]{:S(2)}) collective-permute-start(bf16[2,128,512]{2,1,0:T(8,128)(2,1)S(1)} %get-tuple-element.84), channel_id=1, source_target_pairs={{0,4},{2,6},{4,0},{6,2},{8,12},{10,14},{12,8},{14,10},{16,20},{18,... | collective-permute-start | bytes 786440 | tf_op jit(solution)/shard_map/ppermute | solution.py:348
  12.1 0.1 copy.10.next_ref
  12.3 0.1 collective-permute-start.2
  12.4 1.8 %take_seats.1 = (s32[17]{0:T(128)S(1)}, bf16[512,128]{1,0:T(8,128)(2,1)S(1)}, s32[512,8]{1,0:T(8,128)S(1)}, bf16[128,1024]{1,0:T(8,128)(2,1)S(1)}) custom-call(s32[8,128]{1,0:T(8,128)S(1)} %bitcast.27, s32[1,128]{1,0:T(1,128)S(1)} %bitcast.28, s32[256,8]{1,0:T(8,128)S(1)} %copy.10.next_ref, s32[256,1024]{1,0:T(8,128)} %token_hbm), custom_call_target="tpu_custom_call" | custom-call | flops 1048576 | bytes 1048576 | tf_op jit(solution)/shard_map/take_seats/pallas_call | solution.py:122
  14.2 5.1 %collective-permute-done.1 = bf16[2,128,512]{2,1,0:T(8,128)(2,1)S(1)} collective-permute-done((bf16[2,128,512]{2,1,0:T(8,128)(2,1)S(1)}, bf16[2,128,512]{2,1,0:T(8,128)(2,1)S(1)}, u32[]{:S(2)}, u32[]{:S(2)}) %collective-permute-start.1) | collective-permute-done | bytes 262176 | tf_op jit(solution)/shard_map/ppermute | solution.py:348
  19.3 0.1 add_convert_fusion
  19.4 3.1 %collective-permute-start.3 = (bf16[128,512]{1,0:T(8,128)(2,1)S(1)}, bf16[128,512]{1,0:T(8,128)(2,1)S(1)}, u32[]{:S(2)}, u32[]{:S(2)}) collective-permute-start(bf16[128,512]{1,0:T(8,128)(2,1)S(1)} %get-tuple-element.86), channel_id=1, source_target_pairs={{0,16},{2,18},{4,20},{6,22},{8,24},{10,26},{12,28},{14,30},{16,0},... | collective-permute-start | bytes 393224 | tf_op jit(solution)/shard_map/ppermute | solution.py:348
  22.5 1.3 %collective-permute-start.4 = (bf16[128,512]{1,0:T(8,128)(2,1)S(1)}, bf16[128,512]{1,0:T(8,128)(2,1)S(1)}, u32[]{:S(2)}, u32[]{:S(2)}) collective-permute-start(bf16[128,512]{1,0:T(8,128)(2,1)S(1)} %get-tuple-element.85), channel_id=1, source_target_pairs={{0,24},{2,26},{4,28},{6,30},{8,16},{10,18},{12,20},{14,22},{16,8},... | collective-permute-start | bytes 393224 | tf_op jit(solution)/shard_map/ppermute | solution.py:348
  23.9 0.9 %collective-permute-done.2 = bf16[2,128,512]{2,1,0:T(8,128)(2,1)S(1)} collective-permute-done((bf16[2,128,512]{2,1,0:T(8,128)(2,1)S(1)}, bf16[2,128,512]{2,1,0:T(8,128)(2,1)S(1)}, u32[]{:S(2)}, u32[]{:S(2)}) %collective-permute-start.2) | collective-permute-done | bytes 262176 | tf_op jit(solution)/shard_map/ppermute | solution.py:348
  24.7 0.1 convert_add_fusion
  24.8 1.9 %collective-permute-start.5 = (bf16[128,512]{1,0:T(8,128)(2,1)S(1)}, bf16[128,512]{1,0:T(8,128)(2,1)S(1)}, u32[]{:S(2)}, u32[]{:S(2)}) collective-permute-start(bf16[128,512]{1,0:T(8,128)(2,1)S(1)} %fusion.4), channel_id=1, source_target_pairs={{0,8},{2,10},{4,12},{6,14},{8,0},{10,2},{12,4},{14,6},{16,24},{18,... | collective-permute-start | bytes 393224 | tf_op jit(solution)/shard_map/ppermute | solution.py:348
  26.7 7.5 %successor_rows.1 = (bf16[1024,8192]{1,0:T(8,128)(2,1)S(1)}, bf16[4096,8192]{1,0:T(8,128)(2,1)}) custom-call(s32[17]{0:T(128)S(1)} %get-tuple-element.51.head_ref, s32[512,8]{1,0:T(8,128)S(1)} %get-tuple-element.56.after_ref, bf16[256,8192]{1,0:T(8,128)(2,1)} %adv_hbm.1), custom_call_target="tpu_custom_call" | custom-call | flops 1048576 | bytes 1048576 | tf_op jit(solution)/shard_map/successor_rows/pallas_call | solution.py:184
  34.3 0.1 fusion.3
  34.3 2.7 %collective-permute-start.8 = (bf16[128,512]{1,0:T(8,128)(2,1)S(1)}, bf16[128,512]{1,0:T(8,128)(2,1)S(1)}, u32[]{:S(2)}, u32[]{:S(2)}) collective-permute-start(bf16[128,512]{1,0:T(8,128)(2,1)S(1)} %fusion.3), channel_id=1, source_target_pairs={{0,16},{2,18},{4,20},{6,22},{8,24},{10,26},{12,28},{14,30},{16,0},... | collective-permute-start | bytes 393224 | tf_op jit(solution)/shard_map/ppermute | solution.py:348
  37.0 0.6 collective-permute-start.9
  37.6 1.5 %collective-permute-start.6 = (bf16[128,512]{1,0:T(8,128)(2,1)S(1)}, bf16[128,512]{1,0:T(8,128)(2,1)S(1)}, u32[]{:S(2)}, u32[]{:S(2)}) collective-permute-start(bf16[128,512]{1,0:T(8,128)(2,1)S(1)} %fusion.3), channel_id=1, source_target_pairs={{0,4},{2,6},{4,0},{6,2},{8,12},{10,14},{12,8},{14,10},{16,20},{18,... | collective-permute-start | bytes 393224 | tf_op jit(solution)/shard_map/ppermute | solution.py:348
  39.1 5.9 %stage.1.refs_7_ = bf16[8192,1024]{1,0:T(8,128)(2,1)S(1)} custom-call(bf16[8192,1024]{1,0:T(8,128)(2,1)} %hbm), custom_call_target="tpu_custom_call" | custom-call | flops 1048576 | bytes 1048576 | tf_op jit(solution)/shard_map/stage/pallas_call | solution.py:215
  45.0 1.9 %collective-permute-done.8 = bf16[128,512]{1,0:T(8,128)(2,1)S(1)} collective-permute-done((bf16[128,512]{1,0:T(8,128)(2,1)S(1)}, bf16[128,512]{1,0:T(8,128)(2,1)S(1)}, u32[]{:S(2)}, u32[]{:S(2)}) %collective-permute-start.8) | collective-permute-done | bytes 131104 | tf_op jit(solution)/shard_map/ppermute | solution.py:348
  47.0 0.1 collective-permute-start.12
  47.1 0.5 collective-permute-start.11
  47.7 1.5 %collective-permute-start.10 = (bf16[2,128,512]{2,1,0:T(8,128)(2,1)S(1)}, bf16[2,128,512]{2,1,0:T(8,128)(2,1)S(1)}, u32[]{:S(2)}, u32[]{:S(2)}) collective-permute-start(bf16[2,128,512]{2,1,0:T(8,128)(2,1)S(1)} %pad_maximum_fusion.1.refs_2_), channel_id=1, source_target_pairs={{0,4},{2,6},{4,0},{6,2},{8,12},{10,14},{12,8},{14,10},{16,20},{18,... | collective-permute-start | bytes 786440 | tf_op jit(solution)/shard_map/ppermute | solution.py:348
  49.2 2.5 %collective-permute-start.7 = (bf16[2,128,512]{2,1,0:T(8,128)(2,1)S(1)}, bf16[2,128,512]{2,1,0:T(8,128)(2,1)S(1)}, u32[]{:S(2)}, u32[]{:S(2)}) collective-permute-start(bf16[2,128,512]{2,1,0:T(8,128)(2,1)S(1)} %pad_maximum_fusion.refs_0_), channel_id=1, source_target_pairs={{0,8},{2,10},{4,12},{6,14},{8,0},{10,2},{12,4},{14,6},{16,24},{18,... | collective-permute-start | bytes 786440 | tf_op jit(solution)/shard_map/ppermute | solution.py:348
  51.7 4.3 %piece_scores.2.refs_9_ = f32[512,256]{1,0:T(8,128)S(1)} custom-call(s32[17]{0:T(128)S(1)} %get-tuple-element.51.head_ref, bf16[2,128,512]{2,1,0:T(8,128)(2,1)S(1)} %pad_maximum_fusion.refs_0_, bf16[2,128,512]{2,1,0:T(8,128)(2,1)S(1)} %collective-permute-done.11.refs_1_, bf16[2,128,512]{2,1,0:T(8,128)(2,1)S(1)} %pad_maximum_fusion.1.refs_2_, ...), custom_call_target="tpu_custom_call" | custom-call | flops 1048576 | bytes 1048576 | tf_op jit(solution)/shard_map/piece_scores/pallas_call | solution.py:317
  56.0 1.9 %collective-permute-done.7.refs_0_ = bf16[2,128,512]{2,1,0:T(8,128)(2,1)S(1)} collective-permute-done((bf16[2,128,512]{2,1,0:T(8,128)(2,1)S(1)}, bf16[2,128,512]{2,1,0:T(8,128)(2,1)S(1)}, u32[]{:S(2)}, u32[]{:S(2)}) %collective-permute-start.7) | collective-permute-done | bytes 262176 | tf_op jit(solution)/shard_map/ppermute | solution.py:348
  57.9 0.5 collective-permute-start.14
  58.4 1.0 %collective-permute-done.13.refs_1_ = bf16[2,128,512]{2,1,0:T(8,128)(2,1)S(1)} collective-permute-done((bf16[2,128,512]{2,1,0:T(8,128)(2,1)S(1)}, bf16[2,128,512]{2,1,0:T(8,128)(2,1)S(1)}, u32[]{:S(2)}, u32[]{:S(2)}) %collective-permute-start.13) | collective-permute-done | bytes 262176 | tf_op jit(solution)/shard_map/ppermute | solution.py:348
  59.5 0.4 collective-permute-done.14.refs_3_
  59.8 5.5 %piece_scores.3 = (f32[64,1024]{1,0:T(8,128)S(1)}, bf16[64,1024]{1,0:T(8,128)(2,1)S(1)}, f32[1,128]{1,0:T(1,128)S(1)}) custom-call(s32[17]{0:T(128)S(1)} %get-tuple-element.51.head_ref, bf16[2,128,512]{2,1,0:T(8,128)(2,1)S(1)} %collective-permute-done.7.refs_0_, bf16[2,128,512]{2,1,0:T(8,128)(2,1)S(1)} %collective-permute-done.13.refs_1_, ...), custom_call_target="tpu_custom_call" | custom-call | flops 1048576 | bytes 1048576 | tf_op jit(solution)/shard_map/piece_scores/pallas_call | solution.py:317
  65.4 3.7 %collective-permute-start.15 = (f32[1,128]{1,0:T(1,128)S(1)}, f32[1,128]{1,0:T(1,128)S(1)}, u32[]{:S(2)}, u32[]{:S(2)}) collective-permute-start(f32[1,128]{1,0:T(1,128)S(1)} %get-tuple-element.75), channel_id=1, source_target_pairs={{0,16},{2,18},{4,20},{6,22},{8,24},{10,26},{12,28},{14,30},{16,0},... | collective-permute-start | bytes 1544 | tf_op jit(solution)/shard_map/ppermute | solution.py:348
  69.1 1.5 %collective-permute-done.15 = f32[1,128]{1,0:T(1,128)S(1)} collective-permute-done((f32[1,128]{1,0:T(1,128)S(1)}, f32[1,128]{1,0:T(1,128)S(1)}, u32[]{:S(2)}, u32[]{:S(2)}) %collective-permute-start.15) | collective-permute-done | bytes 544 | tf_op jit(solution)/shard_map/ppermute | solution.py:348
  70.6 1.5 %collective-permute-start.19 = (bf16[64,1024]{1,0:T(8,128)(2,1)S(1)}, bf16[64,1024]{1,0:T(8,128)(2,1)S(1)}, u32[]{:S(2)}, u32[]{:S(2)}) collective-permute-start(bf16[64,1024]{1,0:T(8,128)(2,1)S(1)} %get-tuple-element.78), channel_id=1, source_target_pairs={{0,1},{1,0},{2,3},{3,2},{4,5},{5,4},{6,7},{7,6},{8,9},{9,8},{10,11... | collective-permute-start | bytes 393224 | tf_op jit(solution)/shard_map/ppermute | solution.py:421
  72.2 1.0 %collective-permute-start.16 = (f32[1,128]{1,0:T(1,128)S(1)}, f32[1,128]{1,0:T(1,128)S(1)}, u32[]{:S(2)}, u32[]{:S(2)}) collective-permute-start(f32[1,128]{1,0:T(1,128)S(1)} %add.59), channel_id=1, source_target_pairs={{0,8},{2,10},{4,12},{6,14},{8,0},{10,2},{12,4},{14,6},{16,24},{18,... | collective-permute-start | bytes 1544 | tf_op jit(solution)/shard_map/ppermute | solution.py:348
  73.2 2.5 %collective-permute-done.16 = f32[1,128]{1,0:T(1,128)S(1)} collective-permute-done((f32[1,128]{1,0:T(1,128)S(1)}, f32[1,128]{1,0:T(1,128)S(1)}, u32[]{:S(2)}, u32[]{:S(2)}) %collective-permute-start.16) | collective-permute-done | bytes 544 | tf_op jit(solution)/shard_map/ppermute | solution.py:348
  75.7 0.5 collective-permute-start.17
  76.3 3.0 %collective-permute-done.17 = f32[1,128]{1,0:T(1,128)S(1)} collective-permute-done((f32[1,128]{1,0:T(1,128)S(1)}, f32[1,128]{1,0:T(1,128)S(1)}, u32[]{:S(2)}, u32[]{:S(2)}) %collective-permute-start.17) | collective-permute-done | bytes 544 | tf_op jit(solution)/shard_map/ppermute | solution.py:348
  79.3 1.1 %collective-permute-done.18 = f32[1,128]{1,0:T(1,128)S(1)} collective-permute-done((f32[1,128]{1,0:T(1,128)S(1)}, f32[1,128]{1,0:T(1,128)S(1)}, u32[]{:S(2)}, u32[]{:S(2)}) %collective-permute-start.18) | collective-permute-done | bytes 544 | tf_op jit(solution)/shard_map/ppermute | solution.py:348
  80.4 0.5 collective-permute-start.20
  80.9 0.1 dynamic-slice_compare_fusion
  81.0 0.1 copy.9
  81.1 2.9 %collective-permute-done.20 = f32[1,128]{1,0:T(1,128)S(1)} collective-permute-done((f32[1,128]{1,0:T(1,128)S(1)}, f32[1,128]{1,0:T(1,128)S(1)}, u32[]{:S(2)}, u32[]{:S(2)}) %collective-permute-start.20) | collective-permute-done | bytes 544 | tf_op jit(solution)/shard_map/ppermute | solution.py:424
  83.9 0.1 log_bitcast_fusion
  84.0 0.1 broadcast_in_dim.14
  84.2 0.8 subtract_select_fusion
  (28 shorter events, 0.2 us)
Async XLA Ops:
  0.0 0.9 %copy-start = (bf16[128,1024]{1,0:T(8,128)(2,1)S(1)}, bf16[128,1024]{1,0:T(8,128)(2,1)}, u32[]{:S(2)}) copy-start(bf16[128,1024]{1,0:T(8,128)(2,1)} %post_ref.3) | copy-start | bytes 786436
  1.0 11.2 %copy-start.3 = (s32[256,8]{0,1:T(8,128)S(1)}, s32[256,8]{0,1:T(8,128)}, u32[]{:S(2)}) copy-start(s32[256,8]{0,1:T(8,128)} %param.13) | copy-start | bytes 24580
  1.0 11.4 %copy-start.1 = (s32[128,8]{0,1:T(8,128)S(1)}, s32[128,8]{0,1:T(8,128)}, u32[]{:S(2)}) copy-start(s32[128,8]{0,1:T(8,128)} %param.15) | copy-start | bytes 12292
  1.0 11.4 %copy-start.2 = (s32[128]{0:T(128)S(1)}, s32[128]{0:T(128)}, u32[]{:S(2)}) copy-start(s32[128]{0:T(128)} %param.12) | copy-start | bytes 1540
  4.9 4.4 %collective-permute-start = (bf16[8,128,512]{2,1,0:T(8,128)(2,1)S(1)}, bf16[8,128,512]{2,1,0:T(8,128)(2,1)S(1)}, u32[]{:S(2)}, u32[]{:S(2)}) collective-permute-start(bf16[8,128,512]{2,1,0:T(8,128)(2,1)S(1)} %prior_half.3), channel_id=1, source_target_pairs={{0,2},{2,0},{4,6},{6,4},{8,10},{10,8},{12,14},{14,12},{16,18},{18,... | collective-permute-start | bytes 3145736 | tf_op jit(solution)/shard_map/ppermute | solution.py:348
  9.6 9.7 %collective-permute-start.1 = (bf16[2,128,512]{2,1,0:T(8,128)(2,1)S(1)}, bf16[2,128,512]{2,1,0:T(8,128)(2,1)S(1)}, u32[]{:S(2)}, u32[]{:S(2)}) collective-permute-start(bf16[2,128,512]{2,1,0:T(8,128)(2,1)S(1)} %get-tuple-element.84), channel_id=1, source_target_pairs={{0,4},{2,6},{4,0},{6,2},{8,12},{10,14},{12,8},{14,10},{16,20},{18,... | collective-permute-start | bytes 786440 | tf_op jit(solution)/shard_map/ppermute | solution.py:348
  12.3 12.4 %collective-permute-start.2 = (bf16[2,128,512]{2,1,0:T(8,128)(2,1)S(1)}, bf16[2,128,512]{2,1,0:T(8,128)(2,1)S(1)}, u32[]{:S(2)}, u32[]{:S(2)}) collective-permute-start(bf16[2,128,512]{2,1,0:T(8,128)(2,1)S(1)} %get-tuple-element.53), channel_id=1, source_target_pairs={{0,4},{2,6},{4,0},{6,2},{8,12},{10,14},{12,8},{14,10},{16,20},{18,... | collective-permute-start | bytes 786440 | tf_op jit(solution)/shard_map/ppermute | solution.py:348
  19.4 14.8 %collective-permute-start.3 = (bf16[128,512]{1,0:T(8,128)(2,1)S(1)}, bf16[128,512]{1,0:T(8,128)(2,1)S(1)}, u32[]{:S(2)}, u32[]{:S(2)}) collective-permute-start(bf16[128,512]{1,0:T(8,128)(2,1)S(1)} %get-tuple-element.86), channel_id=1, source_target_pairs={{0,16},{2,18},{4,20},{6,22},{8,24},{10,26},{12,28},{14,30},{16,0},... | collective-permute-start | bytes 393224 | tf_op jit(solution)/shard_map/ppermute | solution.py:348
  22.5 11.7 %collective-permute-start.4 = (bf16[128,512]{1,0:T(8,128)(2,1)S(1)}, bf16[128,512]{1,0:T(8,128)(2,1)S(1)}, u32[]{:S(2)}, u32[]{:S(2)}) collective-permute-start(bf16[128,512]{1,0:T(8,128)(2,1)S(1)} %get-tuple-element.85), channel_id=1, source_target_pairs={{0,24},{2,26},{4,28},{6,30},{8,16},{10,18},{12,20},{14,22},{16,8},... | collective-permute-start | bytes 393224 | tf_op jit(solution)/shard_map/ppermute | solution.py:348
  24.8 9.4 %collective-permute-start.5 = (bf16[128,512]{1,0:T(8,128)(2,1)S(1)}, bf16[128,512]{1,0:T(8,128)(2,1)S(1)}, u32[]{:S(2)}, u32[]{:S(2)}) collective-permute-start(bf16[128,512]{1,0:T(8,128)(2,1)S(1)} %fusion.4), channel_id=1, source_target_pairs={{0,8},{2,10},{4,12},{6,14},{8,0},{10,2},{12,4},{14,6},{16,24},{18,... | collective-permute-start | bytes 393224 | tf_op jit(solution)/shard_map/ppermute | solution.py:348
  34.3 12.6 %collective-permute-start.8 = (bf16[128,512]{1,0:T(8,128)(2,1)S(1)}, bf16[128,512]{1,0:T(8,128)(2,1)S(1)}, u32[]{:S(2)}, u32[]{:S(2)}) collective-permute-start(bf16[128,512]{1,0:T(8,128)(2,1)S(1)} %fusion.3), channel_id=1, source_target_pairs={{0,16},{2,18},{4,20},{6,22},{8,24},{10,26},{12,28},{14,30},{16,0},... | collective-permute-start | bytes 393224 | tf_op jit(solution)/shard_map/ppermute | solution.py:348
  37.0 10.0 %collective-permute-start.9 = (bf16[128,512]{1,0:T(8,128)(2,1)S(1)}, bf16[128,512]{1,0:T(8,128)(2,1)S(1)}, u32[]{:S(2)}, u32[]{:S(2)}) collective-permute-start(bf16[128,512]{1,0:T(8,128)(2,1)S(1)} %fusion.3), channel_id=1, source_target_pairs={{0,24},{2,26},{4,28},{6,30},{8,16},{10,18},{12,20},{14,22},{16,8},... | collective-permute-start | bytes 393224 | tf_op jit(solution)/shard_map/ppermute | solution.py:348
  37.6 9.5 %collective-permute-start.6 = (bf16[128,512]{1,0:T(8,128)(2,1)S(1)}, bf16[128,512]{1,0:T(8,128)(2,1)S(1)}, u32[]{:S(2)}, u32[]{:S(2)}) collective-permute-start(bf16[128,512]{1,0:T(8,128)(2,1)S(1)} %fusion.3), channel_id=1, source_target_pairs={{0,4},{2,6},{4,0},{6,2},{8,12},{10,14},{12,8},{14,10},{16,20},{18,... | collective-permute-start | bytes 393224 | tf_op jit(solution)/shard_map/ppermute | solution.py:348
  47.0 4.6 %collective-permute-start.12 = (bf16[2,128,512]{2,1,0:T(8,128)(2,1)S(1)}, bf16[2,128,512]{2,1,0:T(8,128)(2,1)S(1)}, u32[]{:S(2)}, u32[]{:S(2)}) collective-permute-start(bf16[2,128,512]{2,1,0:T(8,128)(2,1)S(1)} %pad_maximum_fusion.1.refs_2_), channel_id=1, source_target_pairs={{0,2},{2,0},{4,6},{6,4},{8,10},{10,8},{12,14},{14,12},{16,18},{18,... | collective-permute-start | bytes 786440 | tf_op jit(solution)/shard_map/ppermute | solution.py:348
  47.1 4.5 %collective-permute-start.11 = (bf16[2,128,512]{2,1,0:T(8,128)(2,1)S(1)}, bf16[2,128,512]{2,1,0:T(8,128)(2,1)S(1)}, u32[]{:S(2)}, u32[]{:S(2)}) collective-permute-start(bf16[2,128,512]{2,1,0:T(8,128)(2,1)S(1)} %pad_maximum_fusion.refs_0_), channel_id=1, source_target_pairs={{0,2},{2,0},{4,6},{6,4},{8,10},{10,8},{12,14},{14,12},{16,18},{18,... | collective-permute-start | bytes 786440 | tf_op jit(solution)/shard_map/ppermute | solution.py:348
  47.7 8.3 %collective-permute-start.10 = (bf16[2,128,512]{2,1,0:T(8,128)(2,1)S(1)}, bf16[2,128,512]{2,1,0:T(8,128)(2,1)S(1)}, u32[]{:S(2)}, u32[]{:S(2)}) collective-permute-start(bf16[2,128,512]{2,1,0:T(8,128)(2,1)S(1)} %pad_maximum_fusion.1.refs_2_), channel_id=1, source_target_pairs={{0,4},{2,6},{4,0},{6,2},{8,12},{10,14},{12,8},{14,10},{16,20},{18,... | collective-permute-start | bytes 786440 | tf_op jit(solution)/shard_map/ppermute | solution.py:348
  49.2 8.8 %collective-permute-start.7 = (bf16[2,128,512]{2,1,0:T(8,128)(2,1)S(1)}, bf16[2,128,512]{2,1,0:T(8,128)(2,1)S(1)}, u32[]{:S(2)}, u32[]{:S(2)}) collective-permute-start(bf16[2,128,512]{2,1,0:T(8,128)(2,1)S(1)} %pad_maximum_fusion.refs_0_), channel_id=1, source_target_pairs={{0,8},{2,10},{4,12},{6,14},{8,0},{10,2},{12,4},{14,6},{16,24},{18,... | collective-permute-start | bytes 786440 | tf_op jit(solution)/shard_map/ppermute | solution.py:348
  57.9 1.5 %collective-permute-start.13 = (bf16[2,128,512]{2,1,0:T(8,128)(2,1)S(1)}, bf16[2,128,512]{2,1,0:T(8,128)(2,1)S(1)}, u32[]{:S(2)}, u32[]{:S(2)}) collective-permute-start(bf16[2,128,512]{2,1,0:T(8,128)(2,1)S(1)} %collective-permute-done.7.refs_0_), channel_id=1, source_target_pairs={{0,2},{2,0},{4,6},{6,4},{8,10},{10,8},{12,14},{14,12},{16,18},{18,... | collective-permute-start | bytes 786440 | tf_op jit(solution)/shard_map/ppermute | solution.py:348
  57.9 1.9 %collective-permute-start.14 = (bf16[2,128,512]{2,1,0:T(8,128)(2,1)S(1)}, bf16[2,128,512]{2,1,0:T(8,128)(2,1)S(1)}, u32[]{:S(2)}, u32[]{:S(2)}) collective-permute-start(bf16[2,128,512]{2,1,0:T(8,128)(2,1)S(1)} %collective-permute-done.10.refs_2_), channel_id=1, source_target_pairs={{0,2},{2,0},{4,6},{6,4},{8,10},{10,8},{12,14},{14,12},{16,18},{18,... | collective-permute-start | bytes 786440 | tf_op jit(solution)/shard_map/ppermute | solution.py:348
  65.4 5.2 %collective-permute-start.15 = (f32[1,128]{1,0:T(1,128)S(1)}, f32[1,128]{1,0:T(1,128)S(1)}, u32[]{:S(2)}, u32[]{:S(2)}) collective-permute-start(f32[1,128]{1,0:T(1,128)S(1)} %get-tuple-element.75), channel_id=1, source_target_pairs={{0,16},{2,18},{4,20},{6,22},{8,24},{10,26},{12,28},{14,30},{16,0},... | collective-permute-start | bytes 1544 | tf_op jit(solution)/shard_map/ppermute | solution.py:348
  70.6 9.8 %collective-permute-start.19 = (bf16[64,1024]{1,0:T(8,128)(2,1)S(1)}, bf16[64,1024]{1,0:T(8,128)(2,1)S(1)}, u32[]{:S(2)}, u32[]{:S(2)}) collective-permute-start(bf16[64,1024]{1,0:T(8,128)(2,1)S(1)} %get-tuple-element.78), channel_id=1, source_target_pairs={{0,1},{1,0},{2,3},{3,2},{4,5},{5,4},{6,7},{7,6},{8,9},{9,8},{10,11... | collective-permute-start | bytes 393224 | tf_op jit(solution)/shard_map/ppermute | solution.py:421
  72.2 3.5 %collective-permute-start.16 = (f32[1,128]{1,0:T(1,128)S(1)}, f32[1,128]{1,0:T(1,128)S(1)}, u32[]{:S(2)}, u32[]{:S(2)}) collective-permute-start(f32[1,128]{1,0:T(1,128)S(1)} %add.59), channel_id=1, source_target_pairs={{0,8},{2,10},{4,12},{6,14},{8,0},{10,2},{12,4},{14,6},{16,24},{18,... | collective-permute-start | bytes 1544 | tf_op jit(solution)/shard_map/ppermute | solution.py:348
  75.7 3.5 %collective-permute-start.17 = (f32[1,128]{1,0:T(1,128)S(1)}, f32[1,128]{1,0:T(1,128)S(1)}, u32[]{:S(2)}, u32[]{:S(2)}) collective-permute-start(f32[1,128]{1,0:T(1,128)S(1)} %add.60), channel_id=1, source_target_pairs={{0,4},{2,6},{4,0},{6,2},{8,12},{10,14},{12,8},{14,10},{16,20},{18,... | collective-permute-start | bytes 1544 | tf_op jit(solution)/shard_map/ppermute | solution.py:348
  79.3 1.1 %collective-permute-start.18 = (f32[1,128]{1,0:T(1,128)S(1)}, f32[1,128]{1,0:T(1,128)S(1)}, u32[]{:S(2)}, u32[]{:S(2)}) collective-permute-start(f32[1,128]{1,0:T(1,128)S(1)} %add.61), channel_id=1, source_target_pairs={{0,2},{2,0},{4,6},{6,4},{8,10},{10,8},{12,14},{14,12},{16,18},{18,... | collective-permute-start | bytes 1544 | tf_op jit(solution)/shard_map/ppermute | solution.py:348
  80.4 3.5 %collective-permute-start.20 = (f32[1,128]{1,0:T(1,128)S(1)}, f32[1,128]{1,0:T(1,128)S(1)}, u32[]{:S(2)}, u32[]{:S(2)}) collective-permute-start(f32[1,128]{1,0:T(1,128)S(1)} %add.62), channel_id=1, source_target_pairs={{0,1},{1,0},{2,3},{3,2},{4,5},{5,4},{6,7},{7,6},{8,9},{9,8},{10,11... | collective-permute-start | bytes 1544 | tf_op jit(solution)/shard_map/ppermute | solution.py:424

commit v4 on v3

--- a/solution.py
+++ b/solution.py
@@ -355,9 +355,12 @@
         order = FAR_OTHER + FAR_SAME + NEAR_OTHER + NEAR_SAME
         away = half_product(posterior, transition, True, order, chips, width)
         came = swap(away, 1)
-        kept = half_product(posterior, transition, False, order, chips, width)
-        parts = [(kept[n : n + 2].astype(F32) + came[n : n + 2].astype(F32)).astype(BF16) for n in (0, 2, 4, 6)]
+        kept = half_product(posterior, transition, False, order[:4], chips, width)
+        parts = [(kept[n : n + 2].astype(F32) + came[n : n + 2].astype(F32)).astype(BF16) for n in (0, 2)]
+        parts, posterior = lax.optimization_barrier((parts, posterior))
         far = swap(parts[0], 2)
+        kept = half_product(posterior, transition, False, order[4:], chips, width)
+        parts += [(kept[n : n + 2].astype(F32) + came[n + 4 : n + 6].astype(F32)).astype(BF16) for n in (0, 2)]
         parts, small = lax.optimization_barrier((parts, small))
         near = swap(parts[2], 2)
         head, select, after, edges = seated(*small)
@@ -413,15 +416,16 @@
     mine, theirs, part = got
 
     if hid_size == 2:
-        bits = vocab_size // 2
-        while bits:
-            part = part + swap(part, bits)
-            if bits == vocab_size // 2:
-                part, theirs = lax.optimization_barrier((part, theirs))
-                theirs = lax.ppermute(theirs, "hid", [(0, 1), (1, 0)])
-            bits //= 2
-        part, theirs = lax.optimization_barrier((part, theirs))
-        part = part + lax.ppermute(part, "hid", [(0, 1), (1, 0)])
+        theirs = lax.ppermute(theirs, "hid", [(0, 1), (1, 0)])
+        if direct:
+            part = part + swap(part, 8) + swap(part, 12) + swap(part, 4)
+            part = part + swap(part, 1)
+            part, theirs = lax.optimization_barrier((part, theirs))
+            across = [(i, i ^ 5) for i in range(2 * vocab_size)]
+            beside = lax.ppermute(part, "hid", [(0, 1), (1, 0)])
+            part = part + swap(part, 2) + beside + lax.ppermute(part, ("vocab", "hid"), across)
+        else:
+            part = lax.psum(part, ("vocab", "hid"))
         totals = lax.dynamic_slice_in_dim(part[0], first, local, 0)
         mine = mine + theirs.astype(F32)
     else:

time: 85.1 us -> 81.9 us (0.962)
  waiting for transfers between devices: 22.3 us -> 15.5 us
  starting transfers between devices: 26.7 us -> 28.9 us
  Pallas kernels: 32.9 us -> 34.1 us
    ppermute x19 -> x20, waiting for transfers between devices: 19.4 us -> 12.7 us  [swap(): lax.ppermute(array, 'vocab', [(i, i ^ bits) for i in range(vocab_size)])]
    ppermute x1 -> x2, starting transfers between devices: 0.49 us -> 2.94 us  [the longest x1 1.52 us: body(): beside = lax.ppermute(part, 'hid', [(0, 1), (1, 0)])]
    pallas_call x2 -> x3, Pallas kernels: 7.76 us -> 8.95 us  [half_product(): pl.pallas_call(kernel, in_specs=[VMEM, HBM], out_specs=VMEM, out_shape=ja...]
    ppermute x19 -> x20, starting transfers between devices: 24.7 us -> 24.5 us  [swap(): lax.ppermute(array, 'vocab', [(i, i ^ bits) for i in range(vocab_size)])]
    ppermute x1 -> x2, waiting for transfers between devices: 2.87 us -> 2.83 us  [the longest x1 2.42 us: body(): lax.ppermute(part, ('vocab', 'hid'), across)]
  transfers between devices with their start and end apart: 21 -> 23, of which waited for: 11 -> 10; matrix products, arithmetic and copies ran while one was open for 1% -> 1% of each run, Pallas kernels for 28% -> 30%
where the time goes in v4:
time: 81.9 us; the launch traced here: 81.7 us
  Pallas kernels  34.1 us (42%)
  starting transfers between devices  28.9 us (35%)
  waiting for transfers between devices  15.5 us (19%)
  local copies, waits for them, and re-layouts  1.45 us (2%)
  other arithmetic  1.42 us (2%)
    ppermute x20, starting transfers between devices, swap(): lax.ppermute(array, 'vocab', [(i, i ^ bits) for i in range(vocab_size)])  24.5 us
    ppermute x20, waiting for transfers between devices, swap(): lax.ppermute(array, 'vocab', [(i, i ^ bits) for i in range(vocab_size)])  12.7 us
    pallas_call x2, Pallas kernels, piece_scores(): pl.pallas_call(kernel, in_specs=[SMEM] + [VMEM] * len(arrays) + [VMEM, VM...  9.88 us
    pallas_call x3, Pallas kernels, half_product(): pl.pallas_call(kernel, in_specs=[VMEM, HBM], out_specs=VMEM, out_shape=ja...  8.95 us
    pallas_call x1, Pallas kernels, successor_rows(): pl.pallas_call(kernel, in_specs=[SMEM, VMEM, HBM], out_specs=[VMEM, HBM],...  7.52 us
    pallas_call x1, Pallas kernels, stage(): pl.pallas_call(kernel, in_specs=[HBM], out_specs=VMEM, out_shape=pltpu.VM...  5.92 us
    ppermute x1, waiting for transfers between devices, body(): lax.ppermute(part, ('vocab', 'hid'), across)  2.42 us
    pallas_call x1, Pallas kernels, take_seats(): pl.pallas_call(kernel, in_specs=[VMEM] * 3 + [HBM], out_specs=[SMEM, VMEM...  1.83 us
  transfers between devices with their start and end apart: 23, of which 10 were waited for; matrix products, arithmetic and copies ran while one was open for 1% of the time, Pallas kernels for 30%

profile of v4, /device:TPU:0, one launch (start us, length us, event | category | flops | bytes accessed | tf_op | source)
XLA Modules:
  0.0 81.7 jit_solution(7475778313861123600)
XLA Ops:
  0.0 0.9 %copy-done = bf16[128,1024]{1,0:T(8,128)(2,1)S(1)} copy-done((bf16[128,1024]{1,0:T(8,128)(2,1)S(1)}, bf16[128,1024]{1,0:T(8,128)(2,1)}, u32[]{:S(2)}) %copy-start) | copy-done | bytes 262168
  1.0 3.9 %prior_half.4 = bf16[8,128,512]{2,1,0:T(8,128)(2,1)S(1)} custom-call(bf16[128,1024]{1,0:T(8,128)(2,1)S(1)} %copy-done, bf16[1024,8192]{1,0:T(8,128)(2,1)} %trans_ref.5), custom_call_target="tpu_custom_call" | custom-call | flops 1048576 | bytes 1048576 | tf_op jit(solution)/shard_map/prior_half/pallas_call | solution.py:62
  4.9 0.5 collective-permute-start
  5.4 2.5 %prior_half.3 = bf16[4,128,512]{2,1,0:T(8,128)(2,1)S(1)} custom-call(bf16[128,1024]{1,0:T(8,128)(2,1)S(1)} %copy-done, bf16[1024,8192]{1,0:T(8,128)(2,1)} %trans_ref.5), custom_call_target="tpu_custom_call" | custom-call | flops 1048576 | bytes 1048576 | tf_op jit(solution)/shard_map/prior_half/pallas_call | solution.py:62
  7.9 0.1 add_convert_fusion.3
  8.1 2.6 %collective-permute-start.1 = (bf16[2,128,512]{2,1,0:T(8,128)(2,1)S(1)}, bf16[2,128,512]{2,1,0:T(8,128)(2,1)S(1)}, u32[]{:S(2)}, u32[]{:S(2)}) collective-permute-start(bf16[2,128,512]{2,1,0:T(8,128)(2,1)S(1)} %get-tuple-element.44), channel_id=1, source_target_pairs={{0,4},{2,6},{4,0},{6,2},{8,12},{10,14},{12,8},{14,10},{16,20},{18,... | collective-permute-start | bytes 786440 | tf_op jit(solution)/shard_map/ppermute | solution.py:348
  10.7 2.5 %prior_half.5 = bf16[4,128,512]{2,1,0:T(8,128)(2,1)S(1)} custom-call(bf16[128,1024]{1,0:T(8,128)(2,1)S(1)} %copy-done, bf16[1024,8192]{1,0:T(8,128)(2,1)} %trans_ref.5), custom_call_target="tpu_custom_call" | custom-call | flops 1048576 | bytes 1048576 | tf_op jit(solution)/shard_map/prior_half/pallas_call | solution.py:62
  13.3 0.1 add_convert_fusion.1
  13.4 0.1 copy.10.next_ref
  13.6 0.1 collective-permute-start.2
  13.7 1.8 %take_seats.1 = (s32[17]{0:T(128)S(1)}, bf16[512,128]{1,0:T(8,128)(2,1)S(1)}, s32[512,8]{1,0:T(8,128)S(1)}, bf16[128,1024]{1,0:T(8,128)(2,1)S(1)}) custom-call(s32[8,128]{1,0:T(8,128)S(1)} %bitcast.27, s32[1,128]{1,0:T(1,128)S(1)} %bitcast.28, s32[256,8]{1,0:T(8,128)S(1)} %copy.10.next_ref, s32[256,1024]{1,0:T(8,128)} %token_hbm), custom_call_target="tpu_custom_call" | custom-call | flops 1048576 | bytes 1048576 | tf_op jit(solution)/shard_map/take_seats/pallas_call | solution.py:122
  15.5 2.4 %collective-permute-done.1 = bf16[2,128,512]{2,1,0:T(8,128)(2,1)S(1)} collective-permute-done((bf16[2,128,512]{2,1,0:T(8,128)(2,1)S(1)}, bf16[2,128,512]{2,1,0:T(8,128)(2,1)S(1)}, u32[]{:S(2)}, u32[]{:S(2)}) %collective-permute-start.1) | collective-permute-done | bytes 262176 | tf_op jit(solution)/shard_map/ppermute | solution.py:348
  18.0 3.1 %collective-permute-start.3 = (bf16[128,512]{1,0:T(8,128)(2,1)S(1)}, bf16[128,512]{1,0:T(8,128)(2,1)S(1)}, u32[]{:S(2)}, u32[]{:S(2)}) collective-permute-start(bf16[128,512]{1,0:T(8,128)(2,1)S(1)} %get-tuple-element.88), channel_id=1, source_target_pairs={{0,16},{2,18},{4,20},{6,22},{8,24},{10,26},{12,28},{14,30},{16,0},... | collective-permute-start | bytes 393224 | tf_op jit(solution)/shard_map/ppermute | solution.py:348
  21.1 1.4 %collective-permute-start.4 = (bf16[128,512]{1,0:T(8,128)(2,1)S(1)}, bf16[128,512]{1,0:T(8,128)(2,1)S(1)}, u32[]{:S(2)}, u32[]{:S(2)}) collective-permute-start(bf16[128,512]{1,0:T(8,128)(2,1)S(1)} %get-tuple-element.87), channel_id=1, source_target_pairs={{0,24},{2,26},{4,28},{6,30},{8,16},{10,18},{12,20},{14,22},{16,8},... | collective-permute-start | bytes 393224 | tf_op jit(solution)/shard_map/ppermute | solution.py:348
  22.5 0.8 collective-permute-done.2
  23.3 1.9 %collective-permute-start.5 = (bf16[128,512]{1,0:T(8,128)(2,1)S(1)}, bf16[128,512]{1,0:T(8,128)(2,1)S(1)}, u32[]{:S(2)}, u32[]{:S(2)}) collective-permute-start(bf16[128,512]{1,0:T(8,128)(2,1)S(1)} %fusion.4), channel_id=1, source_target_pairs={{0,8},{2,10},{4,12},{6,14},{8,0},{10,2},{12,4},{14,6},{16,24},{18,... | collective-permute-start | bytes 393224 | tf_op jit(solution)/shard_map/ppermute | solution.py:348
  25.2 7.5 %successor_rows.1 = (bf16[1024,8192]{1,0:T(8,128)(2,1)S(1)}, bf16[4096,8192]{1,0:T(8,128)(2,1)}) custom-call(s32[17]{0:T(128)S(1)} %get-tuple-element.55.head_ref, s32[512,8]{1,0:T(8,128)S(1)} %get-tuple-element.60.after_ref, bf16[256,8192]{1,0:T(8,128)(2,1)} %adv_hbm.1), custom_call_target="tpu_custom_call" | custom-call | flops 1048576 | bytes 1048576 | tf_op jit(solution)/shard_map/successor_rows/pallas_call | solution.py:184
  32.8 0.1 fusion.3
  32.9 2.7 %collective-permute-start.8 = (bf16[128,512]{1,0:T(8,128)(2,1)S(1)}, bf16[128,512]{1,0:T(8,128)(2,1)S(1)}, u32[]{:S(2)}, u32[]{:S(2)}) collective-permute-start(bf16[128,512]{1,0:T(8,128)(2,1)S(1)} %fusion.3), channel_id=1, source_target_pairs={{0,16},{2,18},{4,20},{6,22},{8,24},{10,26},{12,28},{14,30},{16,0},... | collective-permute-start | bytes 393224 | tf_op jit(solution)/shard_map/ppermute | solution.py:348
  35.5 0.6 collective-permute-start.9
  36.1 1.5 %collective-permute-start.6 = (bf16[128,512]{1,0:T(8,128)(2,1)S(1)}, bf16[128,512]{1,0:T(8,128)(2,1)S(1)}, u32[]{:S(2)}, u32[]{:S(2)}) collective-permute-start(bf16[128,512]{1,0:T(8,128)(2,1)S(1)} %fusion.3), channel_id=1, source_target_pairs={{0,4},{2,6},{4,0},{6,2},{8,12},{10,14},{12,8},{14,10},{16,20},{18,... | collective-permute-start | bytes 393224 | tf_op jit(solution)/shard_map/ppermute | solution.py:348
  37.6 5.9 %stage.1.refs_7_ = bf16[8192,1024]{1,0:T(8,128)(2,1)S(1)} custom-call(bf16[8192,1024]{1,0:T(8,128)(2,1)} %hbm), custom_call_target="tpu_custom_call" | custom-call | flops 1048576 | bytes 1048576 | tf_op jit(solution)/shard_map/stage/pallas_call | solution.py:215
  43.5 1.9 %collective-permute-done.8 = bf16[128,512]{1,0:T(8,128)(2,1)S(1)} collective-permute-done((bf16[128,512]{1,0:T(8,128)(2,1)S(1)}, bf16[128,512]{1,0:T(8,128)(2,1)S(1)}, u32[]{:S(2)}, u32[]{:S(2)}) %collective-permute-start.8) | collective-permute-done | bytes 131104 | tf_op jit(solution)/shard_map/ppermute | solution.py:348
  45.6 0.5 collective-permute-start.11
  46.2 1.5 %collective-permute-start.10 = (bf16[2,128,512]{2,1,0:T(8,128)(2,1)S(1)}, bf16[2,128,512]{2,1,0:T(8,128)(2,1)S(1)}, u32[]{:S(2)}, u32[]{:S(2)}) collective-permute-start(bf16[2,128,512]{2,1,0:T(8,128)(2,1)S(1)} %pad_maximum_fusion.1.refs_2_), channel_id=1, source_target_pairs={{0,4},{2,6},{4,0},{6,2},{8,12},{10,14},{12,8},{14,10},{16,20},{18,... | collective-permute-start | bytes 786440 | tf_op jit(solution)/shard_map/ppermute | solution.py:348
  47.7 2.5 %collective-permute-start.7 = (bf16[2,128,512]{2,1,0:T(8,128)(2,1)S(1)}, bf16[2,128,512]{2,1,0:T(8,128)(2,1)S(1)}, u32[]{:S(2)}, u32[]{:S(2)}) collective-permute-start(bf16[2,128,512]{2,1,0:T(8,128)(2,1)S(1)} %pad_maximum_fusion.refs_0_), channel_id=1, source_target_pairs={{0,8},{2,10},{4,12},{6,14},{8,0},{10,2},{12,4},{14,6},{16,24},{18,... | collective-permute-start | bytes 786440 | tf_op jit(solution)/shard_map/ppermute | solution.py:348
  50.2 4.3 %piece_scores.2.refs_9_ = f32[512,256]{1,0:T(8,128)S(1)} custom-call(s32[17]{0:T(128)S(1)} %get-tuple-element.55.head_ref, bf16[2,128,512]{2,1,0:T(8,128)(2,1)S(1)} %pad_maximum_fusion.refs_0_, bf16[2,128,512]{2,1,0:T(8,128)(2,1)S(1)} %collective-permute-done.11.refs_1_, bf16[2,128,512]{2,1,0:T(8,128)(2,1)S(1)} %pad_maximum_fusion.1.refs_2_, ...), custom_call_target="tpu_custom_call" | custom-call | flops 1048576 | bytes 1048576 | tf_op jit(solution)/shard_map/piece_scores/pallas_call | solution.py:317
  54.5 1.9 %collective-permute-done.7.refs_0_ = bf16[2,128,512]{2,1,0:T(8,128)(2,1)S(1)} collective-permute-done((bf16[2,128,512]{2,1,0:T(8,128)(2,1)S(1)}, bf16[2,128,512]{2,1,0:T(8,128)(2,1)S(1)}, u32[]{:S(2)}, u32[]{:S(2)}) %collective-permute-start.7) | collective-permute-done | bytes 262176 | tf_op jit(solution)/shard_map/ppermute | solution.py:348
  56.4 0.5 collective-permute-start.14
  56.9 1.0 %collective-permute-done.13.refs_1_ = bf16[2,128,512]{2,1,0:T(8,128)(2,1)S(1)} collective-permute-done((bf16[2,128,512]{2,1,0:T(8,128)(2,1)S(1)}, bf16[2,128,512]{2,1,0:T(8,128)(2,1)S(1)}, u32[]{:S(2)}, u32[]{:S(2)}) %collective-permute-start.13) | collective-permute-done | bytes 262176 | tf_op jit(solution)/shard_map/ppermute | solution.py:348
  58.0 0.4 collective-permute-done.14.refs_3_
  58.3 5.5 %piece_scores.3 = (f32[64,1024]{1,0:T(8,128)S(1)}, bf16[64,1024]{1,0:T(8,128)(2,1)S(1)}, f32[1,128]{1,0:T(1,128)S(1)}) custom-call(s32[17]{0:T(128)S(1)} %get-tuple-element.55.head_ref, bf16[2,128,512]{2,1,0:T(8,128)(2,1)S(1)} %collective-permute-done.7.refs_0_, bf16[2,128,512]{2,1,0:T(8,128)(2,1)S(1)} %collective-permute-done.13.refs_1_, ...), custom_call_target="tpu_custom_call" | custom-call | flops 1048576 | bytes 1048576 | tf_op jit(solution)/shard_map/piece_scores/pallas_call | solution.py:317
  63.9 3.7 %collective-permute-start.15 = (f32[1,128]{1,0:T(1,128)S(1)}, f32[1,128]{1,0:T(1,128)S(1)}, u32[]{:S(2)}, u32[]{:S(2)}) collective-permute-start(f32[1,128]{1,0:T(1,128)S(1)} %get-tuple-element.79), channel_id=1, source_target_pairs={{0,16},{2,18},{4,20},{6,22},{8,24},{10,26},{12,28},{14,30},{16,0},... | collective-permute-start | bytes 1544 | tf_op jit(solution)/shard_map/ppermute | solution.py:348
  67.6 0.4 collective-permute-start.16
  68.1 0.2 collective-permute-start.17
  68.3 1.5 %collective-permute-start.19 = (bf16[64,1024]{1,0:T(8,128)(2,1)S(1)}, bf16[64,1024]{1,0:T(8,128)(2,1)S(1)}, u32[]{:S(2)}, u32[]{:S(2)}) collective-permute-start(bf16[64,1024]{1,0:T(8,128)(2,1)S(1)} %get-tuple-element.80), channel_id=1, source_target_pairs={{0,1},{1,0},{2,3},{3,2},{4,5},{5,4},{6,7},{7,6},{8,9},{9,8},{10,11... | collective-permute-start | bytes 393224 | tf_op jit(solution)/shard_map/ppermute | solution.py:419
  69.8 3.2 %collective-permute-done.16 = f32[1,128]{1,0:T(1,128)S(1)} collective-permute-done((f32[1,128]{1,0:T(1,128)S(1)}, f32[1,128]{1,0:T(1,128)S(1)}, u32[]{:S(2)}, u32[]{:S(2)}) %collective-permute-start.16) | collective-permute-done | bytes 544 | tf_op jit(solution)/shard_map/ppermute | solution.py:348
  73.1 1.1 %collective-permute-done.18 = f32[1,128]{1,0:T(1,128)S(1)} collective-permute-done((f32[1,128]{1,0:T(1,128)S(1)}, f32[1,128]{1,0:T(1,128)S(1)}, u32[]{:S(2)}, u32[]{:S(2)}) %collective-permute-start.18) | collective-permute-done | bytes 544 | tf_op jit(solution)/shard_map/ppermute | solution.py:348
  74.2 0.5 collective-permute-start.20
  74.7 1.5 %collective-permute-start.21 = (f32[1,128]{1,0:T(1,128)S(1)}, f32[1,128]{1,0:T(1,128)S(1)}, u32[]{:S(2)}, u32[]{:S(2)}) collective-permute-start(f32[1,128]{1,0:T(1,128)S(1)} %add.68), channel_id=1, source_target_pairs={{0,1},{1,0},{2,3},{3,2},{4,5},{5,4},{6,7},{7,6},{8,9},{9,8},{10,11... | collective-permute-start | bytes 1544 | tf_op jit(solution)/shard_map/ppermute | solution.py:425
  76.2 1.4 %collective-permute-start.22 = (f32[1,128]{1,0:T(1,128)S(1)}, f32[1,128]{1,0:T(1,128)S(1)}, u32[]{:S(2)}, u32[]{:S(2)}) collective-permute-start(f32[1,128]{1,0:T(1,128)S(1)} %add.68), channel_id=1, source_target_pairs={{0,5},{1,4},{2,7},{3,6},{4,1},{5,0},{6,3},{7,2},{8,13},{9,12},{10,... | collective-permute-start | bytes 1544 | tf_op jit(solution)/shard_map/ppermute | solution.py:426
  77.7 0.1 dynamic-slice_compare_fusion
  77.7 0.1 copy.9
  77.8 0.4 collective-permute-done.21
  78.3 2.4 %collective-permute-done.22 = f32[1,128]{1,0:T(1,128)S(1)} collective-permute-done((f32[1,128]{1,0:T(1,128)S(1)}, f32[1,128]{1,0:T(1,128)S(1)}, u32[]{:S(2)}, u32[]{:S(2)}) %collective-permute-start.22) | collective-permute-done | bytes 544 | tf_op jit(solution)/shard_map/ppermute | solution.py:426
  80.7 0.1 log_bitcast_fusion
  80.8 0.1 broadcast_in_dim.14
  80.9 0.8 subtract_select_fusion
  (32 shorter events, 0.4 us)
Async XLA Ops:
  0.0 0.9 %copy-start = (bf16[128,1024]{1,0:T(8,128)(2,1)S(1)}, bf16[128,1024]{1,0:T(8,128)(2,1)}, u32[]{:S(2)}) copy-start(bf16[128,1024]{1,0:T(8,128)(2,1)} %post_ref.4) | copy-start | bytes 786436
  4.8 8.6 %copy-start.3 = (s32[256,8]{0,1:T(8,128)S(1)}, s32[256,8]{0,1:T(8,128)}, u32[]{:S(2)}) copy-start(s32[256,8]{0,1:T(8,128)} %param.13) | copy-start | bytes 24580
  4.8 8.8 %copy-start.1 = (s32[128,8]{0,1:T(8,128)S(1)}, s32[128,8]{0,1:T(8,128)}, u32[]{:S(2)}) copy-start(s32[128,8]{0,1:T(8,128)} %param.15) | copy-start | bytes 12292
  4.8 8.8 %copy-start.2 = (s32[128]{0:T(128)S(1)}, s32[128]{0:T(128)}, u32[]{:S(2)}) copy-start(s32[128]{0:T(128)} %param.12) | copy-start | bytes 1540
  4.9 3.1 %collective-permute-start = (bf16[8,128,512]{2,1,0:T(8,128)(2,1)S(1)}, bf16[8,128,512]{2,1,0:T(8,128)(2,1)S(1)}, u32[]{:S(2)}, u32[]{:S(2)}) collective-permute-start(bf16[8,128,512]{2,1,0:T(8,128)(2,1)S(1)} %prior_half.4), channel_id=1, source_target_pairs={{0,2},{2,0},{4,6},{6,4},{8,10},{10,8},{12,14},{14,12},{16,18},{18,... | collective-permute-start | bytes 3145736 | tf_op jit(solution)/shard_map/ppermute | solution.py:348
  8.1 9.8 %collective-permute-start.1 = (bf16[2,128,512]{2,1,0:T(8,128)(2,1)S(1)}, bf16[2,128,512]{2,1,0:T(8,128)(2,1)S(1)}, u32[]{:S(2)}, u32[]{:S(2)}) collective-permute-start(bf16[2,128,512]{2,1,0:T(8,128)(2,1)S(1)} %get-tuple-element.44), channel_id=1, source_target_pairs={{0,4},{2,6},{4,0},{6,2},{8,12},{10,14},{12,8},{14,10},{16,20},{18,... | collective-permute-start | bytes 786440 | tf_op jit(solution)/shard_map/ppermute | solution.py:348
  13.6 9.7 %collective-permute-start.2 = (bf16[2,128,512]{2,1,0:T(8,128)(2,1)S(1)}, bf16[2,128,512]{2,1,0:T(8,128)(2,1)S(1)}, u32[]{:S(2)}, u32[]{:S(2)}) collective-permute-start(bf16[2,128,512]{2,1,0:T(8,128)(2,1)S(1)} %get-tuple-element.57), channel_id=1, source_target_pairs={{0,4},{2,6},{4,0},{6,2},{8,12},{10,14},{12,8},{14,10},{16,20},{18,... | collective-permute-start | bytes 786440 | tf_op jit(solution)/shard_map/ppermute | solution.py:348
  18.0 14.8 %collective-permute-start.3 = (bf16[128,512]{1,0:T(8,128)(2,1)S(1)}, bf16[128,512]{1,0:T(8,128)(2,1)S(1)}, u32[]{:S(2)}, u32[]{:S(2)}) collective-permute-start(bf16[128,512]{1,0:T(8,128)(2,1)S(1)} %get-tuple-element.88), channel_id=1, source_target_pairs={{0,16},{2,18},{4,20},{6,22},{8,24},{10,26},{12,28},{14,30},{16,0},... | collective-permute-start | bytes 393224 | tf_op jit(solution)/shard_map/ppermute | solution.py:348
  21.1 11.7 %collective-permute-start.4 = (bf16[128,512]{1,0:T(8,128)(2,1)S(1)}, bf16[128,512]{1,0:T(8,128)(2,1)S(1)}, u32[]{:S(2)}, u32[]{:S(2)}) collective-permute-start(bf16[128,512]{1,0:T(8,128)(2,1)S(1)} %get-tuple-element.87), channel_id=1, source_target_pairs={{0,24},{2,26},{4,28},{6,30},{8,16},{10,18},{12,20},{14,22},{16,8},... | collective-permute-start | bytes 393224 | tf_op jit(solution)/shard_map/ppermute | solution.py:348
  23.3 9.5 %collective-permute-start.5 = (bf16[128,512]{1,0:T(8,128)(2,1)S(1)}, bf16[128,512]{1,0:T(8,128)(2,1)S(1)}, u32[]{:S(2)}, u32[]{:S(2)}) collective-permute-start(bf16[128,512]{1,0:T(8,128)(2,1)S(1)} %fusion.4), channel_id=1, source_target_pairs={{0,8},{2,10},{4,12},{6,14},{8,0},{10,2},{12,4},{14,6},{16,24},{18,... | collective-permute-start | bytes 393224 | tf_op jit(solution)/shard_map/ppermute | solution.py:348
  32.9 12.6 %collective-permute-start.8 = (bf16[128,512]{1,0:T(8,128)(2,1)S(1)}, bf16[128,512]{1,0:T(8,128)(2,1)S(1)}, u32[]{:S(2)}, u32[]{:S(2)}) collective-permute-start(bf16[128,512]{1,0:T(8,128)(2,1)S(1)} %fusion.3), channel_id=1, source_target_pairs={{0,16},{2,18},{4,20},{6,22},{8,24},{10,26},{12,28},{14,30},{16,0},... | collective-permute-start | bytes 393224 | tf_op jit(solution)/shard_map/ppermute | solution.py:348
  35.5 9.9 %collective-permute-start.9 = (bf16[128,512]{1,0:T(8,128)(2,1)S(1)}, bf16[128,512]{1,0:T(8,128)(2,1)S(1)}, u32[]{:S(2)}, u32[]{:S(2)}) collective-permute-start(bf16[128,512]{1,0:T(8,128)(2,1)S(1)} %fusion.3), channel_id=1, source_target_pairs={{0,24},{2,26},{4,28},{6,30},{8,16},{10,18},{12,20},{14,22},{16,8},... | collective-permute-start | bytes 393224 | tf_op jit(solution)/shard_map/ppermute | solution.py:348
  36.1 9.5 %collective-permute-start.6 = (bf16[128,512]{1,0:T(8,128)(2,1)S(1)}, bf16[128,512]{1,0:T(8,128)(2,1)S(1)}, u32[]{:S(2)}, u32[]{:S(2)}) collective-permute-start(bf16[128,512]{1,0:T(8,128)(2,1)S(1)} %fusion.3), channel_id=1, source_target_pairs={{0,4},{2,6},{4,0},{6,2},{8,12},{10,14},{12,8},{14,10},{16,20},{18,... | collective-permute-start | bytes 393224 | tf_op jit(solution)/shard_map/ppermute | solution.py:348
  45.5 4.6 %collective-permute-start.12 = (bf16[2,128,512]{2,1,0:T(8,128)(2,1)S(1)}, bf16[2,128,512]{2,1,0:T(8,128)(2,1)S(1)}, u32[]{:S(2)}, u32[]{:S(2)}) collective-permute-start(bf16[2,128,512]{2,1,0:T(8,128)(2,1)S(1)} %pad_maximum_fusion.1.refs_2_), channel_id=1, source_target_pairs={{0,2},{2,0},{4,6},{6,4},{8,10},{10,8},{12,14},{14,12},{16,18},{18,... | collective-permute-start | bytes 786440 | tf_op jit(solution)/shard_map/ppermute | solution.py:348
  45.6 4.5 %collective-permute-start.11 = (bf16[2,128,512]{2,1,0:T(8,128)(2,1)S(1)}, bf16[2,128,512]{2,1,0:T(8,128)(2,1)S(1)}, u32[]{:S(2)}, u32[]{:S(2)}) collective-permute-start(bf16[2,128,512]{2,1,0:T(8,128)(2,1)S(1)} %pad_maximum_fusion.refs_0_), channel_id=1, source_target_pairs={{0,2},{2,0},{4,6},{6,4},{8,10},{10,8},{12,14},{14,12},{16,18},{18,... | collective-permute-start | bytes 786440 | tf_op jit(solution)/shard_map/ppermute | solution.py:348
  46.2 8.3 %collective-permute-start.10 = (bf16[2,128,512]{2,1,0:T(8,128)(2,1)S(1)}, bf16[2,128,512]{2,1,0:T(8,128)(2,1)S(1)}, u32[]{:S(2)}, u32[]{:S(2)}) collective-permute-start(bf16[2,128,512]{2,1,0:T(8,128)(2,1)S(1)} %pad_maximum_fusion.1.refs_2_), channel_id=1, source_target_pairs={{0,4},{2,6},{4,0},{6,2},{8,12},{10,14},{12,8},{14,10},{16,20},{18,... | collective-permute-start | bytes 786440 | tf_op jit(solution)/shard_map/ppermute | solution.py:348
  47.7 8.8 %collective-permute-start.7 = (bf16[2,128,512]{2,1,0:T(8,128)(2,1)S(1)}, bf16[2,128,512]{2,1,0:T(8,128)(2,1)S(1)}, u32[]{:S(2)}, u32[]{:S(2)}) collective-permute-start(bf16[2,128,512]{2,1,0:T(8,128)(2,1)S(1)} %pad_maximum_fusion.refs_0_), channel_id=1, source_target_pairs={{0,8},{2,10},{4,12},{6,14},{8,0},{10,2},{12,4},{14,6},{16,24},{18,... | collective-permute-start | bytes 786440 | tf_op jit(solution)/shard_map/ppermute | solution.py:348
  56.4 1.5 %collective-permute-start.13 = (bf16[2,128,512]{2,1,0:T(8,128)(2,1)S(1)}, bf16[2,128,512]{2,1,0:T(8,128)(2,1)S(1)}, u32[]{:S(2)}, u32[]{:S(2)}) collective-permute-start(bf16[2,128,512]{2,1,0:T(8,128)(2,1)S(1)} %collective-permute-done.7.refs_0_), channel_id=1, source_target_pairs={{0,2},{2,0},{4,6},{6,4},{8,10},{10,8},{12,14},{14,12},{16,18},{18,... | collective-permute-start | bytes 786440 | tf_op jit(solution)/shard_map/ppermute | solution.py:348
  56.4 1.9 %collective-permute-start.14 = (bf16[2,128,512]{2,1,0:T(8,128)(2,1)S(1)}, bf16[2,128,512]{2,1,0:T(8,128)(2,1)S(1)}, u32[]{:S(2)}, u32[]{:S(2)}) collective-permute-start(bf16[2,128,512]{2,1,0:T(8,128)(2,1)S(1)} %collective-permute-done.10.refs_2_), channel_id=1, source_target_pairs={{0,2},{2,0},{4,6},{6,4},{8,10},{10,8},{12,14},{14,12},{16,18},{18,... | collective-permute-start | bytes 786440 | tf_op jit(solution)/shard_map/ppermute | solution.py:348
  63.9 5.9 %collective-permute-start.15 = (f32[1,128]{1,0:T(1,128)S(1)}, f32[1,128]{1,0:T(1,128)S(1)}, u32[]{:S(2)}, u32[]{:S(2)}) collective-permute-start(f32[1,128]{1,0:T(1,128)S(1)} %get-tuple-element.79), channel_id=1, source_target_pairs={{0,16},{2,18},{4,20},{6,22},{8,24},{10,26},{12,28},{14,30},{16,0},... | collective-permute-start | bytes 1544 | tf_op jit(solution)/shard_map/ppermute | solution.py:348
  67.6 5.3 %collective-permute-start.16 = (f32[1,128]{1,0:T(1,128)S(1)}, f32[1,128]{1,0:T(1,128)S(1)}, u32[]{:S(2)}, u32[]{:S(2)}) collective-permute-start(f32[1,128]{1,0:T(1,128)S(1)} %get-tuple-element.79), channel_id=1, source_target_pairs={{0,24},{2,26},{4,28},{6,30},{8,16},{10,18},{12,20},{14,22},{16,8},... | collective-permute-start | bytes 1544 | tf_op jit(solution)/shard_map/ppermute | solution.py:348
  68.1 4.9 %collective-permute-start.17 = (f32[1,128]{1,0:T(1,128)S(1)}, f32[1,128]{1,0:T(1,128)S(1)}, u32[]{:S(2)}, u32[]{:S(2)}) collective-permute-start(f32[1,128]{1,0:T(1,128)S(1)} %get-tuple-element.79), channel_id=1, source_target_pairs={{0,8},{2,10},{4,12},{6,14},{8,0},{10,2},{12,4},{14,6},{16,24},{18,... | collective-permute-start | bytes 1544 | tf_op jit(solution)/shard_map/ppermute | solution.py:348
  68.3 5.9 %collective-permute-start.19 = (bf16[64,1024]{1,0:T(8,128)(2,1)S(1)}, bf16[64,1024]{1,0:T(8,128)(2,1)S(1)}, u32[]{:S(2)}, u32[]{:S(2)}) collective-permute-start(bf16[64,1024]{1,0:T(8,128)(2,1)S(1)} %get-tuple-element.80), channel_id=1, source_target_pairs={{0,1},{1,0},{2,3},{3,2},{4,5},{5,4},{6,7},{7,6},{8,9},{9,8},{10,11... | collective-permute-start | bytes 393224 | tf_op jit(solution)/shard_map/ppermute | solution.py:419
  73.0 1.2 %collective-permute-start.18 = (f32[1,128]{1,0:T(1,128)S(1)}, f32[1,128]{1,0:T(1,128)S(1)}, u32[]{:S(2)}, u32[]{:S(2)}) collective-permute-start(f32[1,128]{1,0:T(1,128)S(1)} %add_add_fusion.1), channel_id=1, source_target_pairs={{0,2},{2,0},{4,6},{6,4},{8,10},{10,8},{12,14},{14,12},{16,18},{18,... | collective-permute-start | bytes 1544 | tf_op jit(solution)/shard_map/ppermute | solution.py:348
  74.2 3.7 %collective-permute-start.20 = (f32[1,128]{1,0:T(1,128)S(1)}, f32[1,128]{1,0:T(1,128)S(1)}, u32[]{:S(2)}, u32[]{:S(2)}) collective-permute-start(f32[1,128]{1,0:T(1,128)S(1)} %add.68), channel_id=1, source_target_pairs={{0,4},{2,6},{4,0},{6,2},{8,12},{10,14},{12,8},{14,10},{16,20},{18,... | collective-permute-start | bytes 1544 | tf_op jit(solution)/shard_map/ppermute | solution.py:348
  74.7 3.5 %collective-permute-start.21 = (f32[1,128]{1,0:T(1,128)S(1)}, f32[1,128]{1,0:T(1,128)S(1)}, u32[]{:S(2)}, u32[]{:S(2)}) collective-permute-start(f32[1,128]{1,0:T(1,128)S(1)} %add.68), channel_id=1, source_target_pairs={{0,1},{1,0},{2,3},{3,2},{4,5},{5,4},{6,7},{7,6},{8,9},{9,8},{10,11... | collective-permute-start | bytes 1544 | tf_op jit(solution)/shard_map/ppermute | solution.py:425
  76.2 4.4 %collective-permute-start.22 = (f32[1,128]{1,0:T(1,128)S(1)}, f32[1,128]{1,0:T(1,128)S(1)}, u32[]{:S(2)}, u32[]{:S(2)}) collective-permute-start(f32[1,128]{1,0:T(1,128)S(1)} %add.68), channel_id=1, source_target_pairs={{0,5},{1,4},{2,7},{3,6},{4,1},{5,0},{6,3},{7,2},{8,13},{9,12},{10,... | collective-permute-start | bytes 1544 | tf_op jit(solution)/shard_map/ppermute | solution.py:426

commit v5 on v4

--- a/solution.py
+++ b/solution.py
@@ -130,26 +130,35 @@
             jax.ShapeDtypeStruct((seats, slots), jnp.int32),
             jax.ShapeDtypeStruct((rows, columns), BF16),
         ],
-        compiler_params=params(16),
+        compiler_params=params(12),
         cost_estimate=cheap(),
         name="take_seats",
     )(allowed, state, edge_next, token_edge)
 
 
-def successor_rows(head, after, advance):
+def successor_rows(head, after, advance, emission):
     seats, slots = after.shape
     states, hidden = advance.shape
     width = min(1024, hidden)
     steps = hidden // width
     full = BATCH * UNIT
-
-    def kernel(head_ref, after_ref, adv_hbm, first_ref, rest_ref, adv_ref, hot, held, left, came):
+    deep = emission.shape[0] // 8
+
+    def kernel(
+        head_ref, after_ref, adv_hbm, emit_hbm, first_ref, rest_ref, emit_ref, adv_ref, hot, held, left, came, staged
+    ):
+        def stage(n):
+            span = pl.ds(n * deep, deep)
+            return pltpu.make_async_copy(emit_hbm.at[span, :], emit_ref.at[span, :], staged.at[n])
+
         def inward(n):
             span = pl.ds(n * width, width)
             return pltpu.make_async_copy(adv_hbm.at[:, span], adv_ref.at[:, span], came.at[n])
 
         for n in range(steps):
             inward(n).start()
+        for n in range(8):
+            stage(n).start()
         names = lax.broadcasted_iota(jnp.int32, (GROUP, states), 1)
 
         def mark(c):
@@ -181,47 +190,30 @@
                 copy(c, n).start()
                 copy(c, n).wait()
 
+        for n in range(8):
+            stage(n).wait()
+
     return pl.pallas_call(
         kernel,
-        in_specs=[SMEM, VMEM, HBM],
-        out_specs=[VMEM, HBM],
+        in_specs=[SMEM, VMEM, HBM, HBM],
+        out_specs=[VMEM, HBM, VMEM],
         scratch_shapes=[
             pltpu.VMEM((states, hidden), BF16),
             pltpu.VMEM((full, states), BF16),
             pltpu.VMEM((full, width), BF16),
             pltpu.SemaphoreType.DMA,
             pltpu.SemaphoreType.DMA((steps,)),
+            pltpu.SemaphoreType.DMA((8,)),
         ],
-        out_shape=[pltpu.VMEM((full, hidden), BF16), jax.ShapeDtypeStruct((seats * slots, hidden), BF16)],
-        compiler_params=params(16),
+        out_shape=[
+            pltpu.VMEM((full, hidden), BF16),
+            jax.ShapeDtypeStruct((seats * slots, hidden), BF16),
+            pltpu.VMEM(emission.shape, BF16),
+        ],
+        compiler_params=params(12),
         cost_estimate=cheap(),
         name="successor_rows",
-    )(head, after, advance)
-
-
-def stage(emission):
-    deep = emission.shape[0] // 8
-
-    def kernel(hbm, out_ref, came):
-        copies = []
-        for n in range(8):
-            span = pl.ds(n * deep, deep)
-            copies.append(pltpu.make_async_copy(hbm.at[span, :], out_ref.at[span, :], came.at[n]))
-        for copy in copies:
-            copy.start()
-        for copy in copies:
-            copy.wait()
-
-    return pl.pallas_call(
-        kernel,
-        in_specs=[HBM],
-        out_specs=VMEM,
-        out_shape=pltpu.VMEM(emission.shape, BF16),
-        scratch_shapes=[pltpu.SemaphoreType.DMA((8,))],
-        compiler_params=params(16),
-        cost_estimate=cheap(),
-        name="stage",
-    )(emission)
+    )(head, after, advance, emission)
 
 
 def piece_scores(arrays, places, head, select, look, emission, edges, before, slots, tile, last, local):
@@ -325,7 +317,7 @@
             pltpu.SemaphoreType.DMA((count, BATCH)),
         ],
         out_shape=[jax.ShapeDtypeStruct(*shape) for shape in shapes],
-        compiler_params=params(16),
+        compiler_params=params(12),
         cost_estimate=cheap(),
         name="piece_scores",
     )(head, *arrays, select, *look, emission, edges, *([before] if started else []))
@@ -369,27 +361,23 @@
         sent = [swap(far[0].astype(BF16), 8), swap(far[1].astype(BF16), 12)]
         near = parts[3].astype(F32) + near.astype(F32)
         sent.append(swap(near[1].astype(BF16), 4))
-        look = successor_rows(head, after, in_hbm(advance))
-        sent, look = lax.optimization_barrier((sent, look))
         own = near[0] + sent[0].astype(F32) + sent[1].astype(F32) + sent[2].astype(F32)
         own = own.astype(BF16)
 
-        own, emission = lax.optimization_barrier((own, emission))
+        own, head = lax.optimization_barrier((own, head))
         far = [swap(own, 8), swap(own, 12)]
-        far, emission = lax.optimization_barrier((far, stage(in_hbm(emission))))
+        *look, emission = successor_rows(head, after, in_hbm(advance), in_hbm(emission))
+        far, column, emission = lax.optimization_barrier((far, swap(own, 4), emission))
         far = jnp.stack(far)
-        near = jnp.stack([own, swap(own, 2)])
-        batches = [((near, far), (0, 1, 4, 6)), ((swap(near, 4), swap(far, 2)), (2, 3, 5, 7))]
+        beside = swap(own, 2)
+        near = jnp.stack([own, beside])
 
         def one_batch(arrays, bits, before, last):
             def places():
-                groups = (bits[:2], bits[2:])
+                groups = [bits[n : n + 2] for n in range(0, len(bits), 2)]
                 return [piece_place(chips, other, b) for group in groups for other in (False, True) for b in group]
 
-            first, second = arrays
-            if before is not None:
-                first, second, before = lax.optimization_barrier((first, second, before))
-            arrays = [first, swap(first, 1), second, swap(second, 1)]
+            arrays = [one for array in arrays for one in (array, swap(array, 1))]
             return piece_scores(
                 arrays, places, head, select, look, emission, edges, before, slots, tile, last, local
             )
@@ -400,19 +388,23 @@
         ).astype(BF16)
         prior = lax.all_gather(own, "vocab", axis=0, tiled=True)
         head, select, after, edges = seated(*small)
-        look = successor_rows(head, after, in_hbm(advance))
+        *look, emission = successor_rows(head, after, in_hbm(advance), in_hbm(emission))
         wide = min(512, hidden)
-        batches = [(prior[None, :, wide * j : wide * (j + 1)], j) for j in range(hidden // wide)]
 
         def one_batch(array, j, before, last):
             return piece_scores(
                 [array], lambda: [j], head, select, look, emission, edges, before, slots, tile, last, rows
             )
 
-    chosen = None
-    for n, (array, where) in enumerate(batches):
-        got = one_batch(array, where, chosen, n == len(batches) - 1)
-        chosen = got[0]
+    if direct:
+        chosen = one_batch([near, far], (0, 1, 4, 6), None, False)[0]
+        across, diagonal, chosen = lax.optimization_barrier((swap(far, 2), swap(beside, 4), chosen))
+        got = one_batch([across, jnp.stack([column, diagonal])], (5, 7, 2, 3), chosen, True)
+    else:
+        chosen = None
+        for j in range(hidden // wide):
+            got = one_batch(prior[None, :, wide * j : wide * (j + 1)], j, chosen, j == hidden // wide - 1)
+            chosen = got[0]
     mine, theirs, part = got
 
     if hid_size == 2:
@@ -420,10 +412,10 @@
         if direct:
             part = part + swap(part, 8) + swap(part, 12) + swap(part, 4)
             part = part + swap(part, 1)
-            part, theirs = lax.optimization_barrier((part, theirs))
             across = [(i, i ^ 5) for i in range(2 * vocab_size)]
-            beside = lax.ppermute(part, "hid", [(0, 1), (1, 0)])
-            part = part + swap(part, 2) + beside + lax.ppermute(part, ("vocab", "hid"), across)
+            later = swap(part, 2) + lax.ppermute(part, ("vocab", "hid"), across)
+            again, theirs = lax.optimization_barrier((part, theirs))
+            part = part + lax.ppermute(again, "hid", [(0, 1), (1, 0)]) + later
         else:
             part = lax.psum(part, ("vocab", "hid"))
         totals = lax.dynamic_slice_in_dim(part[0], first, local, 0)

time: 81.9 us -> 80.8 us (0.987)
  Pallas kernels: 34.1 us -> 28.6 us
  waiting for transfers between devices: 15.5 us -> 19 us
  starting transfers between devices: 28.9 us -> 29.9 us
    pallas_call x2 -> x1, Pallas kernels: 13.4 us -> 7.95 us  [successor_rows(): pl.pallas_call(kernel, in_specs=[SMEM, VMEM, HBM, HBM], out_specs=[VMEM,...]
    ppermute x20 -> x21, waiting for transfers between devices: 12.7 us -> 16.1 us  [swap(): lax.ppermute(array, 'vocab', [(i, i ^ bits) for i in range(vocab_size)])]
    ppermute x20 -> x21, starting transfers between devices: 24.5 us -> 26.4 us  [swap(): lax.ppermute(array, 'vocab', [(i, i ^ bits) for i in range(vocab_size)])]
    ppermute x2, starting transfers between devices: 2.94 us -> 1.97 us  [the longest x1 1.47 us: body(): later = swap(part, 2) + lax.ppermute(part, ('vocab', 'hid'), across)]
  transfers between devices with their start and end apart: 23 -> 24, of which waited for: 10 -> 11; matrix products, arithmetic and copies ran while one was open for 1% -> 1% of each run, Pallas kernels for 30% -> 24%
where the time goes in v5:
time: 80.8 us; the launch traced here: 80.6 us
  starting transfers between devices  29.9 us (37%)
  Pallas kernels  28.6 us (35%)
  waiting for transfers between devices  19 us (24%)
  other arithmetic  1.46 us (2%)
  local copies, waits for them, and re-layouts  1.45 us (2%)
    ppermute x21, starting transfers between devices, swap(): lax.ppermute(array, 'vocab', [(i, i ^ bits) for i in range(vocab_size)])  26.4 us
    ppermute x21, waiting for transfers between devices, swap(): lax.ppermute(array, 'vocab', [(i, i ^ bits) for i in range(vocab_size)])  16.1 us
    pallas_call x2, Pallas kernels, piece_scores(): pl.pallas_call(kernel, in_specs=[SMEM] + [VMEM] * len(arrays) + [VMEM, VM...  9.89 us
    pallas_call x3, Pallas kernels, half_product(): pl.pallas_call(kernel, in_specs=[VMEM, HBM], out_specs=VMEM, out_shape=ja...  8.95 us
    pallas_call x1, Pallas kernels, successor_rows(): pl.pallas_call(kernel, in_specs=[SMEM, VMEM, HBM, HBM], out_specs=[VMEM,...  7.95 us
    ppermute x1, waiting for transfers between devices, body(): later = swap(part, 2) + lax.ppermute(part, ('vocab', 'hid'), across)  2.28 us
    pallas_call x1, Pallas kernels, take_seats(): pl.pallas_call(kernel, in_specs=[VMEM] * 3 + [HBM], out_specs=[SMEM, VMEM...  1.83 us
  transfers between devices with their start and end apart: 24, of which 11 were waited for; matrix products, arithmetic and copies ran while one was open for 1% of the time, Pallas kernels for 24%

profile of v5, /device:TPU:0, one launch (start us, length us, event | category | flops | bytes accessed | tf_op | source)
XLA Modules:
  0.0 80.6 jit_solution(3661159537853228216)
XLA Ops:
  0.0 0.9 %copy-done = bf16[128,1024]{1,0:T(8,128)(2,1)S(1)} copy-done((bf16[128,1024]{1,0:T(8,128)(2,1)S(1)}, bf16[128,1024]{1,0:T(8,128)(2,1)}, u32[]{:S(2)}) %copy-start) | copy-done | bytes 262168
  1.0 3.9 %prior_half.4 = bf16[8,128,512]{2,1,0:T(8,128)(2,1)S(1)} custom-call(bf16[128,1024]{1,0:T(8,128)(2,1)S(1)} %copy-done, bf16[1024,8192]{1,0:T(8,128)(2,1)} %trans_ref.5), custom_call_target="tpu_custom_call" | custom-call | flops 1048576 | bytes 1048576 | tf_op jit(solution)/shard_map/prior_half/pallas_call | solution.py:62
  4.9 0.5 collective-permute-start
  5.4 2.5 %prior_half.3 = bf16[4,128,512]{2,1,0:T(8,128)(2,1)S(1)} custom-call(bf16[128,1024]{1,0:T(8,128)(2,1)S(1)} %copy-done, bf16[1024,8192]{1,0:T(8,128)(2,1)} %trans_ref.5), custom_call_target="tpu_custom_call" | custom-call | flops 1048576 | bytes 1048576 | tf_op jit(solution)/shard_map/prior_half/pallas_call | solution.py:62
  7.9 0.1 add_convert_fusion.3
  8.1 2.6 %collective-permute-start.2 = (bf16[2,128,512]{2,1,0:T(8,128)(2,1)S(1)}, bf16[2,128,512]{2,1,0:T(8,128)(2,1)S(1)}, u32[]{:S(2)}, u32[]{:S(2)}) collective-permute-start(bf16[2,128,512]{2,1,0:T(8,128)(2,1)S(1)} %get-tuple-element.41), channel_id=1, source_target_pairs={{0,4},{2,6},{4,0},{6,2},{8,12},{10,14},{12,8},{14,10},{16,20},{18,... | collective-permute-start | bytes 786440 | tf_op jit(solution)/shard_map/ppermute | solution.py:340
  10.7 2.5 %prior_half.5 = bf16[4,128,512]{2,1,0:T(8,128)(2,1)S(1)} custom-call(bf16[128,1024]{1,0:T(8,128)(2,1)S(1)} %copy-done, bf16[1024,8192]{1,0:T(8,128)(2,1)} %trans_ref.5), custom_call_target="tpu_custom_call" | custom-call | flops 1048576 | bytes 1048576 | tf_op jit(solution)/shard_map/prior_half/pallas_call | solution.py:62
  13.3 0.1 add_convert_fusion.1
  13.4 0.1 copy.10.next_ref
  13.6 0.1 collective-permute-start.1
  13.7 1.8 %take_seats.1 = (s32[17]{0:T(128)S(1)}, bf16[512,128]{1,0:T(8,128)(2,1)S(1)}, s32[512,8]{1,0:T(8,128)S(1)}, bf16[128,1024]{1,0:T(8,128)(2,1)S(1)}) custom-call(s32[8,128]{1,0:T(8,128)S(1)} %bitcast.29, s32[1,128]{1,0:T(1,128)S(1)} %bitcast.30, s32[256,8]{1,0:T(8,128)S(1)} %copy.10.next_ref, s32[256,1024]{1,0:T(8,128)} %token_hbm), custom_call_target="tpu_custom_call" | custom-call | flops 1048576 | bytes 1048576 | tf_op jit(solution)/shard_map/take_seats/pallas_call | solution.py:122
  15.5 2.4 %collective-permute-done.2 = bf16[2,128,512]{2,1,0:T(8,128)(2,1)S(1)} collective-permute-done((bf16[2,128,512]{2,1,0:T(8,128)(2,1)S(1)}, bf16[2,128,512]{2,1,0:T(8,128)(2,1)S(1)}, u32[]{:S(2)}, u32[]{:S(2)}) %collective-permute-start.2) | collective-permute-done | bytes 262176 | tf_op jit(solution)/shard_map/ppermute | solution.py:340
  18.0 3.1 %collective-permute-start.3 = (bf16[128,512]{1,0:T(8,128)(2,1)S(1)}, bf16[128,512]{1,0:T(8,128)(2,1)S(1)}, u32[]{:S(2)}, u32[]{:S(2)}) collective-permute-start(bf16[128,512]{1,0:T(8,128)(2,1)S(1)} %get-tuple-element.81), channel_id=1, source_target_pairs={{0,16},{2,18},{4,20},{6,22},{8,24},{10,26},{12,28},{14,30},{16,0},... | collective-permute-start | bytes 393224 | tf_op jit(solution)/shard_map/ppermute | solution.py:340
  21.1 1.4 %collective-permute-start.4 = (bf16[128,512]{1,0:T(8,128)(2,1)S(1)}, bf16[128,512]{1,0:T(8,128)(2,1)S(1)}, u32[]{:S(2)}, u32[]{:S(2)}) collective-permute-start(bf16[128,512]{1,0:T(8,128)(2,1)S(1)} %get-tuple-element.82), channel_id=1, source_target_pairs={{0,24},{2,26},{4,28},{6,30},{8,16},{10,18},{12,20},{14,22},{16,8},... | collective-permute-start | bytes 393224 | tf_op jit(solution)/shard_map/ppermute | solution.py:340
  22.5 0.8 collective-permute-done.1
  23.3 1.9 %collective-permute-start.5 = (bf16[128,512]{1,0:T(8,128)(2,1)S(1)}, bf16[128,512]{1,0:T(8,128)(2,1)S(1)}, u32[]{:S(2)}, u32[]{:S(2)}) collective-permute-start(bf16[128,512]{1,0:T(8,128)(2,1)S(1)} %fusion.4), channel_id=1, source_target_pairs={{0,8},{2,10},{4,12},{6,14},{8,0},{10,2},{12,4},{14,6},{16,24},{18,... | collective-permute-start | bytes 393224 | tf_op jit(solution)/shard_map/ppermute | solution.py:340
  25.2 5.6 %collective-permute-done.3 = bf16[128,512]{1,0:T(8,128)(2,1)S(1)} collective-permute-done((bf16[128,512]{1,0:T(8,128)(2,1)S(1)}, bf16[128,512]{1,0:T(8,128)(2,1)S(1)}, u32[]{:S(2)}, u32[]{:S(2)}) %collective-permute-start.3) | collective-permute-done | bytes 131104 | tf_op jit(solution)/shard_map/ppermute | solution.py:340
  30.8 1.2 %collective-permute-done.5 = bf16[128,512]{1,0:T(8,128)(2,1)S(1)} collective-permute-done((bf16[128,512]{1,0:T(8,128)(2,1)S(1)}, bf16[128,512]{1,0:T(8,128)(2,1)S(1)}, u32[]{:S(2)}, u32[]{:S(2)}) %collective-permute-start.5) | collective-permute-done | bytes 131104 | tf_op jit(solution)/shard_map/ppermute | solution.py:340
  32.1 3.1 %collective-permute-start.6 = (bf16[128,512]{1,0:T(8,128)(2,1)S(1)}, bf16[128,512]{1,0:T(8,128)(2,1)S(1)}, u32[]{:S(2)}, u32[]{:S(2)}) collective-permute-start(bf16[128,512]{1,0:T(8,128)(2,1)S(1)} %fusion.3), channel_id=1, source_target_pairs={{0,16},{2,18},{4,20},{6,22},{8,24},{10,26},{12,28},{14,30},{16,0},... | collective-permute-start | bytes 393224 | tf_op jit(solution)/shard_map/ppermute | solution.py:340
  35.2 0.9 %collective-permute-start.7 = (bf16[128,512]{1,0:T(8,128)(2,1)S(1)}, bf16[128,512]{1,0:T(8,128)(2,1)S(1)}, u32[]{:S(2)}, u32[]{:S(2)}) collective-permute-start(bf16[128,512]{1,0:T(8,128)(2,1)S(1)} %fusion.3), channel_id=1, source_target_pairs={{0,24},{2,26},{4,28},{6,30},{8,16},{10,18},{12,20},{14,22},{16,8},... | collective-permute-start | bytes 393224 | tf_op jit(solution)/shard_map/ppermute | solution.py:340
  36.1 0.5 collective-permute-start.8
  36.6 1.5 %collective-permute-start.10 = (bf16[128,512]{1,0:T(8,128)(2,1)S(1)}, bf16[128,512]{1,0:T(8,128)(2,1)S(1)}, u32[]{:S(2)}, u32[]{:S(2)}) collective-permute-start(bf16[128,512]{1,0:T(8,128)(2,1)S(1)} %fusion.3), channel_id=1, source_target_pairs={{0,4},{2,6},{4,0},{6,2},{8,12},{10,14},{12,8},{14,10},{16,20},{18,... | collective-permute-start | bytes 393224 | tf_op jit(solution)/shard_map/ppermute | solution.py:340
  38.1 7.9 %successor_rows.1 = (bf16[1024,8192]{1,0:T(8,128)(2,1)S(1)}, bf16[4096,8192]{1,0:T(8,128)(2,1)}, bf16[8192,1024]{1,0:T(8,128)(2,1)S(1)}) custom-call(s32[17]{0:T(128)S(1)} %get-tuple-element.57.head_ref, s32[512,8]{1,0:T(8,128)S(1)} %get-tuple-element.59.after_ref, bf16[256,8192]{1,0:T(8,128)(2,1)} %adv_hbm.1, bf16[8192,1024]{1,0:T(8,128)(2,1)} %emit_hbm.1), custom_call_target="tpu_custom_call" | custom-call | flops 1048576 | bytes 1048576 | tf_op jit(solution)/shard_map/successor_rows/pallas_call | solution.py:196
  46.2 0.5 collective-permute-start.12
  46.8 1.3 %collective-permute-start.9 = (bf16[2,128,512]{2,1,0:T(8,128)(2,1)S(1)}, bf16[2,128,512]{2,1,0:T(8,128)(2,1)S(1)}, u32[]{:S(2)}, u32[]{:S(2)}) collective-permute-start(bf16[2,128,512]{2,1,0:T(8,128)(2,1)S(1)} %pad_maximum_fusion.refs_2_), channel_id=1, source_target_pairs={{0,4},{2,6},{4,0},{6,2},{8,12},{10,14},{12,8},{14,10},{16,20},{18,... | collective-permute-start | bytes 786440 | tf_op jit(solution)/shard_map/ppermute | solution.py:340
  48.1 2.1 %collective-permute-start.11 = (bf16[128,512]{1,0:T(8,128)(2,1)S(1)}, bf16[128,512]{1,0:T(8,128)(2,1)S(1)}, u32[]{:S(2)}, u32[]{:S(2)}) collective-permute-start(bf16[128,512]{1,0:T(8,128)(2,1)S(1)} %collective-permute-done.10), channel_id=1, source_target_pairs={{0,8},{2,10},{4,12},{6,14},{8,0},{10,2},{12,4},{14,6},{16,24},{18,... | collective-permute-start | bytes 393224 | tf_op jit(solution)/shard_map/ppermute | solution.py:340
  50.2 4.4 %piece_scores.2.refs_9_ = f32[512,256]{1,0:T(8,128)S(1)} custom-call(s32[17]{0:T(128)S(1)} %get-tuple-element.57.head_ref, bf16[2,128,512]{2,1,0:T(8,128)(2,1)S(1)} %pad_maximum_fusion.1.refs_0_, bf16[2,128,512]{2,1,0:T(8,128)(2,1)S(1)} %collective-permute-done.12.refs_1_, bf16[2,128,512]{2,1,0:T(8,128)(2,1)S(1)} %pad_maximum_fusion.refs_2_, ...), custom_call_target="tpu_custom_call" | custom-call | flops 1048576 | bytes 1048576 | tf_op jit(solution)/shard_map/piece_scores/pallas_call | solution.py:309
  54.6 0.5 collective-permute-done.9.refs_0_
  55.2 0.5 collective-permute-start.14
  55.7 1.0 %collective-permute-done.15.refs_3_ = bf16[2,128,512]{2,1,0:T(8,128)(2,1)S(1)} collective-permute-done((bf16[2,128,512]{2,1,0:T(8,128)(2,1)S(1)}, bf16[2,128,512]{2,1,0:T(8,128)(2,1)S(1)}, u32[]{:S(2)}, u32[]{:S(2)}) %collective-permute-start.15) | collective-permute-done | bytes 262176 | tf_op jit(solution)/shard_map/ppermute | solution.py:340
  56.7 0.4 collective-permute-done.14.refs_1_
  57.1 5.5 %piece_scores.3 = (f32[64,1024]{1,0:T(8,128)S(1)}, bf16[64,1024]{1,0:T(8,128)(2,1)S(1)}, f32[1,128]{1,0:T(1,128)S(1)}) custom-call(s32[17]{0:T(128)S(1)} %get-tuple-element.57.head_ref, bf16[2,128,512]{2,1,0:T(8,128)(2,1)S(1)} %collective-permute-done.9.refs_0_, bf16[2,128,512]{2,1,0:T(8,128)(2,1)S(1)} %collective-permute-done.14.refs_1_, ...), custom_call_target="tpu_custom_call" | custom-call | flops 1048576 | bytes 1048576 | tf_op jit(solution)/shard_map/piece_scores/pallas_call | solution.py:309
  62.6 3.9 %collective-permute-start.16 = (f32[1,128]{1,0:T(1,128)S(1)}, f32[1,128]{1,0:T(1,128)S(1)}, u32[]{:S(2)}, u32[]{:S(2)}) collective-permute-start(f32[1,128]{1,0:T(1,128)S(1)} %get-tuple-element.73), channel_id=1, source_target_pairs={{0,16},{2,18},{4,20},{6,22},{8,24},{10,26},{12,28},{14,30},{16,0},... | collective-permute-start | bytes 1544 | tf_op jit(solution)/shard_map/ppermute | solution.py:340
  66.5 0.4 collective-permute-start.17
  67.0 0.2 collective-permute-start.18
  67.2 1.5 %collective-permute-start.20 = (bf16[64,1024]{1,0:T(8,128)(2,1)S(1)}, bf16[64,1024]{1,0:T(8,128)(2,1)S(1)}, u32[]{:S(2)}, u32[]{:S(2)}) collective-permute-start(bf16[64,1024]{1,0:T(8,128)(2,1)S(1)} %get-tuple-element.74), channel_id=1, source_target_pairs={{0,1},{1,0},{2,3},{3,2},{4,5},{5,4},{6,7},{7,6},{8,9},{9,8},{10,11... | collective-permute-start | bytes 393224 | tf_op jit(solution)/shard_map/ppermute | solution.py:411
  68.7 3.2 %collective-permute-done.17 = f32[1,128]{1,0:T(1,128)S(1)} collective-permute-done((f32[1,128]{1,0:T(1,128)S(1)}, f32[1,128]{1,0:T(1,128)S(1)}, u32[]{:S(2)}, u32[]{:S(2)}) %collective-permute-start.17) | collective-permute-done | bytes 544 | tf_op jit(solution)/shard_map/ppermute | solution.py:340
  72.0 1.1 %collective-permute-done.19 = f32[1,128]{1,0:T(1,128)S(1)} collective-permute-done((f32[1,128]{1,0:T(1,128)S(1)}, f32[1,128]{1,0:T(1,128)S(1)}, u32[]{:S(2)}, u32[]{:S(2)}) %collective-permute-start.19) | collective-permute-done | bytes 544 | tf_op jit(solution)/shard_map/ppermute | solution.py:340
  73.1 1.5 %collective-permute-start.22 = (f32[1,128]{1,0:T(1,128)S(1)}, f32[1,128]{1,0:T(1,128)S(1)}, u32[]{:S(2)}, u32[]{:S(2)}) collective-permute-start(f32[1,128]{1,0:T(1,128)S(1)} %add.68), channel_id=1, source_target_pairs={{0,4},{2,6},{4,0},{6,2},{8,12},{10,14},{12,8},{14,10},{16,20},{18,... | collective-permute-start | bytes 1544 | tf_op jit(solution)/shard_map/ppermute | solution.py:340
  74.6 1.5 %collective-permute-start.23 = (f32[1,128]{1,0:T(1,128)S(1)}, f32[1,128]{1,0:T(1,128)S(1)}, u32[]{:S(2)}, u32[]{:S(2)}) collective-permute-start(f32[1,128]{1,0:T(1,128)S(1)} %add.68), channel_id=1, source_target_pairs={{0,5},{1,4},{2,7},{3,6},{4,1},{5,0},{6,3},{7,2},{8,13},{9,12},{10,... | collective-permute-start | bytes 1544 | tf_op jit(solution)/shard_map/ppermute | solution.py:416
  76.1 0.5 collective-permute-start.21
  76.6 0.1 dynamic-slice_compare_fusion
  76.6 0.1 copy.9
  76.8 2.3 %collective-permute-done.23 = f32[1,128]{1,0:T(1,128)S(1)} collective-permute-done((f32[1,128]{1,0:T(1,128)S(1)}, f32[1,128]{1,0:T(1,128)S(1)}, u32[]{:S(2)}, u32[]{:S(2)}) %collective-permute-start.23) | collective-permute-done | bytes 544 | tf_op jit(solution)/shard_map/ppermute | solution.py:416
  79.0 0.6 collective-permute-done.21
  79.6 0.1 log_bitcast_fusion
  79.7 0.1 broadcast_in_dim.14
  79.8 0.8 subtract_select_fusion
  (34 shorter events, 0.6 us)
Async XLA Ops:
  0.0 0.9 %copy-start = (bf16[128,1024]{1,0:T(8,128)(2,1)S(1)}, bf16[128,1024]{1,0:T(8,128)(2,1)}, u32[]{:S(2)}) copy-start(bf16[128,1024]{1,0:T(8,128)(2,1)} %post_ref.4) | copy-start | bytes 786436
  4.8 8.6 %copy-start.3 = (s32[256,8]{0,1:T(8,128)S(1)}, s32[256,8]{0,1:T(8,128)}, u32[]{:S(2)}) copy-start(s32[256,8]{0,1:T(8,128)} %param.13) | copy-start | bytes 24580
  4.8 8.8 %copy-start.1 = (s32[128,8]{0,1:T(8,128)S(1)}, s32[128,8]{0,1:T(8,128)}, u32[]{:S(2)}) copy-start(s32[128,8]{0,1:T(8,128)} %param.15) | copy-start | bytes 12292
  4.8 8.8 %copy-start.2 = (s32[128]{0:T(128)S(1)}, s32[128]{0:T(128)}, u32[]{:S(2)}) copy-start(s32[128]{0:T(128)} %param.12) | copy-start | bytes 1540
  4.9 3.1 %collective-permute-start = (bf16[8,128,512]{2,1,0:T(8,128)(2,1)S(1)}, bf16[8,128,512]{2,1,0:T(8,128)(2,1)S(1)}, u32[]{:S(2)}, u32[]{:S(2)}) collective-permute-start(bf16[8,128,512]{2,1,0:T(8,128)(2,1)S(1)} %prior_half.4), channel_id=1, source_target_pairs={{0,2},{2,0},{4,6},{6,4},{8,10},{10,8},{12,14},{14,12},{16,18},{18,... | collective-permute-start | bytes 3145736 | tf_op jit(solution)/shard_map/ppermute | solution.py:340
  8.1 9.8 %collective-permute-start.2 = (bf16[2,128,512]{2,1,0:T(8,128)(2,1)S(1)}, bf16[2,128,512]{2,1,0:T(8,128)(2,1)S(1)}, u32[]{:S(2)}, u32[]{:S(2)}) collective-permute-start(bf16[2,128,512]{2,1,0:T(8,128)(2,1)S(1)} %get-tuple-element.41), channel_id=1, source_target_pairs={{0,4},{2,6},{4,0},{6,2},{8,12},{10,14},{12,8},{14,10},{16,20},{18,... | collective-permute-start | bytes 786440 | tf_op jit(solution)/shard_map/ppermute | solution.py:340
  13.6 9.7 %collective-permute-start.1 = (bf16[2,128,512]{2,1,0:T(8,128)(2,1)S(1)}, bf16[2,128,512]{2,1,0:T(8,128)(2,1)S(1)}, u32[]{:S(2)}, u32[]{:S(2)}) collective-permute-start(bf16[2,128,512]{2,1,0:T(8,128)(2,1)S(1)} %get-tuple-element.45), channel_id=1, source_target_pairs={{0,4},{2,6},{4,0},{6,2},{8,12},{10,14},{12,8},{14,10},{16,20},{18,... | collective-permute-start | bytes 786440 | tf_op jit(solution)/shard_map/ppermute | solution.py:340
  18.0 12.8 %collective-permute-start.3 = (bf16[128,512]{1,0:T(8,128)(2,1)S(1)}, bf16[128,512]{1,0:T(8,128)(2,1)S(1)}, u32[]{:S(2)}, u32[]{:S(2)}) collective-permute-start(bf16[128,512]{1,0:T(8,128)(2,1)S(1)} %get-tuple-element.81), channel_id=1, source_target_pairs={{0,16},{2,18},{4,20},{6,22},{8,24},{10,26},{12,28},{14,30},{16,0},... | collective-permute-start | bytes 393224 | tf_op jit(solution)/shard_map/ppermute | solution.py:340
  21.1 9.7 %collective-permute-start.4 = (bf16[128,512]{1,0:T(8,128)(2,1)S(1)}, bf16[128,512]{1,0:T(8,128)(2,1)S(1)}, u32[]{:S(2)}, u32[]{:S(2)}) collective-permute-start(bf16[128,512]{1,0:T(8,128)(2,1)S(1)} %get-tuple-element.82), channel_id=1, source_target_pairs={{0,24},{2,26},{4,28},{6,30},{8,16},{10,18},{12,20},{14,22},{16,8},... | collective-permute-start | bytes 393224 | tf_op jit(solution)/shard_map/ppermute | solution.py:340
  23.3 8.7 %collective-permute-start.5 = (bf16[128,512]{1,0:T(8,128)(2,1)S(1)}, bf16[128,512]{1,0:T(8,128)(2,1)S(1)}, u32[]{:S(2)}, u32[]{:S(2)}) collective-permute-start(bf16[128,512]{1,0:T(8,128)(2,1)S(1)} %fusion.4), channel_id=1, source_target_pairs={{0,8},{2,10},{4,12},{6,14},{8,0},{10,2},{12,4},{14,6},{16,24},{18,... | collective-permute-start | bytes 393224 | tf_op jit(solution)/shard_map/ppermute | solution.py:340
  32.1 14.0 %collective-permute-start.6 = (bf16[128,512]{1,0:T(8,128)(2,1)S(1)}, bf16[128,512]{1,0:T(8,128)(2,1)S(1)}, u32[]{:S(2)}, u32[]{:S(2)}) collective-permute-start(bf16[128,512]{1,0:T(8,128)(2,1)S(1)} %fusion.3), channel_id=1, source_target_pairs={{0,16},{2,18},{4,20},{6,22},{8,24},{10,26},{12,28},{14,30},{16,0},... | collective-permute-start | bytes 393224 | tf_op jit(solution)/shard_map/ppermute | solution.py:340
  35.2 10.9 %collective-permute-start.7 = (bf16[128,512]{1,0:T(8,128)(2,1)S(1)}, bf16[128,512]{1,0:T(8,128)(2,1)S(1)}, u32[]{:S(2)}, u32[]{:S(2)}) collective-permute-start(bf16[128,512]{1,0:T(8,128)(2,1)S(1)} %fusion.3), channel_id=1, source_target_pairs={{0,24},{2,26},{4,28},{6,30},{8,16},{10,18},{12,20},{14,22},{16,8},... | collective-permute-start | bytes 393224 | tf_op jit(solution)/shard_map/ppermute | solution.py:340
  36.1 10.0 %collective-permute-start.8 = (bf16[128,512]{1,0:T(8,128)(2,1)S(1)}, bf16[128,512]{1,0:T(8,128)(2,1)S(1)}, u32[]{:S(2)}, u32[]{:S(2)}) collective-permute-start(bf16[128,512]{1,0:T(8,128)(2,1)S(1)} %fusion.3), channel_id=1, source_target_pairs={{0,8},{2,10},{4,12},{6,14},{8,0},{10,2},{12,4},{14,6},{16,24},{18,... | collective-permute-start | bytes 393224 | tf_op jit(solution)/shard_map/ppermute | solution.py:340
  36.6 9.6 %collective-permute-start.10 = (bf16[128,512]{1,0:T(8,128)(2,1)S(1)}, bf16[128,512]{1,0:T(8,128)(2,1)S(1)}, u32[]{:S(2)}, u32[]{:S(2)}) collective-permute-start(bf16[128,512]{1,0:T(8,128)(2,1)S(1)} %fusion.3), channel_id=1, source_target_pairs={{0,4},{2,6},{4,0},{6,2},{8,12},{10,14},{12,8},{14,10},{16,20},{18,... | collective-permute-start | bytes 393224 | tf_op jit(solution)/shard_map/ppermute | solution.py:340
  46.1 4.1 %collective-permute-start.13 = (bf16[2,128,512]{2,1,0:T(8,128)(2,1)S(1)}, bf16[2,128,512]{2,1,0:T(8,128)(2,1)S(1)}, u32[]{:S(2)}, u32[]{:S(2)}) collective-permute-start(bf16[2,128,512]{2,1,0:T(8,128)(2,1)S(1)} %pad_maximum_fusion.refs_2_), channel_id=1, source_target_pairs={{0,2},{2,0},{4,6},{6,4},{8,10},{10,8},{12,14},{14,12},{16,18},{18,... | collective-permute-start | bytes 786440 | tf_op jit(solution)/shard_map/ppermute | solution.py:340
  46.2 4.0 %collective-permute-start.12 = (bf16[2,128,512]{2,1,0:T(8,128)(2,1)S(1)}, bf16[2,128,512]{2,1,0:T(8,128)(2,1)S(1)}, u32[]{:S(2)}, u32[]{:S(2)}) collective-permute-start(bf16[2,128,512]{2,1,0:T(8,128)(2,1)S(1)} %pad_maximum_fusion.1.refs_0_), channel_id=1, source_target_pairs={{0,2},{2,0},{4,6},{6,4},{8,10},{10,8},{12,14},{14,12},{16,18},{18,... | collective-permute-start | bytes 786440 | tf_op jit(solution)/shard_map/ppermute | solution.py:340
  46.8 8.3 %collective-permute-start.9 = (bf16[2,128,512]{2,1,0:T(8,128)(2,1)S(1)}, bf16[2,128,512]{2,1,0:T(8,128)(2,1)S(1)}, u32[]{:S(2)}, u32[]{:S(2)}) collective-permute-start(bf16[2,128,512]{2,1,0:T(8,128)(2,1)S(1)} %pad_maximum_fusion.refs_2_), channel_id=1, source_target_pairs={{0,4},{2,6},{4,0},{6,2},{8,12},{10,14},{12,8},{14,10},{16,20},{18,... | collective-permute-start | bytes 786440 | tf_op jit(solution)/shard_map/ppermute | solution.py:340
  48.1 6.5 %collective-permute-start.11 = (bf16[128,512]{1,0:T(8,128)(2,1)S(1)}, bf16[128,512]{1,0:T(8,128)(2,1)S(1)}, u32[]{:S(2)}, u32[]{:S(2)}) collective-permute-start(bf16[128,512]{1,0:T(8,128)(2,1)S(1)} %collective-permute-done.10), channel_id=1, source_target_pairs={{0,8},{2,10},{4,12},{6,14},{8,0},{10,2},{12,4},{14,6},{16,24},{18,... | collective-permute-start | bytes 393224 | tf_op jit(solution)/shard_map/ppermute | solution.py:340
  55.1 1.6 %collective-permute-start.15 = (bf16[2,128,512]{2,1,0:T(8,128)(2,1)S(1)}, bf16[2,128,512]{2,1,0:T(8,128)(2,1)S(1)}, u32[]{:S(2)}, u32[]{:S(2)}) collective-permute-start(bf16[2,128,512]{2,1,0:T(8,128)(2,1)S(1)} %pad_maximum_fusion.2.refs_2_), channel_id=1, source_target_pairs={{0,2},{2,0},{4,6},{6,4},{8,10},{10,8},{12,14},{14,12},{16,18},{18,... | collective-permute-start | bytes 786440 | tf_op jit(solution)/shard_map/ppermute | solution.py:340
  55.2 1.9 %collective-permute-start.14 = (bf16[2,128,512]{2,1,0:T(8,128)(2,1)S(1)}, bf16[2,128,512]{2,1,0:T(8,128)(2,1)S(1)}, u32[]{:S(2)}, u32[]{:S(2)}) collective-permute-start(bf16[2,128,512]{2,1,0:T(8,128)(2,1)S(1)} %collective-permute-done.9.refs_0_), channel_id=1, source_target_pairs={{0,2},{2,0},{4,6},{6,4},{8,10},{10,8},{12,14},{14,12},{16,18},{18,... | collective-permute-start | bytes 786440 | tf_op jit(solution)/shard_map/ppermute | solution.py:340
  62.6 6.1 %collective-permute-start.16 = (f32[1,128]{1,0:T(1,128)S(1)}, f32[1,128]{1,0:T(1,128)S(1)}, u32[]{:S(2)}, u32[]{:S(2)}) collective-permute-start(f32[1,128]{1,0:T(1,128)S(1)} %get-tuple-element.73), channel_id=1, source_target_pairs={{0,16},{2,18},{4,20},{6,22},{8,24},{10,26},{12,28},{14,30},{16,0},... | collective-permute-start | bytes 1544 | tf_op jit(solution)/shard_map/ppermute | solution.py:340
  66.5 5.3 %collective-permute-start.17 = (f32[1,128]{1,0:T(1,128)S(1)}, f32[1,128]{1,0:T(1,128)S(1)}, u32[]{:S(2)}, u32[]{:S(2)}) collective-permute-start(f32[1,128]{1,0:T(1,128)S(1)} %get-tuple-element.73), channel_id=1, source_target_pairs={{0,24},{2,26},{4,28},{6,30},{8,16},{10,18},{12,20},{14,22},{16,8},... | collective-permute-start | bytes 1544 | tf_op jit(solution)/shard_map/ppermute | solution.py:340
  67.0 4.9 %collective-permute-start.18 = (f32[1,128]{1,0:T(1,128)S(1)}, f32[1,128]{1,0:T(1,128)S(1)}, u32[]{:S(2)}, u32[]{:S(2)}) collective-permute-start(f32[1,128]{1,0:T(1,128)S(1)} %get-tuple-element.73), channel_id=1, source_target_pairs={{0,8},{2,10},{4,12},{6,14},{8,0},{10,2},{12,4},{14,6},{16,24},{18,... | collective-permute-start | bytes 1544 | tf_op jit(solution)/shard_map/ppermute | solution.py:340
  67.2 8.9 %collective-permute-start.20 = (bf16[64,1024]{1,0:T(8,128)(2,1)S(1)}, bf16[64,1024]{1,0:T(8,128)(2,1)S(1)}, u32[]{:S(2)}, u32[]{:S(2)}) collective-permute-start(bf16[64,1024]{1,0:T(8,128)(2,1)S(1)} %get-tuple-element.74), channel_id=1, source_target_pairs={{0,1},{1,0},{2,3},{3,2},{4,5},{5,4},{6,7},{7,6},{8,9},{9,8},{10,11... | collective-permute-start | bytes 393224 | tf_op jit(solution)/shard_map/ppermute | solution.py:411
  71.9 1.2 %collective-permute-start.19 = (f32[1,128]{1,0:T(1,128)S(1)}, f32[1,128]{1,0:T(1,128)S(1)}, u32[]{:S(2)}, u32[]{:S(2)}) collective-permute-start(f32[1,128]{1,0:T(1,128)S(1)} %add_add_fusion.1), channel_id=1, source_target_pairs={{0,2},{2,0},{4,6},{6,4},{8,10},{10,8},{12,14},{14,12},{16,18},{18,... | collective-permute-start | bytes 1544 | tf_op jit(solution)/shard_map/ppermute | solution.py:340
  73.1 3.7 %collective-permute-start.22 = (f32[1,128]{1,0:T(1,128)S(1)}, f32[1,128]{1,0:T(1,128)S(1)}, u32[]{:S(2)}, u32[]{:S(2)}) collective-permute-start(f32[1,128]{1,0:T(1,128)S(1)} %add.68), channel_id=1, source_target_pairs={{0,4},{2,6},{4,0},{6,2},{8,12},{10,14},{12,8},{14,10},{16,20},{18,... | collective-permute-start | bytes 1544 | tf_op jit(solution)/shard_map/ppermute | solution.py:340
  74.6 4.4 %collective-permute-start.23 = (f32[1,128]{1,0:T(1,128)S(1)}, f32[1,128]{1,0:T(1,128)S(1)}, u32[]{:S(2)}, u32[]{:S(2)}) collective-permute-start(f32[1,128]{1,0:T(1,128)S(1)} %add.68), channel_id=1, source_target_pairs={{0,5},{1,4},{2,7},{3,6},{4,1},{5,0},{6,3},{7,2},{8,13},{9,12},{10,... | collective-permute-start | bytes 1544 | tf_op jit(solution)/shard_map/ppermute | solution.py:416
  76.1 3.5 %collective-permute-start.21 = (f32[1,128]{1,0:T(1,128)S(1)}, f32[1,128]{1,0:T(1,128)S(1)}, u32[]{:S(2)}, u32[]{:S(2)}) collective-permute-start(f32[1,128]{1,0:T(1,128)S(1)} %add.68), channel_id=1, source_target_pairs={{0,1},{1,0},{2,3},{3,2},{4,5},{5,4},{6,7},{7,6},{8,9},{9,8},{10,11... | collective-permute-start | bytes 1544 | tf_op jit(solution)/shard_map/ppermute | solution.py:418
